TPU v7x, 32 devices: a whole 2x2x4 slice. The times are simulated.
32 devices in a mesh: seq: 8 (over z, x), fsdp: 4 (over y, core).
Axes of the slice: x: 2, y: 2, z: 4, core: 2. Of those that a mesh axis runs over, the one named last changes fastest.
Arguments:
- residual_in: float32 [4, 4096, 1024], P('fsdp', 'seq'), may hold values from -16 to 16, as said below
- doc_starts: int32 [4, 4096], P('fsdp', 'seq'), may hold values from 0 to 1, as said below
- out_grad: float32 [4, 4096, 1024], P('fsdp', 'seq'), may hold values from -6 to 6
- norm_gain: float32 [1024], P('fsdp'), may hold values from 0.5 to 1.5
- qkv_weight: float32 [1024, 4096], P('fsdp'), may hold values from -0.1875 to 0.1875
- gate_weight: float32 [1024, 2048], P('fsdp'), may hold values from -0.1875 to 0.1875
- decay_beta_weight: float32 [1024, 16], P('fsdp'), may hold values from -0.1875 to 0.1875
- conv_weight: float32 [4, 4096], P(None, 'fsdp'), may hold values from -3 to 3
- decay_log: float32 [8], P('fsdp'), as said below
- decay_bias: float32 [8], P('fsdp'), may hold values from -1 to 1
- beta_bias: float32 [8], P('fsdp'), as said below
- head_gain: float32 [256], P('fsdp'), may hold values from 0.5 to 1.5
- out_weight: float32 [2048, 1024], P('fsdp'), may hold values from -0.125 to 0.125
- mlp_gain: float32 [1024], P('fsdp'), may hold values from 0.5 to 1.5
- up_weight: float32 [1024, 5632], P('fsdp'), may hold values from -0.1875 to 0.1875
- down_weight: float32 [2816, 1024], P('fsdp'), may hold values from -0.109375 to 0.109375
Outputs:
- output: float32 [4, 4096, 1024], P('fsdp', 'seq')
- input_grad: float32 [4, 4096, 1024], P('fsdp', 'seq')
- grad_norm_gain: float32 [1024], P('fsdp')
- grad_qkv_weight: float32 [1024, 4096], P('fsdp')
- grad_gate_weight: float32 [1024, 2048], P('fsdp')
- grad_decay_beta_weight: float32 [1024, 16], P('fsdp')
- grad_conv_weight: float32 [4, 4096], P(None, 'fsdp')
- grad_decay_log: float32 [8], P('fsdp')
- grad_decay_bias: float32 [8], P('fsdp')
- grad_beta_bias: float32 [8], P('fsdp')
- grad_head_gain: float32 [256], P('fsdp')
- grad_out_weight: float32 [2048, 1024], P('fsdp')
- grad_mlp_gain: float32 [1024], P('fsdp')
- grad_up_weight: float32 [1024, 5632], P('fsdp')
- grad_down_weight: float32 [2816, 1024], P('fsdp')
- rms: float32 [4], replicated
Inputs may be any that keep to these rules, and one draw needn't show every extreme that they name: `doc_starts`: 1 where a document starts, else 0; the first token of each sequence starts a document; in each sequence one document starts within its first 256 tokens and runs until a start within its last 256 tokens. `residual_in`: rows whose scale changes along the sequence. `decay_log`: the log of a per-token rate between 0.3 / 4096 and 1 / 30. `beta_bias`: a logit between that of 16 / 4096 and 1.5.
All inputs are finite; a program needn't handle non-finite values.
Results may differ from a plain program's by a relative error of at most 0.0003.
Values sent between devices are 32-bit elements; how exact they have to be, the bound alone decides.
No kernel may reach another device: no remote copies, remote signals or barrier semaphores. Data moves between devices by JAX's collectives and lax.ppermute only.
A program may use at most 640 MiB of HBM per device.

v0:
```python
from functools import partial

import jax
import jax.numpy as jnp
from jax import lax
from jax.sharding import PartitionSpec as P

D = 1024
H = 8
DK = 128
DV = 256
FF = 2816
CONV = 4
BLOCK = 64


HIGH_PRECISION = lax.Precision.HIGHEST
NORM_EPS = 1e-05
UNIT_EPS = 1e-06


def passed_along(block, axis, distance):
    devices = range(lax.axis_size(axis))
    route = [(i - distance, i) for i in devices if i - distance in devices]
    return lax.ppermute(block, axis, route)


def entering(part, axis, combine, identity, reverse):
    count = lax.axis_size(axis)
    place = lax.axis_index(axis)
    ahead = count - 1 - place if reverse else place
    gathered = jax.tree.map(lambda a: lax.all_gather(a, axis), part)
    state = jax.tree.map(lambda a, e: jnp.zeros_like(a) + jnp.asarray(e, a.dtype), part, identity)

    def one(step, state):
        source = count - 1 - step if reverse else step
        return combine(
            state, jax.tree.map(lambda a: lax.dynamic_index_in_dim(a, source, 0, False), gathered)
        )

    return lax.fori_loop(0, ahead, one, state)


def matmul(left, right):
    return jnp.dot(left, right, precision=HIGH_PRECISION, preferred_element_type=jnp.float32)


def rms_norm(rows, gain):
    return rows * lax.rsqrt(jnp.mean(rows * rows, axis=-1, keepdims=True) + NORM_EPS) * gain


def unit_rows(rows):
    return rows * lax.rsqrt(jnp.sum(rows * rows, axis=-1, keepdims=True) + UNIT_EPS)


def project(rows, norm_gain, qkv_weight, gate_weight, decay_beta_weight):
    normed = rms_norm(rows, norm_gain)
    return (
        matmul(normed, qkv_weight),
        matmul(normed, gate_weight),
        matmul(normed, decay_beta_weight),
    )


def front(mixed_in, rim_rows, decay_beta, conv_weight, decay_log, decay_bias, beta_bias, counts):
    tokens_here = mixed_in.shape[0]
    extended = jnp.concatenate([rim_rows, mixed_in], 0)
    extended_counts = jnp.concatenate([jnp.zeros((CONV - 1,), jnp.int32), counts], 0)
    convolved = conv_weight[0] * mixed_in
    for shift_by in range(1, CONV):
        offset = CONV - 1 - shift_by
        same = (counts == extended_counts[offset : offset + tokens_here]).astype(jnp.float32)
        convolved = (
            convolved
            + conv_weight[shift_by] * extended[offset : offset + tokens_here] * same[:, None]
        )
    convolved = jax.nn.silu(convolved)
    width_k = H * DK
    queries = unit_rows(convolved[:, :width_k].reshape(tokens_here, H, DK)) * DK ** (-0.5)
    key_rows = unit_rows(convolved[:, width_k : 2 * width_k].reshape(tokens_here, H, DK))
    values = convolved[:, 2 * width_k :].reshape(tokens_here, H, DV)
    log_decay = -jnp.exp(decay_log) * jax.nn.softplus(decay_beta[:, :H] + decay_bias)
    beta_rows = jax.nn.sigmoid(decay_beta[:, H:] + beta_bias)
    return (queries, key_rows, values, log_decay, beta_rows)


def delta_blocks(queries, key_rows, values, log_decay, beta_rows, counts, before):
    tokens_here = queries.shape[0]
    blocks = tokens_here // BLOCK
    width = DV + DK
    padded_values = jnp.concatenate([values, jnp.zeros((tokens_here, H, DK), jnp.float32)], 2)
    identity = jnp.broadcast_to(jnp.eye(DK, dtype=jnp.float32), (H, DK, DK))
    carried_state = jnp.concatenate([jnp.zeros((H, DK, DV), jnp.float32), identity], 2)
    position = jnp.arange(BLOCK)
    strict = position[:, None] > position[None, :]
    within = position[:, None] >= position[None, :]
    unit_block = jnp.eye(BLOCK, dtype=jnp.float32)

    def block_step(carried_state, pieces):
        query_blk, key_blk, value_blk, decay_blk, beta_blk, count_blk, before_blk = pieces
        cumulative = jnp.cumsum(decay_blk, 0).T
        same = count_blk[:, None] == count_blk[None, :]
        spread = cumulative[:, :, None] - cumulative[:, None, :]
        ratios = jnp.where((same & within)[None], jnp.exp(jnp.minimum(spread, 0.0)), 0.0)
        leading = jnp.where((count_blk == before_blk[0])[None, :], jnp.exp(cumulative), 0.0)
        key_dots = jnp.einsum("thd,jhd->htj", key_blk, key_blk, precision=HIGH_PRECISION)
        query_dots = jnp.einsum("thd,jhd->htj", query_blk, key_blk, precision=HIGH_PRECISION)
        beta_cols = beta_blk.T[:, None, :]
        lower_mix = jnp.where(strict[None], ratios, 0.0) * key_dots * beta_cols
        out_mix = ratios * query_dots * beta_cols
        recalled_values = jnp.einsum(
            "thd,hdw->htw", key_blk, carried_state, precision=HIGH_PRECISION
        )
        targets = jnp.transpose(value_blk, (1, 0, 2)) - leading[:, :, None] * recalled_values
        residues = jax.scipy.linalg.solve_triangular(
            unit_block[None] + lower_mix, targets, lower=True
        )
        reading = jnp.einsum("thd,hdw->htw", query_blk, carried_state, precision=HIGH_PRECISION)
        outputs = leading[:, :, None] * reading + jnp.einsum(
            "htj,hjw->htw", out_mix, residues, precision=HIGH_PRECISION
        )
        closing = ratios[:, -1, :] * beta_blk.T
        written = jnp.einsum(
            "hj,jhd,hjw->hdw", closing, key_blk, residues, precision=HIGH_PRECISION
        )
        carried_state = leading[:, -1][:, None, None] * carried_state + written
        return (carried_state, outputs)

    shaped = tuple(
        (
            piece.reshape((blocks, BLOCK) + piece.shape[1:])
            for piece in (queries, key_rows, padded_values, log_decay, beta_rows, counts, before)
        )
    )
    carried_state, outputs = lax.scan(block_step, carried_state, shaped)
    outputs = jnp.transpose(outputs, (0, 2, 1, 3)).reshape(tokens_here, H, width)
    return (
        outputs[:, :, :DV],
        outputs[:, :, DV:],
        carried_state[:, :, DV:],
        carried_state[:, :, :DV],
    )


def finish(head_outputs, gate_rows, rows, head_gain, out_weight, mlp_gain, up_weight, down_weight):
    tokens_here = rows.shape[0]
    scaled = head_outputs * lax.rsqrt(
        jnp.mean(head_outputs * head_outputs, axis=-1, keepdims=True) + NORM_EPS
    )
    gated = scaled * head_gain * jax.nn.silu(gate_rows.reshape(tokens_here, H, DV))
    mixer = matmul(gated.reshape(tokens_here, H * DV), out_weight)
    middle = rows + mixer
    lifted = matmul(rms_norm(middle, mlp_gain), up_weight)
    hidden = jax.nn.silu(lifted[:, :FF]) * lifted[:, FF:]
    branch = matmul(hidden, down_weight)
    return (middle + branch, (mixer, branch))


def compose(earlier, later):
    first = jnp.einsum("hij,hjk->hik", later[0], earlier[0], precision=HIGH_PRECISION)
    second = jnp.einsum("hij,hjk->hik", later[0], earlier[1], precision=HIGH_PRECISION) + later[1]
    return (first, second)


def on_device(
    residual_in,
    doc_starts,
    out_grad,
    norm_gain,
    qkv_weight,
    gate_weight,
    decay_beta_weight,
    conv_weight,
    decay_log,
    decay_bias,
    beta_bias,
    head_gain,
    out_weight,
    mlp_gain,
    up_weight,
    down_weight,
):
    gathered = (
        lax.all_gather(norm_gain, "fsdp", axis=0, tiled=True),
        lax.all_gather(qkv_weight, "fsdp", axis=0, tiled=True),
        lax.all_gather(gate_weight, "fsdp", axis=0, tiled=True),
        lax.all_gather(decay_beta_weight, "fsdp", axis=0, tiled=True),
        lax.all_gather(conv_weight, "fsdp", axis=1, tiled=True),
        lax.all_gather(decay_log, "fsdp", axis=0, tiled=True),
        lax.all_gather(decay_bias, "fsdp", axis=0, tiled=True),
        lax.all_gather(beta_bias, "fsdp", axis=0, tiled=True),
        lax.all_gather(head_gain, "fsdp", axis=0, tiled=True),
        lax.all_gather(out_weight, "fsdp", axis=0, tiled=True),
        lax.all_gather(mlp_gain, "fsdp", axis=0, tiled=True),
        lax.all_gather(up_weight, "fsdp", axis=0, tiled=True),
        lax.all_gather(down_weight, "fsdp", axis=0, tiled=True),
    )
    (
        full_norm,
        full_qkv,
        full_gate,
        full_decay_beta,
        full_conv,
        full_decay_log,
        full_decay_bias,
        full_beta_bias,
        full_head_gain,
        full_out,
        full_mlp_gain,
        full_up,
        full_down,
    ) = gathered
    rows = residual_in[0]
    starts = doc_starts[0]
    cotangent = out_grad[0]
    tokens_here = rows.shape[0]
    counts = jnp.cumsum(starts)
    before = counts - starts
    after = jnp.flip(jnp.cumsum(jnp.flip(starts))) - starts
    tail_mask = (after[tokens_here - CONV + 1 :] == 0).astype(jnp.float32)[:, None]
    projected, project_pull = jax.vjp(
        project, rows, full_norm, full_qkv, full_gate, full_decay_beta
    )
    mixed_in, gate_rows, decay_beta = projected
    rim_rows = passed_along(mixed_in[tokens_here - CONV + 1 :] * tail_mask, "seq", 1)
    front_parts, front_pull = jax.vjp(
        partial(front, counts=counts),
        mixed_in,
        rim_rows,
        decay_beta,
        full_conv,
        full_decay_log,
        full_decay_bias,
        full_beta_bias,
    )
    delta_parts, delta_pull = jax.vjp(
        partial(delta_blocks, counts=counts, before=before), *front_parts
    )
    local_output, query_mapping, trans_a, trans_b = delta_parts
    identity = jnp.broadcast_to(jnp.eye(DK, dtype=jnp.float32), trans_a.shape)
    empty = jnp.zeros(trans_b.shape, jnp.float32)
    prefix = entering((trans_a, trans_b), "seq", compose, (identity, empty), False)
    incoming_state = prefix[1]
    head_outputs = local_output + jnp.einsum(
        "mgs,gse->mge", query_mapping, incoming_state, precision=HIGH_PRECISION
    )
    result, finish_pull, branches = jax.vjp(
        finish,
        head_outputs,
        gate_rows,
        rows,
        full_head_gain,
        full_out,
        full_mlp_gain,
        full_up,
        full_down,
        has_aux=True,
    )
    mixer, branch = branches
    squares = jnp.stack(
        [
            jnp.sum(rows * rows),
            jnp.sum(mixer * mixer),
            jnp.sum(branch * branch),
            jnp.sum(result * result),
        ]
    )
    totals = lax.psum(squares, ("seq", "fsdp"))
    count = lax.axis_size("seq") * lax.axis_size("fsdp") * tokens_here * D
    rms_values = jnp.sqrt(totals / count)
    again = (
        lax.all_gather(norm_gain, "fsdp", axis=0, tiled=True),
        lax.all_gather(qkv_weight, "fsdp", axis=0, tiled=True),
        lax.all_gather(gate_weight, "fsdp", axis=0, tiled=True),
        lax.all_gather(decay_beta_weight, "fsdp", axis=0, tiled=True),
        lax.all_gather(head_gain, "fsdp", axis=0, tiled=True),
        lax.all_gather(out_weight, "fsdp", axis=0, tiled=True),
        lax.all_gather(mlp_gain, "fsdp", axis=0, tiled=True),
        lax.all_gather(up_weight, "fsdp", axis=0, tiled=True),
        lax.all_gather(down_weight, "fsdp", axis=0, tiled=True),
    )
    unused, project_pull = jax.vjp(project, rows, again[0], again[1], again[2], again[3])
    unused, finish_pull, unused_aux = jax.vjp(
        finish,
        head_outputs,
        gate_rows,
        rows,
        again[4],
        again[5],
        again[6],
        again[7],
        again[8],
        has_aux=True,
    )
    finish_grads = finish_pull(cotangent)
    (
        head_gradient,
        grad_gate_rows,
        grad_rows_late,
        grad_head_gain,
        grad_out,
        grad_mlp_gain,
        grad_up,
        grad_down,
    ) = finish_grads
    direct_term = jnp.einsum("xcg,xcy->cgy", query_mapping, head_gradient, precision=HIGH_PRECISION)
    gradient_mapping = jnp.einsum(
        "wgi,gbi->wgb", head_gradient, incoming_state, precision=HIGH_PRECISION
    )
    suffix = entering(
        (jnp.swapaxes(trans_a, 1, 2), direct_term), "seq", compose, (identity, empty), True
    )
    state_gradient = suffix[1]
    transposed_gradient = jnp.einsum(
        "amp,adp->amd", state_gradient, incoming_state, precision=HIGH_PRECISION
    )
    grads_front = delta_pull((head_gradient, gradient_mapping, transposed_gradient, state_gradient))
    (
        grad_mixed,
        grad_rim,
        grad_decay_beta,
        grad_conv,
        grad_decay_log,
        grad_decay_bias,
        grad_beta_bias,
    ) = front_pull(grads_front)
    returned = passed_along(grad_rim, "seq", -1)
    grad_mixed = grad_mixed.at[tokens_here - CONV + 1 :].add(returned * tail_mask)
    grad_rows_early, grad_norm, grad_qkv, grad_gate_w, grad_decay_beta_w = project_pull(
        (grad_mixed, grad_gate_rows, grad_decay_beta)
    )
    row_grad = grad_rows_late + grad_rows_early
    shares = (
        lax.psum_scatter(grad_norm, "fsdp", scatter_dimension=0, tiled=True),
        lax.psum_scatter(grad_qkv, "fsdp", scatter_dimension=0, tiled=True),
        lax.psum_scatter(grad_gate_w, "fsdp", scatter_dimension=0, tiled=True),
        lax.psum_scatter(grad_decay_beta_w, "fsdp", scatter_dimension=0, tiled=True),
        lax.psum_scatter(grad_conv, "fsdp", scatter_dimension=1, tiled=True),
        lax.psum_scatter(grad_decay_log, "fsdp", scatter_dimension=0, tiled=True),
        lax.psum_scatter(grad_decay_bias, "fsdp", scatter_dimension=0, tiled=True),
        lax.psum_scatter(grad_beta_bias, "fsdp", scatter_dimension=0, tiled=True),
        lax.psum_scatter(grad_head_gain, "fsdp", scatter_dimension=0, tiled=True),
        lax.psum_scatter(grad_out, "fsdp", scatter_dimension=0, tiled=True),
        lax.psum_scatter(grad_mlp_gain, "fsdp", scatter_dimension=0, tiled=True),
        lax.psum_scatter(grad_up, "fsdp", scatter_dimension=0, tiled=True),
        lax.psum_scatter(grad_down, "fsdp", scatter_dimension=0, tiled=True),
    )
    (
        share_norm,
        share_qkv,
        share_gate,
        share_decay_beta,
        share_conv,
        share_decay_log,
        share_decay_bias,
        share_beta_bias,
        share_head_gain,
        share_out,
        share_mlp_gain,
        share_up,
        share_down,
    ) = shares
    summed = lax.psum(
        (
            share_norm,
            share_qkv,
            share_gate,
            share_decay_beta,
            share_conv,
            share_decay_log,
            share_decay_bias,
            share_beta_bias,
            share_head_gain,
            share_out,
            share_mlp_gain,
            share_up,
            share_down,
        ),
        "seq",
    )
    return (
        result[None],
        row_grad[None],
        summed[0],
        summed[1],
        summed[2],
        summed[3],
        summed[4],
        summed[5],
        summed[6],
        summed[7],
        summed[8],
        summed[9],
        summed[10],
        summed[11],
        summed[12],
        rms_values,
    )


def solution(mesh):
    return jax.shard_map(
        on_device,
        mesh=mesh,
        in_specs=(
            P("fsdp", "seq", None),
            P("fsdp", "seq"),
            P("fsdp", "seq", None),
            P("fsdp"),
            P("fsdp", None),
            P("fsdp", None),
            P("fsdp", None),
            P(None, "fsdp"),
            P("fsdp"),
            P("fsdp"),
            P("fsdp"),
            P("fsdp"),
            P("fsdp", None),
            P("fsdp"),
            P("fsdp", None),
            P("fsdp", None),
        ),
        out_specs=(
            P("fsdp", "seq", None),
            P("fsdp", "seq", None),
            P("fsdp"),
            P("fsdp", None),
            P("fsdp", None),
            P("fsdp", None),
            P(None, "fsdp"),
            P("fsdp"),
            P("fsdp"),
            P("fsdp"),
            P("fsdp"),
            P("fsdp", None),
            P("fsdp"),
            P("fsdp", None),
            P("fsdp", None),
            P(),
        ),
        check_vma=False,
    )
```

profile of v0, /device:TPU:0, one launch (start us, length us, event | category | flops | bytes accessed | tf_op | source)
XLA Modules:
  0.0 3057.0 jit_solution(17586468279711752988)
XLA Ops:
  42.4 76.4 %all-gather.16.cloned.1.call-done = f32[1024,4096]{1,0:T(8,128)} async-done(((f32[256,4096]{1,0:T(8,128)}), f32[1024,4096]{1,0:T(8,128)}) %all-gather.16.cloned.1.call-update) | async-done | bytes 16777232 | tf_op jit(solution)/shard_map/all_gather | solution.py:185
  197.7 519.4 %while.122 = (s32[]{:T(128)}, f32[8,128,384]{2,1,0:T(8,128)S(1)}, f32[8,8,64,384]{3,2,1,0:T(8,128)}, f32[8,8,64,64]{3,2,1,0:T(8,128)}, f32[8,8,64,64]{3,2,1,0:T(...) while((s32[]{:T(128)}, f32[8,128,384]{2,1,0:T(8,128)S(1)}, ...), condition=%wide.region_9.10_spmd.clone.clone, body=%wide.region_7.9_spmd.clone.clone.sunk | while | flops 1311368192 | bytes 26823780 | solution.py:135
  203.0 39.3 %custom-call.53 = f32[8,1,64,64]{2,3,1,0:T(8,128)S(1)} custom-call(f32[8,1,64,64]{3,2,1,0:T(8,128)S(1)} %get-tuple-element.2895), custom_call_target="InvertDiagBlocksLowerTriangular" | custom-call | tf_op jit(solution)/shard_map/jvp()/while/body/eval_jaxpr/jit(_solve_triangular)/vmap()/triangular_solve | solution.py:115
  267.9 39.3 %custom-call.53 = f32[8,1,64,64]{2,3,1,0:T(8,128)S(1)} custom-call(f32[8,1,64,64]{3,2,1,0:T(8,128)S(1)} %get-tuple-element.2895), custom_call_target="InvertDiagBlocksLowerTriangular" | custom-call | tf_op jit(solution)/shard_map/jvp()/while/body/eval_jaxpr/jit(_solve_triangular)/vmap()/triangular_solve | solution.py:115
  332.8 39.3 %custom-call.53 = f32[8,1,64,64]{2,3,1,0:T(8,128)S(1)} custom-call(f32[8,1,64,64]{3,2,1,0:T(8,128)S(1)} %get-tuple-element.2895), custom_call_target="InvertDiagBlocksLowerTriangular" | custom-call | tf_op jit(solution)/shard_map/jvp()/while/body/eval_jaxpr/jit(_solve_triangular)/vmap()/triangular_solve | solution.py:115
  397.6 39.3 %custom-call.53 = f32[8,1,64,64]{2,3,1,0:T(8,128)S(1)} custom-call(f32[8,1,64,64]{3,2,1,0:T(8,128)S(1)} %get-tuple-element.2895), custom_call_target="InvertDiagBlocksLowerTriangular" | custom-call | tf_op jit(solution)/shard_map/jvp()/while/body/eval_jaxpr/jit(_solve_triangular)/vmap()/triangular_solve | solution.py:115
  462.6 39.3 %custom-call.53 = f32[8,1,64,64]{2,3,1,0:T(8,128)S(1)} custom-call(f32[8,1,64,64]{3,2,1,0:T(8,128)S(1)} %get-tuple-element.2895), custom_call_target="InvertDiagBlocksLowerTriangular" | custom-call | tf_op jit(solution)/shard_map/jvp()/while/body/eval_jaxpr/jit(_solve_triangular)/vmap()/triangular_solve | solution.py:115
  527.6 39.3 %custom-call.53 = f32[8,1,64,64]{2,3,1,0:T(8,128)S(1)} custom-call(f32[8,1,64,64]{3,2,1,0:T(8,128)S(1)} %get-tuple-element.2895), custom_call_target="InvertDiagBlocksLowerTriangular" | custom-call | tf_op jit(solution)/shard_map/jvp()/while/body/eval_jaxpr/jit(_solve_triangular)/vmap()/triangular_solve | solution.py:115
  592.5 39.3 %custom-call.53 = f32[8,1,64,64]{2,3,1,0:T(8,128)S(1)} custom-call(f32[8,1,64,64]{3,2,1,0:T(8,128)S(1)} %get-tuple-element.2895), custom_call_target="InvertDiagBlocksLowerTriangular" | custom-call | tf_op jit(solution)/shard_map/jvp()/while/body/eval_jaxpr/jit(_solve_triangular)/vmap()/triangular_solve | solution.py:115
  657.4 39.3 %custom-call.53 = f32[8,1,64,64]{2,3,1,0:T(8,128)S(1)} custom-call(f32[8,1,64,64]{3,2,1,0:T(8,128)S(1)} %get-tuple-element.2895), custom_call_target="InvertDiagBlocksLowerTriangular" | custom-call | tf_op jit(solution)/shard_map/jvp()/while/body/eval_jaxpr/jit(_solve_triangular)/vmap()/triangular_solve | solution.py:115
  742.9 49.7 %all-gather.26.cloned.1.call-done = f32[64,128,128]{2,1,0:T(8,128)} async-done(((f32[8,128,128]{2,1,0:T(8,128)}), f32[64,128,128]{2,1,0:T(8,128)}) %all-gather.26.cloned.1.call-update) | async-done | bytes 4194320 | tf_op jit(solution)/shard_map/all_gather | solution.py:32
  792.7 125.8 %all-gather.28.cloned.1.call-done = f32[64,128,256]{2,1,0:T(8,128)} async-done(((f32[8,128,256]{2,1,0:T(8,128)}), f32[64,128,256]{2,1,0:T(8,128)}) %all-gather.28.cloned.1.call-update) | async-done | bytes 8388624 | tf_op jit(solution)/shard_map/all_gather | solution.py:32
  995.2 125.8 %all-gather.22.cloned.1.call-done = f32[1024,5632]{1,0:T(8,128)} async-done(((f32[256,5632]{1,0:T(8,128)}), f32[1024,5632]{1,0:T(8,128)}) %all-gather.22.cloned.1.call-update) | async-done | bytes 23068688 | tf_op jit(solution)/shard_map/all_gather | solution.py:195
  1121.0 44.8 %fusion.196 = f32[512,5632]{1,0:T(8,128)} fusion(f32[1024,5632]{1,0:T(8,128)} %all-gather.22.cloned.1.call-done, f32[512,1024]{1,0:T(8,128)} %get-tuple-element.2273, f32[1024]{0:T(1024)S(1)} %bitcast.785, f32[512]{0:T(512)S(1)} %fusion.243), kind=kOutput, calls=%fused_computation.323 | convolution fusion | flops 35434528768 | bytes 36706304 | tf_op jit(solution)/shard_map/jvp()/dot_general | solution.py:45
  1165.8 32.9 %all-gather.24.cloned.1.call-done = f32[2816,1024]{1,0:T(8,128)} async-done(((f32[704,1024]{1,0:T(8,128)}), f32[2816,1024]{1,0:T(8,128)}) %all-gather.24.cloned.1.call-update) | async-done | bytes 11534352 | tf_op jit(solution)/shard_map/all_gather | solution.py:196
  1226.7 42.8 %fusion.164 = f32[512,1024]{1,0:T(8,128)} fusion(f32[1024,5632]{1,0:T(8,128)} %all-gather.22.cloned.1.call-done, f32[512,2816]{1,0:T(8,128)} %get-tuple-element.2318, f32[512,2816]{1,0:T(8,128)} %get-tuple-element.2317), kind=kOutput, calls=%fused_computation.235 | convolution fusion | flops 35436363776 | bytes 36700160 | tf_op jit(solution)/shard_map/transpose(jvp())/dot_general | solution.py:45
  1436.5 47.9 %fusion.163 = f32[1024,5632]{1,0:T(8,128)} fusion(f32[512,2816]{1,0:T(8,128)} %get-tuple-element.2318, f32[512,2816]{1,0:T(8,128)S(1)} %bitcast.794, f32[512,1024]{1,0:T(8,128)S(1)} %copy-done.21, f32[1024]{0:T(1024)S(1)} %bitcast.788, f32[512]{0:T(512)S(1)} %fusion.243), kind=kOutput, calls=%fused_computation.234 | convolution fusion | flops 35437412352 | bytes 36706304 | tf_op jit(solution)/shard_map/transpose(jvp())/dot_general | solution.py:45
  1510.7 708.1 %while.121 = (s32[]{:T(128)}, f32[8,128,384]{2,1,0:T(8,128)S(1)}, f32[8,64,8,128]{3,2,1,0:T(8,128)}, f32[8,64,8,128]{3,2,1,0:T(8,128)}, f32[8,64,8,384]{3,2,1,0:...) while((s32[]{:T(128)}, f32[8,128,384]{2,1,0:T(8,128)S(1)}, ...), condition=%wide.region_27.28_spmd.clone, body=%wide.region_18.27_spmd.clone.sunk | while | flops 2648184320 | bytes 42815636 | solution.py:135
  1516.1 39.3 %custom-call.52 = f32[8,1,64,64]{2,3,1,0:T(8,128)S(1)} custom-call(f32[8,1,64,64]{3,2,1,0:T(8,128)S(1)} %select_bitcast_fusion.3), custom_call_target="InvertDiagBlocksLowerTriangular" | custom-call | tf_op jit(solution)/shard_map/transpose(jvp())/while/body/eval_jaxpr/jit(_solve_triangular)/vmap()/triangular_solve | solution.py:115
  1605.1 39.3 %custom-call.52 = f32[8,1,64,64]{2,3,1,0:T(8,128)S(1)} custom-call(f32[8,1,64,64]{3,2,1,0:T(8,128)S(1)} %select_bitcast_fusion.3), custom_call_target="InvertDiagBlocksLowerTriangular" | custom-call | tf_op jit(solution)/shard_map/transpose(jvp())/while/body/eval_jaxpr/jit(_solve_triangular)/vmap()/triangular_solve | solution.py:115
  1693.7 39.3 %custom-call.52 = f32[8,1,64,64]{2,3,1,0:T(8,128)S(1)} custom-call(f32[8,1,64,64]{3,2,1,0:T(8,128)S(1)} %select_bitcast_fusion.3), custom_call_target="InvertDiagBlocksLowerTriangular" | custom-call | tf_op jit(solution)/shard_map/transpose(jvp())/while/body/eval_jaxpr/jit(_solve_triangular)/vmap()/triangular_solve | solution.py:115
  1783.2 39.3 %custom-call.52 = f32[8,1,64,64]{2,3,1,0:T(8,128)S(1)} custom-call(f32[8,1,64,64]{3,2,1,0:T(8,128)S(1)} %select_bitcast_fusion.3), custom_call_target="InvertDiagBlocksLowerTriangular" | custom-call | tf_op jit(solution)/shard_map/transpose(jvp())/while/body/eval_jaxpr/jit(_solve_triangular)/vmap()/triangular_solve | solution.py:115
  1871.5 39.3 %custom-call.52 = f32[8,1,64,64]{2,3,1,0:T(8,128)S(1)} custom-call(f32[8,1,64,64]{3,2,1,0:T(8,128)S(1)} %select_bitcast_fusion.3), custom_call_target="InvertDiagBlocksLowerTriangular" | custom-call | tf_op jit(solution)/shard_map/transpose(jvp())/while/body/eval_jaxpr/jit(_solve_triangular)/vmap()/triangular_solve | solution.py:115
  1959.5 39.3 %custom-call.52 = f32[8,1,64,64]{2,3,1,0:T(8,128)S(1)} custom-call(f32[8,1,64,64]{3,2,1,0:T(8,128)S(1)} %select_bitcast_fusion.3), custom_call_target="InvertDiagBlocksLowerTriangular" | custom-call | tf_op jit(solution)/shard_map/transpose(jvp())/while/body/eval_jaxpr/jit(_solve_triangular)/vmap()/triangular_solve | solution.py:115
  2047.5 39.3 %custom-call.52 = f32[8,1,64,64]{2,3,1,0:T(8,128)S(1)} custom-call(f32[8,1,64,64]{3,2,1,0:T(8,128)S(1)} %select_bitcast_fusion.3), custom_call_target="InvertDiagBlocksLowerTriangular" | custom-call | tf_op jit(solution)/shard_map/transpose(jvp())/while/body/eval_jaxpr/jit(_solve_triangular)/vmap()/triangular_solve | solution.py:115
  2135.6 39.3 %custom-call.52 = f32[8,1,64,64]{2,3,1,0:T(8,128)S(1)} custom-call(f32[8,1,64,64]{3,2,1,0:T(8,128)S(1)} %select_bitcast_fusion.3), custom_call_target="InvertDiagBlocksLowerTriangular" | custom-call | tf_op jit(solution)/shard_map/transpose(jvp())/while/body/eval_jaxpr/jit(_solve_triangular)/vmap()/triangular_solve | solution.py:115
  2294.3 31.3 %fusion.202 = f32[1024,4096]{1,0:T(8,128)} fusion(f32[512,4096]{1,0:T(8,128)} %scatter-add.4, f32[1,512,1024]{2,1,0:T(8,128)S(1)} %copy-done.2, f32[1024]{0:T(1024)S(1)} %bitcast.754, f32[512]{0:T(512)S(1)} %copy-done.35), kind=kOutput, calls=%fused_computation.330 | convolution fusion | flops 25770852352 | bytes 27269120 | tf_op jit(solution)/shard_map/transpose(jvp())/dot_general | solution.py:45
  2331.3 119.8 %reduce-scatter.10.cloned.1.call-done = f32[256,4096]{1,0:T(8,128)} async-done(((f32[1024,4096]{1,0:T(8,128)}), f32[256,4096]{1,0:T(8,128)}) %reduce-scatter.10.cloned.1.call-update) | async-done | bytes 4194320 | tf_op jit(solution)/shard_map/reduce_scatter | solution.py:335
  2484.9 33.7 %multiply_reduce_fusion.11 = (f32[1024]{0:T(1024)S(1)}, f32[512]{0:T(512)S(1)}, f32[]{:T(128)}, f32[512,1024]{1,0:T(8,128)}) fusion(f32[1,512,1024]{2,1,0:T(8,128)S(1)} %copy-done.2, f32[512]{0:T(512)S(1)} %copy-done.35, f32[1024]{0:T(1024)S(1)} %bitcast.756, f32[512,4096]{1,0:T(8,128)} %scatter-add.4, f32[1024,4096]{1,0:T(8,128)} %all-gather.16.cloned.1.call-done, ...), kind=kOutput, calls=%fused_computation.305 | convolution fusion | flops 25775044608 | bytes 33566724 | tf_op jit(solution)/shard_map/transpose(jvp())/dot_general | solution.py:45
  2521.3 43.9 %psum.111 = f32[4]{0:T(128)S(1)} all-reduce(f32[4]{0:T(128)S(1)} %pad_maximum_fusion.1), channel_id=1, replica_groups=mesh['seq'=8,'fsdp'=4] {'seq','fsdp'}, use_global_device_ids=true, to_apply=%region_71.72 | all-reduce | flops 4 | bytes 32 | tf_op jit(solution)/shard_map/psum | solution.py:268
  2583.3 41.0 %all-reduce.33 = (f32[256]{0:T(256)}, f32[256,16]{0,1:T(8,128)}, f32[4,1024]{1,0:T(4,128)}, f32[2]{0:T(128)}, f32[2]{0:T(128)}, /*index=5*/f32[2]{0:T(128)}, f32[64]{0:T(128)}, f32[256]{0:T(256)}) all-reduce(f32[256]{0:T(256)S(1)} %dynamic-slice.13, ...), channel_id=1, replica_groups=mesh['seq'=8,'fsdp'=4] {'seq'}, use_global_device_ids=true, to_apply=%region_33.34 | all-reduce | flops 8774 | bytes 70192 | tf_op jit(solution)/shard_map/psum | solution.py:363
  2624.3 412.1 %all-reduce.39.cloned.1.call-done = (f32[256,4096]{1,0:T(8,128)}, f32[256,2048]{1,0:T(8,128)}, f32[512,1024]{1,0:T(8,128)}, f32[256,5632]{1,0:T(8,128)}, f32[704,1024]{1,0:T(8,128)}) async-done(((f32[256,4096]{1,0:T(8,128)}, f32[256,2048]{1,0:T(8,128)}, f32[512,1024]{1,0:T(8,128)}, f32[256,5632]{1,0:T(8,128)}, f32[704,1024]{1,0:T(8,128)}), (f32[256,4096]{1,0:T(8,128)}, f32[256,2048]{1,0:T(8,128)}, ...) | async-done | bytes 17039376 | tf_op jit(solution)/shard_map/psum | solution.py:363
  (994 shorter events, 1196.3 us)
Async XLA Ops:
  7.3 111.5 %all-gather.16.cloned.1.call-start = ((), (), s32[]{:S(2)}) async-start(), calls=%async_computation.7 | async-start | bytes 20971520 | tf_op jit(solution)/shard_map/all_gather | solution.py:185
  8.0 718.3 %all-gather.18.cloned.1.call-start = ((), (), s32[]{:S(2)}) async-start(), calls=%async_computation.8 | async-start | bytes 10485760 | tf_op jit(solution)/shard_map/all_gather | solution.py:186
  8.8 783.9 %all-gather.26.cloned.1.call-start = ((), (), s32[]{:S(2)}) async-start(), calls=%async_computation.18 | async-start | bytes 4718592 | tf_op jit(solution)/shard_map/all_gather | solution.py:32
  9.1 1357.8 %copy-start.34 = (f32[512]{0:T(512)}, f32[512]{0:T(512)S(1)}, u32[]{:S(2)}) copy-start(f32[512]{0:T(512)S(1)} %fusion.242) | copy-start | bytes 6148
  15.1 1351.7 %copy-start.30 = (f32[4,1,256]{2,1,0:T(1,128)}, f32[4,1,256]{2,1,0:T(1,128)S(1)}, u32[]{:S(2)}) copy-start(f32[4,1,256]{2,1,0:T(1,128)S(1)} %all-gather.4) | copy-start | bytes 12292
  16.0 133.0 %copy-start.75 = (f32[3]{0:T(128)}, f32[3]{0:T(128)S(1)}, u32[]{:S(2)}) copy-start(f32[3]{0:T(128)S(1)} %compare_convert_fusion) | copy-start | bytes 40
  16.7 141.0 %copy-start.59 = (f32[512]{0:T(512)}, f32[512]{0:T(512)S(1)}, u32[]{:S(2)}) copy-start(f32[512]{0:T(512)S(1)} %get-tuple-element.2340) | copy-start | bytes 6148
  16.7 141.0 %copy-start.61 = (f32[512]{0:T(512)}, f32[512]{0:T(512)S(1)}, u32[]{:S(2)}) copy-start(f32[512]{0:T(512)S(1)} %get-tuple-element.2341) | copy-start | bytes 6148
  16.7 140.9 %copy-start.63 = (f32[512]{0:T(512)}, f32[512]{0:T(512)S(1)}, u32[]{:S(2)}) copy-start(f32[512]{0:T(512)S(1)} %get-tuple-element.2342) | copy-start | bytes 6148
  22.3 135.4 %copy-start.43 = (f32[1,4096]{1,0:T(1,128)}, f32[1,4096]{1,0:T(1,128)S(1)}, u32[]{:S(2)}) copy-start(f32[1,4096]{1,0:T(1,128)S(1)} %get-tuple-element.2332) | copy-start | bytes 49156
  22.3 135.4 %copy-start.45 = (f32[1,4096]{1,0:T(1,128)}, f32[1,4096]{1,0:T(1,128)S(1)}, u32[]{:S(2)}) copy-start(f32[1,4096]{1,0:T(1,128)S(1)} %get-tuple-element.2333) | copy-start | bytes 49156
  22.3 135.4 %copy-start.47 = (f32[1,4096]{1,0:T(1,128)}, f32[1,4096]{1,0:T(1,128)S(1)}, u32[]{:S(2)}) copy-start(f32[1,4096]{1,0:T(1,128)S(1)} %get-tuple-element.2334) | copy-start | bytes 49156
  22.4 135.4 %copy-start.57 = (f32[1,4096]{1,0:T(1,128)}, f32[1,4096]{1,0:T(1,128)S(1)}, u32[]{:S(2)}) copy-start(f32[1,4096]{1,0:T(1,128)S(1)} %get-tuple-element.2331) | copy-start | bytes 49156
  38.8 110.3 %copy-start.36 = (f32[1024,16]{0,1:T(8,128)}, f32[1024,16]{0,1:T(8,128)S(1)}, u32[]{:S(2)}) copy-start(f32[1024,16]{0,1:T(8,128)S(1)} %all_gather.74) | copy-start | bytes 196612
  42.2 106.8 %copy-start.41 = (f32[512,16]{0,1:T(8,128)}, f32[512,16]{0,1:T(8,128)S(1)}, u32[]{:S(2)}) copy-start(f32[512,16]{0,1:T(8,128)S(1)} %fusion.206) | copy-start | bytes 98308
  42.4 114.6 %copy-start.53 = (f32[512,8]{0,1:T(8,128)}, f32[512,8]{0,1:T(8,128)S(1)}, u32[]{:S(2)}) copy-start(f32[512,8]{0,1:T(8,128)S(1)} %get-tuple-element.2336) | copy-start | bytes 49156
  152.4 5.3 collective-permute-start
  718.1 200.4 %all-gather.28.cloned.1.call-start = ((), (), s32[]{:S(2)}) async-start(), calls=%async_computation.19 | async-start | bytes 9437184 | tf_op jit(solution)/shard_map/all_gather | solution.py:32
  719.2 257.2 %all-gather.20.cloned.1.call-start = ((), (), s32[]{:S(2)}) async-start(), calls=%async_computation.9 | async-start | bytes 10485760 | tf_op jit(solution)/shard_map/all_gather | solution.py:193
  719.8 401.2 %all-gather.22.cloned.1.call-start = ((), (), s32[]{:S(2)}) async-start(), calls=%async_computation.10 | async-start | bytes 28835840 | tf_op jit(solution)/shard_map/all_gather | solution.py:195
  720.4 478.4 %all-gather.24.cloned.1.call-start = ((), (), s32[]{:S(2)}) async-start(), calls=%async_computation.11 | async-start | bytes 14417920 | tf_op jit(solution)/shard_map/all_gather | solution.py:196
  721.2 763.3 %all-gather.30.cloned.1.call-start = ((), (), s32[]{:S(2)}) async-start(), calls=%async_computation.20 | async-start | bytes 4718592 | tf_op jit(solution)/shard_map/all_gather | solution.py:32
  742.9 741.6 %all-gather.32.cloned.1.call-start = ((), (), s32[]{:S(2)}) async-start(), calls=%async_computation.21 | async-start | bytes 9437184 | tf_op jit(solution)/shard_map/all_gather | solution.py:32
  1343.4 987.8 %reduce-scatter.16.cloned.1.call-start = ((), (), s32[]{:S(2)}) async-start(), calls=%async_computation.15 | async-start | bytes 10485760 | tf_op jit(solution)/shard_map/reduce_scatter | solution.py:343
  1361.4 969.8 %reduce-scatter.12.cloned.1.call-start = ((), (), s32[]{:S(2)}) async-start(), calls=%async_computation.13 | async-start | bytes 10485760 | tf_op jit(solution)/shard_map/reduce_scatter | solution.py:336
  1397.6 933.7 %reduce-scatter.20.cloned.1.call-start = ((), (), s32[]{:S(2)}) async-start(), calls=%async_computation.17 | async-start | bytes 14417920 | tf_op jit(solution)/shard_map/reduce_scatter | solution.py:346
  1423.5 907.8 %reduce-scatter.18.cloned.1.call-start = ((), (), s32[]{:S(2)}) async-start(), calls=%async_computation.16 | async-start | bytes 28835840 | tf_op jit(solution)/shard_map/reduce_scatter | solution.py:345
  1484.4 966.7 %reduce-scatter.10.cloned.1.call-start = ((), (), s32[]{:S(2)}) async-start(), calls=%async_computation.12 | async-start | bytes 20971520 | tf_op jit(solution)/shard_map/reduce_scatter | solution.py:335
  2270.9 20.8 collective-permute-start.1
  2325.6 256.4 %reduce-scatter.22.cloned.1.call-start = ((), (), s32[]{:S(2)}) async-start(), calls=%async_computation.22 | async-start | bytes 2621440
  2329.1 254.2 %reduce-scatter.14.cloned.1.call-start = ((), (), s32[]{:S(2)}) async-start(), calls=%async_computation.14 | async-start | bytes 81920 | tf_op jit(solution)/shard_map/reduce_scatter | solution.py:337
  2331.2 705.2 %all-reduce.39.cloned.1.call-start = ((), (), s32[]{:S(2)}) async-start(), calls=%async_computation.23 | async-start | bytes 34078720 | tf_op jit(solution)/shard_map/psum | solution.py:363
  (83 other events, 1142.1 us)
Sparse Core Ops, SparseCore 0:
  9.7 109.0 all-gather.15
  120.4 58.3 all-gather.17
  718.2 74.4 all-gather.25
  795.2 123.1 all-gather.27
  919.9 56.4 all-gather.19
  977.8 143.2 all-gather.21
  1122.6 76.1 all-gather.23
  1200.9 73.3 all-gather.29
  1343.5 124.9 all-gather.31
  1470.9 69.8 reduce-scatter.15
  1543.6 71.7 reduce-scatter.11
  1617.9 92.4 reduce-scatter.19
  1713.0 166.7 reduce-scatter.17
  2325.7 125.3 reduce-scatter.9
  2454.1 31.4 reduce-scatter.21
  2488.5 19.4 reduce-scatter.13
  2513.0 523.3 all-reduce.38
where the time goes:
time: 3070 us; the launch traced here: 3060 us
  waiting for transfers between devices  971 us (32%)
  matrix products  921 us (30%)
  other arithmetic  807 us (26%)
  local copies, waits for them, and re-layouts  203 us (7%)
  blocking collectives  127 us (4%)
    another operation x32, other arithmetic, block_step(): jax.scipy.linalg.solve_triangular(unit_block[None] + lower_mix, targets,...  637 us
    dot_general x18, matrix products, matmul(): jnp.dot(left, right, precision=HIGH_PRECISION, preferred_element_type=jnp...  454 us
    psum x1, waiting for transfers between devices, on_device(): lax.psum((share_norm, share_qkv, share_gate, share_decay_beta, share_conv...  412 us
    all_gather x4, waiting for transfers between devices, entering(): gathered = jax.tree.map(lambda a: lax.all_gather(a, axis), part)  176 us
    all_gather x1, waiting for transfers between devices, on_device(): lax.all_gather(up_weight, 'fsdp', axis=0, tiled=True)  126 us
    reduce_scatter x1, waiting for transfers between devices, on_device(): lax.psum_scatter(grad_qkv, 'fsdp', scatter_dimension=0, tiled=True)  120 us
    dot_general x24, matrix products, block_step(): jnp.einsum('thd,hdw->htw', key_blk, carried_state, precision=HIGH_PRECISION)  79.2 us
    dot_general x24, matrix products, block_step(): jnp.einsum('thd,hdw->htw', query_blk, carried_state, precision=HIGH_PRECI...  77.9 us
  transfers between devices with their start and end apart: 19, of which 9 were waited for; matrix products, arithmetic and copies ran while one was open for 62% of the time, Pallas kernels for 0%

commit v1 on v0

v1 whole, which is shorter than its diff:
```python
from functools import partial

import jax
import jax.numpy as jnp
from jax import lax
from jax.experimental import pallas as pl
from jax.experimental.pallas import tpu as pltpu
from jax.sharding import PartitionSpec as P

D = 1024
H = 8
DK = 128
DV = 256
FF = 2816
CONV = 4
C = 64

NORM_EPS = 1e-05
UNIT_EPS = 1e-06
F32 = jnp.float32
BF16 = jnp.bfloat16
VMEM_BYTES = 48 * 1024 * 1024

NN = (((1,), (0,)), ((), ()))
NT = (((1,), (1,)), ((), ()))
TN = (((0,), (0,)), ((), ()))


def swapped(block, axis, distance):
    return lax.ppermute(block, axis, [(i, i ^ distance) for i in range(lax.axis_size(axis))])


def passed_along(block, axis, distance):
    devices = range(lax.axis_size(axis))
    route = [(i - distance, i) for i in devices if i - distance in devices]
    return lax.ppermute(block, axis, route)


def rows_of(block, start, size):
    return lax.dynamic_slice_in_dim(block, start, size, 0)


def columns_of(block, start, size):
    return lax.dynamic_slice_in_dim(block, start, size, 1)


def gathered_weight(shard, bit):
    half = shard.shape[0] // 2
    near = swapped(shard, "fsdp", 1)
    far_a = swapped(rows_of(shard, bit * half, half), "fsdp", 2)
    far_b = swapped(far_a, "seq", 1)
    return [
        shard,
        near,
        far_a,
        far_b,
        swapped(far_a, "fsdp", 1),
        swapped(far_b, "fsdp", 1),
    ]


def block_starts(shard_rows, place, bit):
    half = shard_rows // 2
    far, last = (place ^ 2) * shard_rows, (place ^ 3) * shard_rows
    return [
        (place * shard_rows, shard_rows),
        ((place ^ 1) * shard_rows, shard_rows),
        (far + bit * half, half),
        (far + (1 - bit) * half, half),
        (last + bit * half, half),
        (last + (1 - bit) * half, half),
    ]


def reduced_shard(grads, bits):
    first = grads[0] + swapped(grads[1], "fsdp", 1)
    second = grads[2] + swapped(grads[3], "fsdp", 1)
    total = first + swapped(second, "fsdp", 2)
    for step, bit in enumerate(bits):
        half = total.shape[0] // 2
        kept = rows_of(total, bit * half, half)
        total = kept + swapped(rows_of(total, (1 - bit) * half, half), "seq", 1 << step)
    for step, bit in reversed(list(enumerate(bits))):
        half = total.shape[0]
        other = swapped(total, "seq", 1 << step)
        whole = jnp.zeros((2 * half, total.shape[1]), F32)
        whole = lax.dynamic_update_slice_in_dim(whole, total, bit * half, 0)
        total = lax.dynamic_update_slice_in_dim(whole, other, (1 - bit) * half, 0)
    return total


def summed_small(rows4, bits):
    near = swapped(rows4[1::2], "fsdp", 1)
    pair = rows4[0::2] + near
    total = pair[0] + swapped(pair[1], "fsdp", 2)
    for step in range(len(bits)):
        total = total + swapped(total, "seq", 1 << step)
    return total


def dot(left, right, dims=NN):
    return lax.dot_general(
        left, right, dims, precision=lax.Precision.HIGH, preferred_element_type=F32
    )


def split(x):
    high = x.astype(BF16)
    return high, (x - high.astype(F32)).astype(BF16)


def dot3(left, right, dims=NN):
    lh, ll = split(left)
    rh, rl = split(right)
    one = partial(lax.dot_general, dimension_numbers=dims, preferred_element_type=F32)
    return one(lh, rh) + (one(lh, rl) + one(ll, rh))


def rms_norm(rows, gain):
    return rows * lax.rsqrt(jnp.mean(rows * rows, axis=-1, keepdims=True) + NORM_EPS) * gain


def unit_rows(rows):
    return rows * lax.rsqrt(jnp.sum(rows * rows, axis=-1, keepdims=True) + UNIT_EPS)


def front(mixed_in, rim_rows, decay_beta, conv_weight, decay_log, decay_bias, beta_bias, counts):
    tokens_here = mixed_in.shape[0]
    extended = jnp.concatenate([rim_rows, mixed_in], 0)
    extended_counts = jnp.concatenate([jnp.zeros((CONV - 1,), jnp.int32), counts], 0)
    convolved = conv_weight[0] * mixed_in
    for shift_by in range(1, CONV):
        offset = CONV - 1 - shift_by
        same = (counts == extended_counts[offset : offset + tokens_here]).astype(F32)
        convolved = (
            convolved
            + conv_weight[shift_by] * extended[offset : offset + tokens_here] * same[:, None]
        )
    convolved = jax.nn.silu(convolved)
    width_k = H * DK
    queries = unit_rows(convolved[:, :width_k].reshape(tokens_here, H, DK)) * DK ** (-0.5)
    key_rows = unit_rows(convolved[:, width_k : 2 * width_k].reshape(tokens_here, H, DK))
    values = convolved[:, 2 * width_k :]
    log_decay = -jnp.exp(decay_log) * jax.nn.softplus(decay_beta[:, :H] + decay_bias)
    beta_rows = jax.nn.sigmoid(decay_beta[:, H:] + beta_bias)
    return (
        queries.reshape(tokens_here, width_k),
        key_rows.reshape(tokens_here, width_k),
        values,
        log_decay,
        beta_rows,
    )


def gate_heads(head_outputs, gate_rows, head_gain):
    tokens_here = head_outputs.shape[0]
    heads = head_outputs.reshape(tokens_here, H, DV)
    scaled = heads * lax.rsqrt(jnp.mean(heads * heads, axis=-1, keepdims=True) + NORM_EPS)
    gated = scaled * head_gain * jax.nn.silu(gate_rows.reshape(tokens_here, H, DV))
    return gated.reshape(tokens_here, H * DV)


def swiglu(lifted):
    return jax.nn.silu(lifted[:, :FF]) * lifted[:, FF:]


def call(kernel, grid, in_specs, out_specs, out_shapes, scratch=(), name=None, flops=0, bytes_=0):
    return pl.pallas_call(
        kernel,
        grid=grid,
        in_specs=in_specs,
        out_specs=out_specs,
        out_shape=out_shapes,
        scratch_shapes=scratch,
        name=name,
        compiler_params=pltpu.CompilerParams(
            vmem_limit_bytes=VMEM_BYTES,
            dimension_semantics=("arbitrary",) * len(grid),
        ),
        cost_estimate=pl.CostEstimate(flops=flops, bytes_accessed=bytes_, transcendentals=0),
    )


def shape(*dims):
    return jax.ShapeDtypeStruct(dims, F32)


def head_block(tokens, width):
    return pl.BlockSpec((tokens, width), lambda h: (0, h))


def per_head(*dims):
    return pl.BlockSpec((1,) + dims, lambda h: (h,) + (0,) * len(dims))


def per_chunk_head(chunks, *dims):
    return pl.BlockSpec((chunks, 1) + dims, lambda h: (0, h) + (0,) * len(dims))


def positions():
    row = lax.broadcasted_iota(jnp.int32, (C, C), 0)
    column = lax.broadcasted_iota(jnp.int32, (C, C), 1)
    return row, column


CUM, BETA, LEAD, CLOSE, COUNT = 0, 1, 2, 3, 4


def ratios_of(cols, rows, at):
    row, column = positions()
    spread = cols[0, at, CUM : CUM + 1] - rows[0, CUM : CUM + 1, at]
    same = cols[0, at, COUNT : COUNT + 1] == rows[0, COUNT : COUNT + 1, at]
    return jnp.where(same & (row >= column), jnp.exp(jnp.minimum(spread, 0.0)), 0.0)


def mixes_kernel(q, k, cols, rows, lower, within):
    row, column = positions()
    for c in range(q.shape[0] // C):
        at = pl.ds(c * C, C)
        key = k[at, :]
        dots = dot3(jnp.concatenate([key, q[at, :]], 0), key, NT)
        ratios = ratios_of(cols, rows, at)
        lower[c, 0] = jnp.where(row > column, ratios, 0.0) * dots[:C]
        within[c, 0] = ratios * dots[C:]


def inverse_kernel(lower, inverse):
    lanes = lower.shape[2]
    inverse[...] = jnp.zeros(inverse.shape, F32)
    for base in range(0, C, 4):
        width = (base + 4 + 7) // 8 * 8
        place = lax.broadcasted_iota(jnp.int32, (width, lanes), 0)
        found = tuple(jnp.where(place == base + n, 1.0, 0.0).astype(F32) for n in range(4))

        def earlier(j, found):
            known = inverse[j, :width, :]
            return tuple(f - lower[base + n, pl.ds(j, 1), :] * known for n, f in enumerate(found))

        if base:
            found = lax.fori_loop(0, base, earlier, found, unroll=4)
        done = []
        for n in range(4):
            one = found[n]
            for m in range(n):
                one = one - lower[base + n, base + m : base + m + 1, :] * done[m]
            done.append(one)
            inverse[base + n, :width, :] = one


def pieces_kernel(q, k, v, cols, rows, inv, within, u_out, w_out, qm_out, trans_out, a_out, b_out):
    row = lax.broadcasted_iota(jnp.int32, (DK, DK), 0)
    column = lax.broadcasted_iota(jnp.int32, (DK, DK), 1)
    carried = None
    for c in range(q.shape[0] // C):
        at = pl.ds(c * C, C)
        beta, lead = cols[0, at, BETA : BETA + 1], cols[0, at, LEAD : LEAD + 1]
        close = cols[0, at, CLOSE : CLOSE + 1]
        last = cols[0, c * C + C - 1 : c * C + C, LEAD : LEAD + 1]
        key = k[at, :]
        solved = dot3(inv[c, 0], jnp.concatenate([v[at, :], lead * key], 1))
        mix = within[c, 0] * rows[0, BETA : BETA + 1, at]
        w = solved[:, DV:]
        u_out[at, :] = solved[:, :DV]
        w_out[at, :] = w
        qm_out[at, :] = lead * q[at, :] - dot3(mix, w)
        both = dot3(close * beta * key, solved, TN)
        trans = jnp.where(row == column, last, 0.0) - both[:, DV:]
        trans_out[c, 0] = trans
        if carried is None:
            carried = jnp.concatenate([both[:, :DV], trans], 1)
        else:
            carried = dot3(trans, carried)
            carried = jnp.concatenate([carried[:, :DV] + both[:, :DV], carried[:, DV:]], 1)
    b_out[0] = carried[:, :DV]
    a_out[0] = carried[:, DV:]


def outputs_kernel(s_in, q, k, u, w, cols, rows, within, out, residue, states):
    state = s_in[0]
    for c in range(q.shape[0] // C):
        at = pl.ds(c * C, C)
        beta, lead = cols[0, at, BETA : BETA + 1], cols[0, at, LEAD : LEAD + 1]
        close = cols[0, at, CLOSE : CLOSE + 1]
        last = cols[0, c * C + C - 1 : c * C + C, LEAD : LEAD + 1]
        states[c, 0] = state
        read = dot3(jnp.concatenate([w[at, :], lead * q[at, :]], 0), state)
        left = u[at, :] - read[:C]
        residue[at, :] = left
        out[at, :] = read[C:] + dot3(within[c, 0] * rows[0, BETA : BETA + 1, at], left)
        state = last * state + dot3(close * beta * k[at, :], left, TN)


def adjoint_piece_kernel(qm, d_out, trans, direct):
    carried = None
    for c in reversed(range(qm.shape[0] // C)):
        at = pl.ds(c * C, C)
        here = dot3(qm[at, :], d_out[at, :], TN)
        carried = here if carried is None else here + dot3(trans[c, 0], carried, TN)
    direct[0] = carried


def adjoint_kernel(
    z_in, q, k, cols, rows, inv, lower, within, residue, states, d_out,
    dq, dk, dv, dcols, drows,
):
    z = z_in[0]
    row, column = positions()
    for c in reversed(range(q.shape[0] // C)):
        at = pl.ds(c * C, C)
        beta, lead = cols[0, at, BETA : BETA + 1], cols[0, at, LEAD : LEAD + 1]
        close = cols[0, at, CLOSE : CLOSE + 1]
        last = cols[0, c * C + C - 1 : c * C + C, LEAD : LEAD + 1]
        beta_row = rows[0, BETA : BETA + 1, at]
        key, query, left, state = k[at, :], q[at, :], residue[at, :], states[c, 0]
        ratios = ratios_of(cols, rows, at)
        grad = d_out[at, :]
        d_left = dot3(within[c, 0] * beta_row, grad, TN) + dot3(close * beta * key, z)
        e = dot3(inv[c, 0], d_left, TN)
        dv[at, :] = e
        both = jnp.concatenate([grad, e], 0)
        back = dot3(both, state, NT)
        d_mix = dot3(both, left, NT)
        d_within = jnp.where(row >= column, d_mix[:C], 0.0)
        d_lower = jnp.where(row > column, -d_mix[C:], 0.0)
        d_close = dot3(left, z, NT)
        d_last = jnp.sum(z * state)
        z = last * z + dot3(jnp.concatenate([lead * query, -lead * key], 0), both, TN)
        of_query = d_within * ratios * beta_row
        of_key = d_lower * ratios * beta_row
        pair = jnp.concatenate([of_query, of_key], 0)
        forth = dot3(pair, key)
        dq[at, :] = lead * back[:C] + forth[:C]
        dk[at, :] = (
            close * beta * d_close
            - lead * back[C:]
            + forth[C:]
            + dot3(pair, jnp.concatenate([query, key], 0), TN)
        )
        share = d_within * within[c, 0] + d_lower * lower[c, 0]
        drows[0, 0:1, at] = jnp.sum(share, 0, keepdims=True)
        dcols[0, at, 0:1] = jnp.sum(share * beta_row, 1, keepdims=True)
        dcols[0, at, 1:2] = jnp.sum(key * d_close, 1, keepdims=True)
        dcols[0, at, 2:3] = jnp.sum(back[:C] * query - back[C:] * key, 1, keepdims=True)
        dcols[0, at, 3:4] = jnp.full((C, 1), d_last, F32)


def states_kernel(me, maps, out):
    count = maps.shape[0]
    state = jnp.zeros((DK, DV), F32)
    for piece in range(count):
        slot = piece ^ me[0]
        out[slot] = state
        if piece < count - 1:
            held = maps[slot]
            state = dot3(held[:, DV:], state) + held[:, :DV]


def adjoints_kernel(me, maps, direct, out):
    count = maps.shape[0]
    z = jnp.zeros((DK, DV), F32)
    for piece in reversed(range(count)):
        slot = piece ^ me[0]
        out[slot] = z
        if piece:
            z = dot3(maps[slot][:, DV:], z, TN) + direct[slot]


def whole_call(kernel, me, args, out_shape, name):
    return pl.pallas_call(
        kernel,
        grid_spec=pltpu.PrefetchScalarGridSpec(
            num_scalar_prefetch=1,
            grid=(1,),
            in_specs=[pl.BlockSpec(a.shape, lambda i, me: (0, 0, 0)) for a in args],
            out_specs=pl.BlockSpec(out_shape.shape, lambda i, me: (0, 0, 0)),
        ),
        out_shape=out_shape,
        name=name,
        compiler_params=pltpu.CompilerParams(vmem_limit_bytes=VMEM_BYTES),
    )(me.reshape(1), *args)


def heads_apart(whole, me):
    parts = [lax.dynamic_index_in_dim(whole, me, 0, False)]
    for r in range(1, whole.shape[0]):
        parts.append(swapped(lax.dynamic_index_in_dim(whole, me ^ r, 0, False), "seq", r))
    return jnp.stack(parts)


def heads_together(parts, me):
    count = parts.shape[0]
    held = jnp.stack([parts[0]] + [swapped(parts[r], "seq", r) for r in range(1, count)])
    return held[jnp.arange(count) ^ me]


def compose(earlier, later):
    first = jnp.einsum("hij,hjk->hik", later[0], earlier[0], precision=lax.Precision.HIGHEST)
    second = jnp.einsum("hij,hjk->hik", later[0], earlier[1], precision=lax.Precision.HIGHEST)
    return (first, second + later[1])


def entering(part, reverse):
    count, place = lax.axis_size("seq"), lax.axis_index("seq")
    ahead = count - 1 - place if reverse else place
    gathered = jax.tree.map(lambda a: lax.all_gather(a, "seq"), part)
    state = (jnp.broadcast_to(jnp.eye(DK, dtype=F32), part[0].shape), jnp.zeros_like(part[1]))

    def one(step, state):
        source = count - 1 - step if reverse else step
        here = jax.tree.map(lambda a: lax.dynamic_index_in_dim(a, source, 0, False), gathered)
        return compose(state, here)

    return lax.fori_loop(0, ahead, one, state)[1]


def on_device(
    residual_in, doc_starts, out_grad, norm_gain, qkv_weight, gate_weight, decay_beta_weight,
    conv_weight, decay_log, decay_bias, beta_bias, head_gain, out_weight, mlp_gain, up_weight,
    down_weight,
):
    place, piece = lax.axis_index("fsdp"), lax.axis_index("seq")
    pieces = lax.axis_size("seq")
    bits = [(piece >> s) & 1 for s in range(pieces.bit_length() - 1)]
    bit = bits[0]
    rows, starts, cotangent = residual_in[0], doc_starts[0], out_grad[0]
    tokens = rows.shape[0]
    chunks = tokens // C

    small = [norm_gain, decay_beta_weight, conv_weight, decay_log, decay_bias, beta_bias, head_gain, mlp_gain]
    sizes = [a.size for a in small]
    packed = jnp.concatenate([a.reshape(-1) for a in small])
    held = jnp.stack([packed] + [swapped(packed, "fsdp", r) for r in range(1, 4)])
    held = held[jnp.arange(4) ^ place]
    parts, offset = [], 0
    for a, size in zip(small, sizes):
        parts.append(held[:, offset : offset + size].reshape((4,) + a.shape))
        offset += size
    full_norm, full_decay_beta = parts[0].reshape(-1), parts[1].reshape(D, 2 * H)
    full_conv = jnp.transpose(parts[2], (1, 0, 2)).reshape(CONV, -1)
    full_decay_log, full_decay_bias, full_beta_bias = (parts[i].reshape(-1) for i in (3, 4, 5))
    full_head_gain, full_mlp_gain = parts[6].reshape(-1), parts[7].reshape(-1)

    qkv = gathered_weight(qkv_weight, bit)
    gate = gathered_weight(gate_weight, bit)
    out_w = gathered_weight(out_weight, bit)
    up = gathered_weight(up_weight, bit)
    down = gathered_weight(down_weight, bit)

    def forward(x, weight):
        starts_ = block_starts(weight[0].shape[0], place, bit)
        x = jnp.concatenate([columns_of(x, at, size) for at, size in starts_], 1)
        return dot(x, jnp.concatenate(weight, 0))

    def backward_rows(dy, weight):
        shard = weight[0].shape[0]
        starts_ = block_starts(shard, place, bit)
        blocks = dot(dy, jnp.concatenate(weight, 0), NT)
        whole, offset = jnp.zeros((tokens, 4 * shard), F32), 0
        for at, size in starts_:
            whole = lax.dynamic_update_slice_in_dim(
                whole, blocks[:, offset : offset + size], at, 1
            )
            offset += size
        return whole

    def weight_grad(x, dy, shard):
        return [dot(columns_of(x, (place ^ r) * shard, shard), dy, TN) for r in range(4)]

    counts = jnp.cumsum(starts)
    after = jnp.flip(jnp.cumsum(jnp.flip(starts))) - starts
    tail_mask = (after[tokens - CONV + 1 :] == 0).astype(F32)[:, None]
    by_chunk = counts.reshape(chunks, C)
    before = (counts - starts).reshape(chunks, C)[:, :1]
    of_lead = (by_chunk == before).astype(F32)
    of_close = (by_chunk == by_chunk[:, -1:]).astype(F32)

    normed, norm_pull = jax.vjp(rms_norm, rows, full_norm)
    mixed_in = forward(normed, qkv)
    rim_rows = passed_along(mixed_in[tokens - CONV + 1 :] * tail_mask, "seq", 1)
    decay_beta = dot(normed, full_decay_beta)
    gate_rows = forward(normed, gate)
    front_parts, front_pull = jax.vjp(
        partial(front, counts=counts),
        mixed_in, rim_rows, decay_beta, full_conv, full_decay_log, full_decay_bias, full_beta_bias,
    )
    queries, key_rows, values, log_decay, beta = front_parts

    cum = jnp.cumsum(log_decay.reshape(chunks, C, H), 1)
    lead = jnp.exp(cum) * of_lead[:, :, None]
    close = jnp.exp(cum[:, -1:] - cum) * of_close[:, :, None]
    count_cols = jnp.broadcast_to(counts.astype(F32)[:, None], (tokens, H))
    flat = [a.reshape(tokens, H) for a in (cum, beta, lead, close)] + [count_cols]
    rows_in = jnp.stack([a.T for a in flat], 1)
    rows_in = jnp.concatenate([rows_in, jnp.zeros((H, 3, tokens), F32)], 1)
    cols_in = jnp.transpose(rows_in, (0, 2, 1))

    key_spec, value_spec = head_block(tokens, DK), head_block(tokens, DV)
    cols_spec, rows_spec = per_head(tokens, 8), per_head(8, tokens)
    square_spec = per_chunk_head(chunks, C, C)
    state_spec = per_chunk_head(chunks, DK, DV)
    square = shape(chunks, H, C, C)
    lower, within = call(
        mixes_kernel, (H,),
        [key_spec, key_spec, cols_spec, rows_spec],
        [square_spec, square_spec], [square, square], name="mixes",
    )(queries, key_rows, cols_in, rows_in)
    lower_mix = lower * rows_in[:, BETA, :].reshape(H, chunks, C).transpose(1, 0, 2)[:, :, None, :]
    lanes = jnp.transpose(lower_mix.reshape(chunks * H, C, C), (1, 2, 0))
    inverse = pl.pallas_call(
        inverse_kernel,
        out_shape=shape(C, C, chunks * H),
        name="inverse",
        compiler_params=pltpu.CompilerParams(vmem_limit_bytes=VMEM_BYTES),
    )(lanes)
    inverse = jnp.transpose(inverse, (2, 0, 1)).reshape(chunks, H, C, C)
    solved_values, solved_keys, query_map, trans, map_a, map_b = call(
        pieces_kernel, (H,),
        [key_spec, key_spec, value_spec, cols_spec, rows_spec, square_spec, square_spec],
        [value_spec, key_spec, key_spec, per_chunk_head(chunks, DK, DK), per_head(DK, DK), per_head(DK, DV)],
        [shape(tokens, H * DV), shape(tokens, H * DK), shape(tokens, H * DK),
         shape(chunks, H, DK, DK), shape(H, DK, DK), shape(H, DK, DV)],
        name="pieces",
    )(queries, key_rows, values, cols_in, rows_in, inverse, within)

    spread = pieces == H
    if spread:
        maps = heads_apart(jnp.concatenate([map_b, map_a], 2), piece)
        incoming = whole_call(states_kernel, piece, [maps], shape(H, DK, DV), "states")
        state_in = heads_together(incoming, piece)
    else:
        state_in = entering((map_a, map_b), False)
    head_outputs, residues, states = call(
        outputs_kernel, (H,),
        [per_head(DK, DV), key_spec, key_spec, value_spec, key_spec, cols_spec, rows_spec, square_spec],
        [value_spec, value_spec, state_spec],
        [shape(tokens, H * DV), shape(tokens, H * DV), shape(chunks, H, DK, DV)],
        name="outputs",
    )(state_in, queries, key_rows, solved_values, solved_keys, cols_in, rows_in, within)

    gated, gated_pull = jax.vjp(gate_heads, head_outputs, gate_rows, full_head_gain)
    mixer = forward(gated, out_w)
    middle = rows + mixer
    lifted_in, lifted_pull = jax.vjp(rms_norm, middle, full_mlp_gain)
    lifted = forward(lifted_in, up)
    hidden, hidden_pull = jax.vjp(swiglu, lifted)
    branch = forward(hidden, down)
    result = middle + branch
    squares = jnp.stack([jnp.sum(a * a) for a in (rows, mixer, branch, result)])

    grad_down = reduced_shard(weight_grad(hidden, cotangent, FF // 4), bits)
    (d_lifted,) = hidden_pull(backward_rows(cotangent, down))
    grad_up = reduced_shard(weight_grad(lifted_in, d_lifted, D // 4), bits)
    d_middle, grad_mlp_gain = lifted_pull(backward_rows(d_lifted, up))
    d_middle = d_middle + cotangent
    grad_out = reduced_shard(weight_grad(gated, d_middle, H * DV // 4), bits)
    d_heads, d_gate, grad_head_gain = gated_pull(backward_rows(d_middle, out_w))
    grad_gate = reduced_shard(weight_grad(normed, d_gate, D // 4), bits)

    direct = call(
        adjoint_piece_kernel, (H,),
        [key_spec, value_spec, per_chunk_head(chunks, DK, DK)],
        per_head(DK, DV), shape(H, DK, DV), name="adjoint_piece",
    )(query_map, d_heads, trans)
    if spread:
        outgoing = whole_call(
            adjoints_kernel, piece, [maps, heads_apart(direct, piece)], shape(H, DK, DV), "adjoints"
        )
        adjoint_in = heads_together(outgoing, piece)
    else:
        adjoint_in = entering((jnp.swapaxes(map_a, 1, 2), direct), True)
    d_queries, d_keys, d_values, dcols, drows = call(
        adjoint_kernel, (H,),
        [per_head(DK, DV), key_spec, key_spec, cols_spec, rows_spec, square_spec, square_spec,
         square_spec, value_spec, state_spec, value_spec],
        [key_spec, key_spec, value_spec, cols_spec, rows_spec],
        [shape(tokens, H * DK), shape(tokens, H * DK), shape(tokens, H * DV),
         shape(H, tokens, 8), shape(H, 8, tokens)],
        name="adjoint",
    )(adjoint_in, queries, key_rows, cols_in, rows_in, inverse, lower, within, residues, states, d_heads)

    def by_token(a):
        return a.T.reshape(chunks, C, H)

    of_share, of_row = by_token(drows[:, 0, :]), by_token(dcols[:, :, 0])
    of_closing, of_leading = by_token(dcols[:, :, 1]), by_token(dcols[:, :, 2])
    of_last = by_token(dcols[:, :, 3])[:, -1:]
    beta_ = beta.reshape(chunks, C, H)
    d_beta = of_share + close * of_closing
    closing = close * beta_ * of_closing
    d_cum = of_row - beta_ * of_share + lead * of_leading - closing
    ending = jnp.sum(closing, 1, keepdims=True) + lead[:, -1:] * of_last
    d_cum = d_cum + jnp.pad(ending, ((0, 0), (C - 1, 0), (0, 0)))
    d_log = jnp.flip(jnp.cumsum(jnp.flip(d_cum, 1), 1), 1)

    (d_mixed, d_rim, d_decay_beta, grad_conv, grad_decay_log, grad_decay_bias, grad_beta_bias) = (
        front_pull(
            (d_queries, d_keys, d_values, d_log.reshape(tokens, H), d_beta.reshape(tokens, H))
        )
    )
    returned = passed_along(d_rim, "seq", -1)
    d_mixed = d_mixed.at[tokens - CONV + 1 :].add(returned * tail_mask)
    grad_qkv = reduced_shard(weight_grad(normed, d_mixed, D // 4), bits)
    grad_decay_beta = dot(normed, d_decay_beta, TN)
    d_normed = (
        backward_rows(d_mixed, qkv)
        + backward_rows(d_gate, gate)
        + dot(d_decay_beta, full_decay_beta, NT)
    )
    d_rows, grad_norm = norm_pull(d_normed)
    row_grad = d_rows + d_middle

    small_grads = [
        grad_norm.reshape(4, -1),
        grad_decay_beta.reshape(4, -1),
        jnp.transpose(grad_conv.reshape(CONV, 4, -1), (1, 0, 2)).reshape(4, -1),
        grad_decay_log.reshape(4, -1),
        grad_decay_bias.reshape(4, -1),
        grad_beta_bias.reshape(4, -1),
        grad_head_gain.reshape(4, -1),
        grad_mlp_gain.reshape(4, -1),
        jnp.broadcast_to(squares, (4, 4)),
    ]
    rows4 = jnp.concatenate(small_grads, 1)[jnp.arange(4) ^ place]
    summed = summed_small(rows4, bits)
    out_small, offset = [], 0
    for a, size in zip(small, sizes):
        out_small.append(summed[offset : offset + size].reshape(a.shape))
        offset += size
    rms_values = jnp.sqrt(summed[offset:] / (pieces * lax.axis_size("fsdp") * tokens * D))

    return (
        result[None],
        row_grad[None],
        out_small[0],
        grad_qkv,
        grad_gate,
        out_small[1],
        out_small[2],
        out_small[3],
        out_small[4],
        out_small[5],
        out_small[6],
        grad_out,
        out_small[7],
        grad_up,
        grad_down,
        rms_values,
    )


def solution(mesh):
    split_tokens = P("fsdp", "seq", None)
    lines = P("fsdp", None)
    return jax.shard_map(
        on_device,
        mesh=mesh,
        in_specs=(
            split_tokens, P("fsdp", "seq"), split_tokens, P("fsdp"), lines, lines, lines,
            P(None, "fsdp"), P("fsdp"), P("fsdp"), P("fsdp"), P("fsdp"), lines, P("fsdp"), lines, lines,
        ),
        out_specs=(
            split_tokens, split_tokens, P("fsdp"), lines, lines, lines, P(None, "fsdp"),
            P("fsdp"), P("fsdp"), P("fsdp"), P("fsdp"), lines, P("fsdp"), lines, lines, P(),
        ),
        check_vma=False,
    )
```

time: 3070 us -> 1810 us (0.59)
  other arithmetic: 807 us -> 135 us
  matrix products: 921 us -> 300 us
  waiting for transfers between devices: 971 us -> 741 us
  Pallas kernels: 0 us -> 147 us
  starting transfers between devices: 5.82 us -> 139 us
  local copies, waits for them, and re-layouts: 203 us -> 335 us
  blocking collectives: 127 us -> 0 us
    ppermute x0 -> x106, waiting for transfers between devices: none -> 739 us  [swapped(): lax.ppermute(block, axis, [(i, i ^ distance) for i in range(lax.axis_size...]
    another operation x83 -> x9, other arithmetic: 650 us -> 16.4 us  [the longest x1 6.54 us: on_device(): cum = jnp.cumsum(log_decay.reshape(chunks, C, H), 1)]
    dot_general x181 -> x33, matrix products: 872 us -> 300 us  [dot(): lax.dot_general(left, right, dims, precision=lax.Precision.HIGH, preferre...]
    all_gather x9 -> x0, waiting for transfers between devices: 436 us -> none  [the longest x4 176 us: entering(): gathered = jax.tree.map(lambda a: lax.all_gather(a, axis), part)]
    psum x1 -> x0, waiting for transfers between devices: 412 us -> none  [on_device(): lax.psum((share_norm, share_qkv, share_gate, share_decay_beta, share_conv...]
    pallas_call x0 -> x8, Pallas kernels: none -> 147 us  [the longest x1 49.5 us: on_device(): call(adjoint_kernel, (H,), [per_head(DK, DV), key_spec, key_spec, cols_sp...]
    ppermute x0 -> x106, starting transfers between devices: none -> 134 us  [swapped(): lax.ppermute(block, axis, [(i, i ^ distance) for i in range(lax.axis_size...]
    reduce_scatter x6 -> x0, waiting for transfers between devices: 120 us -> none  [the longest x1 120 us: on_device(): lax.psum_scatter(grad_qkv, 'fsdp', scatter_dimension=0, tiled=True)]
  transfers between devices with their start and end apart: 19 -> 108, of which waited for: 9 -> 47; matrix products, arithmetic and copies ran while one was open for 62% -> 32% of each run, Pallas kernels for 0% -> 7%
where the time goes in v1:
time: 1810 us; the launch traced here: 1800 us
  waiting for transfers between devices  741 us (41%)
  local copies, waits for them, and re-layouts  335 us (19%)
  matrix products  300 us (17%)
  Pallas kernels  147 us (8%)
  starting transfers between devices  139 us (8%)
  other arithmetic  135 us (7%)
    ppermute x106, waiting for transfers between devices, swapped(): lax.ppermute(block, axis, [(i, i ^ distance) for i in range(lax.axis_size...  739 us
    dot_general x33, matrix products, dot(): lax.dot_general(left, right, dims, precision=lax.Precision.HIGH, preferre...  300 us
    unnamed x392, local copies, waits for them, and re-layouts  153 us
    ppermute x106, starting transfers between devices, swapped(): lax.ppermute(block, axis, [(i, i ^ distance) for i in range(lax.axis_size...  134 us
    pallas_call x1, Pallas kernels, on_device(): call(adjoint_kernel, (H,), [per_head(DK, DV), key_spec, key_spec, cols_sp...  49.5 us
    dynamic_update_slice x30, local copies, waits for them, and re-layouts, backward_rows(): lax.dynamic_update_slice_in_dim(whole, blocks[:, offset:offset + size], a...  49.4 us
  transfers between devices with their start and end apart: 108, of which 47 were waited for; matrix products, arithmetic and copies ran while one was open for 32% of the time, Pallas kernels for 7%

profile of v1, /device:TPU:0, one launch (start us, length us, event | category | flops | bytes accessed | tf_op | source)
XLA Modules:
  0.0 1801.5 jit_solution(3644867766195579189)
XLA Ops:
  46.1 34.6 %collective-permute-done.24 = f32[128,2048]{1,0:T(8,128)} collective-permute-done((f32[128,2048]{1,0:T(8,128)S(1)}, f32[128,2048]{1,0:T(8,128)}, u32[]{:S(2)}, u32[]{:S(2)}) %collective-permute-start.24) | collective-permute-done | bytes 1048608 | tf_op jit(solution)/shard_map/ppermute | solution.py:30
  80.8 22.4 %collective-permute-done.29 = f32[256,1024]{1,0:T(8,128)} collective-permute-done((f32[256,1024]{1,0:T(8,128)}, f32[256,1024]{1,0:T(8,128)}, u32[]{:S(2)}, u32[]{:S(2)}) %collective-permute-start.29) | collective-permute-done | bytes 1048608 | tf_op jit(solution)/shard_map/ppermute | solution.py:30
  106.7 26.9 %collective-permute-done.39 = f32[352,1024]{1,0:T(8,128)} collective-permute-done((f32[352,1024]{1,0:T(8,128)}, f32[352,1024]{1,0:T(8,128)}, u32[]{:S(2)}, u32[]{:S(2)}) %collective-permute-start.39) | collective-permute-done | bytes 1441824 | tf_op jit(solution)/shard_map/ppermute | solution.py:30
  150.9 12.5 collective-permute-done.30
  177.7 15.4 collective-permute-done.40
  240.6 14.3 collective-permute-done.5
  323.7 16.5 fusion.143
  397.9 33.3 %pieces.1 = (f32[512,2048]{1,0:T(8,128)}, f32[512,1024]{1,0:T(8,128)S(1)}, f32[512,1024]{1,0:T(8,128)S(1)}, f32[8,8,128,128]{3,2,1,0:T(8,128)}, f32[8,128,128]{2,1,0:T(8,128)S(1)}, /*index=5*/f32[8,128,256]{2,1,0:T(8,128)S(1)}) custom-call(f32[512,1024]{1,0:T(8,128)} %get-tuple-element.195.q, f32[512,1024]{1,0:T(8,128)} %get-tuple-element.194.k, ...), custom_call_target="tpu_custom_call" | custom-call | tf_op jit(solution)/shard_map/pieces/pallas_call | solution.py:516
  515.4 31.5 %outputs.1 = (f32[512,2048]{1,0:T(8,128)}, f32[512,2048]{1,0:T(8,128)}, f32[8,8,128,256]{3,2,1,0:T(8,128)}) custom-call(f32[8,128,256]{2,1,0:T(8,128)S(1)} %gather_fusion.1, f32[512,1024]{1,0:T(8,128)S(1)} %copy-done.1, f32[512,1024]{1,0:T(8,128)S(1)} %copy-done, f32[512,2048]{1,0:T(8,128)} %get-tuple-element.48.u, f32[512,1024]{1,0:T(8,128)} %copy-done.9, ...), custom_call_target="tpu_custom_call" | custom-call | tf_op jit(solution)/shard_map/outputs/pallas_call | solution.py:532
  557.4 12.8 multiply_multiply_fusion.3
  596.3 25.8 %fusion.144 = f32[512,5632]{1,0:T(8,128)} fusion(f32[512,1024]{1,0:T(8,128)S(1)} %dynamic-slice_dynamic-update-slice_fusion.10, f32[1024,5632]{1,0:T(8,128)} %constant_dynamic-update-slice_fusion.28), kind=kOutput, calls=%fused_computation.482 | convolution fusion | flops 17716740096 | bytes 36700160 | tf_op jit(solution)/shard_map/dot_general | solution.py:102
  635.0 25.1 %fusion.20 = f32[512,1024]{1,0:T(8,128)} fusion(f32[1024,5632]{1,0:T(8,128)} %constant_dynamic-update-slice_fusion.28, f32[512,2816]{1,0:T(8,128)S(1)} %get-tuple-element.184, f32[512,2816]{1,0:T(8,128)S(1)} %get-tuple-element.183), kind=kOutput, calls=%fused_computation.57 | convolution fusion | flops 17719623680 | bytes 36700160 | tf_op jit(solution)/shard_map/dot_general | solution.py:102
  674.4 18.7 %multiply_reduce_fusion.8 = (f32[]{:T(128)}, f32[]{:T(128)}, f32[512]{0:T(512)S(1)}, f32[1024]{0:T(1024)}, f32[1,512,1024]{2,1,0:T(8,128)}) fusion(f32[512,1024]{1,0:T(8,128)} %copy-done.57, f32[512,1024]{1,0:T(8,128)} %slice_dynamic-update-slice_fusion.20, f32[1024]{0:T(1024)S(1)} %bitcast.431, f32[512]{0:T(512)S(1)} %fusion.113, ...), kind=kOutput, calls=%fused_computation.97 | convolution fusion | flops 8864135168 | bytes 23605256 | tf_op jit(solution)/shard_map/dot_general | solution.py:102
  752.4 17.3 adjoint_piece.1
  845.2 49.5 %adjoint.1 = (f32[512,1024]{1,0:T(8,128)S(1)}, f32[512,1024]{1,0:T(8,128)S(1)}, f32[512,2048]{1,0:T(8,128)}, f32[8,512,8]{2,1,0:T(8,128)}, f32[8,8,512]{2,1,0:T(8,128)S(1)}) custom-call(f32[8,128,256]{2,1,0:T(8,128)S(1)} %gather_fusion.2, f32[512,1024]{1,0:T(8,128)} %get-tuple-element.195.q, f32[512,1024]{1,0:T(8,128)} %get-tuple-element.194.k, ...), custom_call_target="tpu_custom_call" | custom-call | tf_op jit(solution)/shard_map/adjoint/pallas_call | solution.py:571
  969.5 12.0 slice_add_fusion
  990.8 18.3 %fusion.146 = f32[512,1024]{1,0:T(8,128)S(1)} fusion(f32[512,4096]{1,0:T(8,128)} %scatter-add.4, f32[1024,4096]{1,0:T(8,128)} %constant_dynamic-update-slice_fusion), kind=kOutput, calls=%fused_computation.484 | convolution fusion | flops 12884901888 | bytes 27262976 | tf_op jit(solution)/shard_map/dot_general | solution.py:102
  1020.7 12.6 fusion.18
  1100.8 34.3 %collective-permute-done.74 = f32[256,2048]{1,0:T(8,128)} collective-permute-done((f32[256,2048]{1,0:T(8,128)S(1)}, f32[256,2048]{1,0:T(8,128)}, u32[]{:S(2)}, u32[]{:S(2)}) %collective-permute-start.74) | collective-permute-done | bytes 2097184 | tf_op jit(solution)/shard_map/ppermute | solution.py:30
  1147.4 13.8 collective-permute-done.84
  1162.6 18.7 %collective-permute-done.75 = f32[128,2048]{1,0:T(8,128)S(1)} collective-permute-done((f32[128,2048]{1,0:T(8,128)S(1)}, f32[128,2048]{1,0:T(8,128)S(1)}, u32[]{:S(2)}, u32[]{:S(2)}) %collective-permute-start.75) | collective-permute-done | bytes 1048608 | tf_op jit(solution)/shard_map/ppermute | solution.py:30
  1183.1 12.9 convolution_add_fusion
  1269.6 16.3 collective-permute-done.102
  1287.3 15.2 collective-permute-start.79
  1302.4 132.3 %collective-permute-done.65 = f32[256,4096]{1,0:T(8,128)} collective-permute-done((f32[256,4096]{1,0:T(8,128)S(1)}, f32[256,4096]{1,0:T(8,128)}, u32[]{:S(2)}, u32[]{:S(2)}) %collective-permute-start.65) | collective-permute-done | bytes 4194336 | tf_op jit(solution)/shard_map/ppermute | solution.py:30
  1446.4 14.5 fusion.5
  1496.1 59.3 %collective-permute-done.93 = f32[128,5632]{1,0:T(8,128)S(1)} collective-permute-done((f32[128,5632]{1,0:T(8,128)S(1)}, f32[128,5632]{1,0:T(8,128)S(1)}, u32[]{:S(2)}, u32[]{:S(2)}) %collective-permute-start.93) | collective-permute-done | bytes 2883616 | tf_op jit(solution)/shard_map/ppermute | solution.py:30
  1559.0 47.9 %collective-permute-done.94 = f32[64,5632]{1,0:T(8,128)S(1)} collective-permute-done((f32[64,5632]{1,0:T(8,128)S(1)}, f32[64,5632]{1,0:T(8,128)S(1)}, u32[]{:S(2)}, u32[]{:S(2)}) %collective-permute-start.94) | collective-permute-done | bytes 1441824 | tf_op jit(solution)/shard_map/ppermute | solution.py:30
  1620.4 32.6 %collective-permute-done.95 = f32[32,5632]{1,0:T(8,128)S(1)} collective-permute-done((f32[32,5632]{1,0:T(8,128)S(1)}, f32[32,5632]{1,0:T(8,128)S(1)}, u32[]{:S(2)}, u32[]{:S(2)}) %collective-permute-start.95) | collective-permute-done | bytes 720928 | tf_op jit(solution)/shard_map/ppermute | solution.py:30
  1678.6 16.8 collective-permute-done.70
  1699.5 21.9 %collective-permute-done.97 = f32[64,5632]{1,0:T(8,128)S(1)} collective-permute-done((f32[64,5632]{1,0:T(8,128)S(1)}, f32[64,5632]{1,0:T(8,128)S(1)}, u32[]{:S(2)}, u32[]{:S(2)}) %collective-permute-start.97) | collective-permute-done | bytes 1441824 | tf_op jit(solution)/shard_map/ppermute | solution.py:30
  1750.1 46.3 %collective-permute-done.98 = f32[128,5632]{1,0:T(8,128)} collective-permute-done((f32[128,5632]{1,0:T(8,128)S(1)}, f32[128,5632]{1,0:T(8,128)}, u32[]{:S(2)}, u32[]{:S(2)}) %collective-permute-start.98) | collective-permute-done | bytes 2883616 | tf_op jit(solution)/shard_map/ppermute | solution.py:30
  (952 shorter events, 914.9 us)
Async XLA Ops:
  9.5 124.2 %collective-permute-start.4 = (f32[128,4096]{1,0:T(8,128)}, f32[128,4096]{1,0:T(8,128)}, u32[]{:S(2)}, u32[]{:S(2)}) collective-permute-start(f32[128,4096]{1,0:T(8,128)} %constant_dynamic-slice_fusion.25), channel_id=1, source_target_pairs={{0,2},{1,3},{2,0},{3,1},{4,6},{5,7},{6,4},{7,5},{8,10},{9,11},{10,... | collective-permute-start | bytes 6291464 | tf_op jit(solution)/shard_map/ppermute | solution.py:30
  11.2 125.7 %collective-permute-start.23 = (f32[256,2048]{1,0:T(8,128)}, f32[256,2048]{1,0:T(8,128)}, u32[]{:S(2)}, u32[]{:S(2)}) collective-permute-start(f32[256,2048]{1,0:T(8,128)} %param.23), channel_id=1, source_target_pairs={{0,1},{1,0},{2,3},{3,2},{4,5},{5,4},{6,7},{7,6},{8,9},{9,8},{10,11... | collective-permute-start | bytes 6291464 | tf_op jit(solution)/shard_map/ppermute | solution.py:30
  44.1 89.5 %collective-permute-start.39 = (f32[352,1024]{1,0:T(8,128)}, f32[352,1024]{1,0:T(8,128)}, u32[]{:S(2)}, u32[]{:S(2)}) collective-permute-start(f32[352,1024]{1,0:T(8,128)} %constant_dynamic-slice_fusion.15), channel_id=1, source_target_pairs={{0,2},{1,3},{2,0},{3,1},{4,6},{5,7},{6,4},{7,5},{8,10},{9,11},{10,... | collective-permute-start | bytes 4325384 | tf_op jit(solution)/shard_map/ppermute | solution.py:30
  80.7 68.6 %collective-permute-start.28 = (f32[512,1024]{1,0:T(8,128)}, f32[512,1024]{1,0:T(8,128)}, u32[]{:S(2)}, u32[]{:S(2)}) collective-permute-start(f32[512,1024]{1,0:T(8,128)} %param.30), channel_id=1, source_target_pairs={{0,1},{1,0},{2,3},{3,2},{4,5},{5,4},{6,7},{7,6},{8,9},{9,8},{10,11... | collective-permute-start | bytes 6291464 | tf_op jit(solution)/shard_map/ppermute | solution.py:30
  138.6 92.2 %collective-permute-start.3 = (f32[256,4096]{1,0:T(8,128)}, f32[256,4096]{1,0:T(8,128)}, u32[]{:S(2)}, u32[]{:S(2)}) collective-permute-start(f32[256,4096]{1,0:T(8,128)} %param.22), channel_id=1, source_target_pairs={{0,1},{1,0},{2,3},{3,2},{4,5},{5,4},{6,7},{7,6},{8,9},{9,8},{10,11... | collective-permute-start | bytes 12582920 | tf_op jit(solution)/shard_map/ppermute | solution.py:30
  165.5 65.3 %collective-permute-start.34 = (f32[128,5632]{1,0:T(8,128)}, f32[128,5632]{1,0:T(8,128)}, u32[]{:S(2)}, u32[]{:S(2)}) collective-permute-start(f32[128,5632]{1,0:T(8,128)} %constant_dynamic-slice_fusion.22), channel_id=1, source_target_pairs={{0,2},{1,3},{2,0},{3,1},{4,6},{5,7},{6,4},{7,5},{8,10},{9,11},{10,... | collective-permute-start | bytes 8650760 | tf_op jit(solution)/shard_map/ppermute | solution.py:30
  193.2 121.6 %collective-permute-start.33 = (f32[256,5632]{1,0:T(8,128)}, f32[256,5632]{1,0:T(8,128)}, u32[]{:S(2)}, u32[]{:S(2)}) collective-permute-start(f32[256,5632]{1,0:T(8,128)} %param.32), channel_id=1, source_target_pairs={{0,1},{1,0},{2,3},{3,2},{4,5},{5,4},{6,7},{7,6},{8,9},{9,8},{10,11... | collective-permute-start | bytes 17301512 | tf_op jit(solution)/shard_map/ppermute | solution.py:30
  230.8 116.4 %collective-permute-start.35 = (f32[128,5632]{1,0:T(8,128)}, f32[128,5632]{1,0:T(8,128)}, u32[]{:S(2)}, u32[]{:S(2)}) collective-permute-start(f32[128,5632]{1,0:T(8,128)} %collective-permute-done.34), channel_id=1, source_target_pairs={{0,4},{4,0},{8,12},{12,8},{16,20},{20,16},{24,28},{28,24},{1,5},{5... | collective-permute-start | bytes 8650760 | tf_op jit(solution)/shard_map/ppermute | solution.py:30
  255.0 221.6 %collective-permute-start.36 = (f32[128,5632]{1,0:T(8,128)}, f32[128,5632]{1,0:T(8,128)}, u32[]{:S(2)}, u32[]{:S(2)}) collective-permute-start(f32[128,5632]{1,0:T(8,128)} %collective-permute-done.34), channel_id=1, source_target_pairs={{0,1},{1,0},{2,3},{3,2},{4,5},{5,4},{6,7},{7,6},{8,9},{9,8},{10,11... | collective-permute-start | bytes 8650760 | tf_op jit(solution)/shard_map/ppermute | solution.py:30
  347.2 245.4 %collective-permute-start.37 = (f32[128,5632]{1,0:T(8,128)}, f32[128,5632]{1,0:T(8,128)}, u32[]{:S(2)}, u32[]{:S(2)}) collective-permute-start(f32[128,5632]{1,0:T(8,128)} %collective-permute-done.35), channel_id=1, source_target_pairs={{0,1},{1,0},{2,3},{3,2},{4,5},{5,4},{6,7},{7,6},{8,9},{9,8},{10,11... | collective-permute-start | bytes 8650760 | tf_op jit(solution)/shard_map/ppermute | solution.py:30
  803.3 257.6 %collective-permute-start.73 = (f32[256,2048]{1,0:T(8,128)}, f32[256,2048]{1,0:T(8,128)}, u32[]{:S(2)}, u32[]{:S(2)}) collective-permute-start(f32[256,2048]{1,0:T(8,128)} %fusion.60), channel_id=1, source_target_pairs={{0,1},{1,0},{2,3},{3,2},{4,5},{5,4},{6,7},{7,6},{8,9},{9,8},{10,11... | collective-permute-start | bytes 6291464 | tf_op jit(solution)/shard_map/ppermute | solution.py:30
  804.3 231.9 %collective-permute-start.82 = (f32[512,1024]{1,0:T(8,128)}, f32[512,1024]{1,0:T(8,128)}, u32[]{:S(2)}, u32[]{:S(2)}) collective-permute-start(f32[512,1024]{1,0:T(8,128)} %fusion.48), channel_id=1, source_target_pairs={{0,1},{1,0},{2,3},{3,2},{4,5},{5,4},{6,7},{7,6},{8,9},{9,8},{10,11... | collective-permute-start | bytes 6291464 | tf_op jit(solution)/shard_map/ppermute | solution.py:30
  805.8 260.9 %collective-permute-start.81 = (f32[512,1024]{1,0:T(8,128)}, f32[512,1024]{1,0:T(8,128)}, u32[]{:S(2)}, u32[]{:S(2)}) collective-permute-start(f32[512,1024]{1,0:T(8,128)} %fusion.53), channel_id=1, source_target_pairs={{0,1},{1,0},{2,3},{3,2},{4,5},{5,4},{6,7},{7,6},{8,9},{9,8},{10,11... | collective-permute-start | bytes 6291464 | tf_op jit(solution)/shard_map/ppermute | solution.py:30
  1033.3 149.3 %collective-permute-start.91 = (f32[256,5632]{1,0:T(8,128)}, f32[256,5632]{1,0:T(8,128)}, u32[]{:S(2)}, u32[]{:S(2)}) collective-permute-start(f32[256,5632]{1,0:T(8,128)} %fusion.18), channel_id=1, source_target_pairs={{0,1},{1,0},{2,3},{3,2},{4,5},{5,4},{6,7},{7,6},{8,9},{9,8},{10,11... | collective-permute-start | bytes 17301512 | tf_op jit(solution)/shard_map/ppermute | solution.py:30
  1066.5 73.7 %collective-permute-start.100 = (f32[704,1024]{1,0:T(8,128)S(1)}, f32[704,1024]{1,0:T(8,128)S(1)}, u32[]{:S(2)}, u32[]{:S(2)}) collective-permute-start(f32[704,1024]{1,0:T(8,128)S(1)} %copy-done.77), channel_id=1, source_target_pairs={{0,1},{1,0},{2,3},{3,2},{4,5},{5,4},{6,7},{7,6},{8,9},{9,8},{10,11... | collective-permute-start | bytes 8650760 | tf_op jit(solution)/shard_map/ppermute | solution.py:30
  1066.7 68.4 %collective-permute-start.74 = (f32[256,2048]{1,0:T(8,128)S(1)}, f32[256,2048]{1,0:T(8,128)}, u32[]{:S(2)}, u32[]{:S(2)}) collective-permute-start(f32[256,2048]{1,0:T(8,128)S(1)} %convolution_add_fusion.4), channel_id=1, source_target_pairs={{0,2},{1,3},{2,0},{3,1},{4,6},{5,7},{6,4},{7,5},{8,10},{9,11},{10,... | collective-permute-start | bytes 6291464 | tf_op jit(solution)/shard_map/ppermute | solution.py:30
  1091.5 106.5 %collective-permute-start.64 = (f32[256,4096]{1,0:T(8,128)}, f32[256,4096]{1,0:T(8,128)}, u32[]{:S(2)}, u32[]{:S(2)}) collective-permute-start(f32[256,4096]{1,0:T(8,128)} %fusion.62), channel_id=1, source_target_pairs={{0,1},{1,0},{2,3},{3,2},{4,5},{5,4},{6,7},{7,6},{8,9},{9,8},{10,11... | collective-permute-start | bytes 12582920 | tf_op jit(solution)/shard_map/ppermute | solution.py:30
  1100.1 96.2 %collective-permute-start.99 = (f32[704,1024]{1,0:T(8,128)}, f32[704,1024]{1,0:T(8,128)}, u32[]{:S(2)}, u32[]{:S(2)}) collective-permute-start(f32[704,1024]{1,0:T(8,128)} %fusion.30), channel_id=1, source_target_pairs={{0,1},{1,0},{2,3},{3,2},{4,5},{5,4},{6,7},{7,6},{8,9},{9,8},{10,11... | collective-permute-start | bytes 8650760 | tf_op jit(solution)/shard_map/ppermute | solution.py:30
  1161.2 65.7 %collective-permute-start.101 = (f32[704,1024]{1,0:T(8,128)}, f32[704,1024]{1,0:T(8,128)}, u32[]{:S(2)}, u32[]{:S(2)}) collective-permute-start(f32[704,1024]{1,0:T(8,128)} %fusion.43), channel_id=1, source_target_pairs={{0,2},{1,3},{2,0},{3,1},{4,6},{5,7},{6,4},{7,5},{8,10},{9,11},{10,... | collective-permute-start | bytes 8650760 | tf_op jit(solution)/shard_map/ppermute | solution.py:30
  1181.3 263.6 %collective-permute-start.90 = (f32[256,5632]{1,0:T(8,128)}, f32[256,5632]{1,0:T(8,128)}, u32[]{:S(2)}, u32[]{:S(2)}) collective-permute-start(f32[256,5632]{1,0:T(8,128)} %fusion.19), channel_id=1, source_target_pairs={{0,1},{1,0},{2,3},{3,2},{4,5},{5,4},{6,7},{7,6},{8,9},{9,8},{10,11... | collective-permute-start | bytes 17301512 | tf_op jit(solution)/shard_map/ppermute | solution.py:30
  1198.1 248.3 %collective-permute-start.92 = (f32[256,5632]{1,0:T(8,128)}, f32[256,5632]{1,0:T(8,128)}, u32[]{:S(2)}, u32[]{:S(2)}) collective-permute-start(f32[256,5632]{1,0:T(8,128)} %convolution_add_fusion), channel_id=1, source_target_pairs={{0,2},{1,3},{2,0},{3,1},{4,6},{5,7},{6,4},{7,5},{8,10},{9,11},{10,... | collective-permute-start | bytes 17301512 | tf_op jit(solution)/shard_map/ppermute | solution.py:30
  1211.0 76.3 %collective-permute-start.63 = (f32[256,4096]{1,0:T(8,128)S(1)}, f32[256,4096]{1,0:T(8,128)}, u32[]{:S(2)}, u32[]{:S(2)}) collective-permute-start(f32[256,4096]{1,0:T(8,128)S(1)} %copy-done.68), channel_id=1, source_target_pairs={{0,1},{1,0},{2,3},{3,2},{4,5},{5,4},{6,7},{7,6},{8,9},{9,8},{10,11... | collective-permute-start | bytes 12582920 | tf_op jit(solution)/shard_map/ppermute | solution.py:30
  1221.5 213.2 %collective-permute-start.65 = (f32[256,4096]{1,0:T(8,128)S(1)}, f32[256,4096]{1,0:T(8,128)}, u32[]{:S(2)}, u32[]{:S(2)}) collective-permute-start(f32[256,4096]{1,0:T(8,128)S(1)} %convolution_add_fusion.2), channel_id=1, source_target_pairs={{0,2},{1,3},{2,0},{3,1},{4,6},{5,7},{6,4},{7,5},{8,10},{9,11},{10,... | collective-permute-start | bytes 12582920 | tf_op jit(solution)/shard_map/ppermute | solution.py:30
  1285.9 180.6 %collective-permute-start.87 = (f32[64,1024]{1,0:T(8,128)}, f32[64,1024]{1,0:T(8,128)S(1)}, u32[]{:S(2)}, u32[]{:S(2)}) collective-permute-start(f32[64,1024]{1,0:T(8,128)} %get-tuple-element.163), channel_id=1, source_target_pairs={{0,16},{4,20},{8,24},{12,28},{16,0},{20,4},{24,8},{28,12},{1,17},{... | collective-permute-start | bytes 786440 | tf_op jit(solution)/shard_map/ppermute | solution.py:30
  1287.3 185.2 %collective-permute-start.79 = (f32[64,2048]{1,0:T(8,128)}, f32[64,2048]{1,0:T(8,128)}, u32[]{:S(2)}, u32[]{:S(2)}) collective-permute-start(f32[64,2048]{1,0:T(8,128)} %constant_dynamic-update-slice_fusion.78), channel_id=1, source_target_pairs={{0,8},{4,12},{8,0},{12,4},{16,24},{20,28},{24,16},{28,20},{1,9},{5... | collective-permute-start | bytes 1572872 | tf_op jit(solution)/shard_map/ppermute | solution.py:30
  1462.9 92.5 %collective-permute-start.93 = (f32[128,5632]{1,0:T(8,128)S(1)}, f32[128,5632]{1,0:T(8,128)S(1)}, u32[]{:S(2)}, u32[]{:S(2)}) collective-permute-start(f32[128,5632]{1,0:T(8,128)S(1)} %constant_dynamic-slice_fusion.5), channel_id=1, source_target_pairs={{0,4},{4,0},{8,12},{12,8},{16,20},{20,16},{24,28},{28,24},{1,5},{5... | collective-permute-start | bytes 8650760 | tf_op jit(solution)/shard_map/ppermute | solution.py:30
  1474.6 255.3 %collective-permute-start.80 = (f32[128,2048]{1,0:T(8,128)}, f32[128,2048]{1,0:T(8,128)}, u32[]{:S(2)}, u32[]{:S(2)}) collective-permute-start(f32[128,2048]{1,0:T(8,128)} %constant_dynamic-update-slice_fusion.76), channel_id=1, source_target_pairs={{0,4},{4,0},{8,12},{12,8},{16,20},{20,16},{24,28},{28,24},{1,5},{5... | collective-permute-start | bytes 3145736 | tf_op jit(solution)/shard_map/ppermute | solution.py:30
  1482.2 246.4 %collective-permute-start.89 = (f32[256,1024]{1,0:T(8,128)}, f32[256,1024]{1,0:T(8,128)}, u32[]{:S(2)}, u32[]{:S(2)}) collective-permute-start(f32[256,1024]{1,0:T(8,128)} %constant_dynamic-update-slice_fusion.70), channel_id=1, source_target_pairs={{0,4},{4,0},{8,12},{12,8},{16,20},{20,16},{24,28},{28,24},{1,5},{5... | collective-permute-start | bytes 3145736 | tf_op jit(solution)/shard_map/ppermute | solution.py:30
  1490.3 67.7 %collective-permute-start.105 = (f32[88,1024]{1,0:T(8,128)S(1)}, f32[88,1024]{1,0:T(8,128)S(1)}, u32[]{:S(2)}, u32[]{:S(2)}) collective-permute-start(f32[88,1024]{1,0:T(8,128)S(1)} %get-tuple-element.159), channel_id=1, source_target_pairs={{0,16},{4,20},{8,24},{12,28},{16,0},{20,4},{24,8},{28,12},{1,17},{... | collective-permute-start | bytes 1081352 | tf_op jit(solution)/shard_map/ppermute | solution.py:30
  1558.0 97.5 %collective-permute-start.106 = (f32[176,1024]{1,0:T(8,128)S(1)}, f32[176,1024]{1,0:T(8,128)S(1)}, u32[]{:S(2)}, u32[]{:S(2)}) collective-permute-start(f32[176,1024]{1,0:T(8,128)S(1)} %constant_dynamic-update-slice_fusion.60), channel_id=1, source_target_pairs={{0,8},{4,12},{8,0},{12,4},{16,24},{20,28},{24,16},{28,20},{1,9},{5... | collective-permute-start | bytes 2162696 | tf_op jit(solution)/shard_map/ppermute | solution.py:30
  1656.4 77.9 %collective-permute-start.107 = (f32[352,1024]{1,0:T(8,128)}, f32[352,1024]{1,0:T(8,128)}, u32[]{:S(2)}, u32[]{:S(2)}) collective-permute-start(f32[352,1024]{1,0:T(8,128)} %constant_dynamic-update-slice_fusion.58), channel_id=1, source_target_pairs={{0,4},{4,0},{8,12},{12,8},{16,20},{20,16},{24,28},{28,24},{1,5},{5... | collective-permute-start | bytes 4325384 | tf_op jit(solution)/shard_map/ppermute | solution.py:30
  1721.5 74.9 %collective-permute-start.98 = (f32[128,5632]{1,0:T(8,128)S(1)}, f32[128,5632]{1,0:T(8,128)}, u32[]{:S(2)}, u32[]{:S(2)}) collective-permute-start(f32[128,5632]{1,0:T(8,128)S(1)} %constant_dynamic-update-slice_fusion.64), channel_id=1, source_target_pairs={{0,4},{4,0},{8,12},{12,8},{16,20},{20,16},{24,28},{28,24},{1,5},{5... | collective-permute-start | bytes 8650760 | tf_op jit(solution)/shard_map/ppermute | solution.py:30
  (229 other events, 6495.0 us)

commit v2 on v1

v2 whole, which is shorter than its diff:
```python
from functools import partial

import jax
import jax.numpy as jnp
from jax import lax
from jax.experimental import pallas as pl
from jax.experimental.pallas import tpu as pltpu
from jax.sharding import PartitionSpec as P

D = 1024
H = 8
DK = 128
DV = 256
FF = 2816
CONV = 4
C = 64
FSDP, SEQ = "fsdp", "seq"
RIM = 16
PAIR = 2

NORM_EPS = 1e-05
UNIT_EPS = 1e-06
F32 = jnp.float32
BF16 = jnp.bfloat16
VMEM_BYTES = 56 * 1024 * 1024

NN = (((1,), (0,)), ((), ()))
NT = (((1,), (1,)), ((), ()))
TN = (((0,), (0,)), ((), ()))


def swapped(block, axis, distance):
    return lax.ppermute(block, axis, [(i, i ^ distance) for i in range(lax.axis_size(axis))])


def passed_along(block, axis, distance):
    devices = range(lax.axis_size(axis))
    route = [(i - distance, i) for i in devices if i - distance in devices]
    return lax.ppermute(block, axis, route)


def rows_of(block, start, size):
    return lax.dynamic_slice_in_dim(block, start, size, 0)


class Free:
    def gate(self, value):
        return value

    def wait(self, *done):
        pass

    def send(self, block, axis, distance):
        return swapped(block, axis, distance)


class Clock:
    def __init__(self):
        self.token = jnp.zeros((8, 128), F32)

    def wait(self, *done):
        self.token = lax.optimization_barrier((self.token,) + done)[0]

    def gate(self, value):
        return lax.optimization_barrier((value, self.token))[0]

    def send(self, block, axis, distance):
        return swapped(self.gate(block), axis, distance)

    def run(self, kernel, first, *rest):
        found = kernel(self.gate(first), *rest)
        self.wait(found[0] if isinstance(found, (list, tuple)) else found)
        return found


class Transfer:
    def __init__(self, clock, source, move):
        self.clock, self.source, self.move = clock, source, move

    def start(self):
        self.come = self.move(self.clock.gate(self.source()))

    def wait(self):
        self.clock.wait(self.come)


def swap(axis, distance):
    return lambda block: swapped(block, axis, distance)


def couples():
    return [[i, i + 1] for i in range(0, lax.axis_size(FSDP), 2)]


class Whole:
    def __init__(self, clock, shard):
        self.shard = shard
        self.near = Transfer(
            clock,
            lambda: shard,
            lambda a: lax.all_gather(a, FSDP, axis=0, tiled=True, axis_index_groups=couples()),
        )


class Piece:
    def __init__(self, clock, whole, column, width, step, bits, place):
        self.clock, self.whole, self.column, self.width = clock, whole, column, width
        self.bit, self.place = bits[min(step, len(bits) - 1)], place
        half = whole.shard.shape[0] // 2
        self.own = lax.dynamic_slice(whole.shard, (self.bit * half, column), (half, width))
        step = min(step, len(bits) - 1)
        self.far = Transfer(clock, lambda: self.own, swap(FSDP, 2))
        self.side = Transfer(clock, lambda: self.far.come, swap(SEQ, 1 << step))
        self.last_a = Transfer(clock, lambda: self.far.come, swap(FSDP, 1))
        self.last_b = Transfer(clock, lambda: self.side.come, swap(FSDP, 1))

    def weight(self):
        shard, place = self.whole.shard.shape[0], self.place
        half = shard // 2
        blocks = [self.whole.near.come] + [
            t.come for t in (self.far, self.side, self.last_a, self.last_b)
        ]
        starts = [(place & 2) * shard] + [
            (place ^ r) * shard + (self.bit ^ part) * half for r in (2, 3) for part in range(2)
        ]
        return Weight(blocks, [self.column] + [0] * 4, self.width, [1] * 5, jnp.stack(starts))

    def pack(self, tile, us):
        weight = self.weight()
        weight.blocks[0] = self.clock.gate(weight.blocks[0])
        self.packed = packed_weight(weight, tile, us)
        self.clock.wait(*self.packed)


class SmallSum:
    def __init__(self, clock, rows4, bits):
        self.clock, self.rows, self.at, self.count = clock, rows4, 0, len(bits)

    def start(self):
        block = (self.rows[1::2], self.rows[1:])[self.at] if self.at < 2 else self.rows
        axis, distance = (FSDP, 1 << self.at) if self.at < 2 else (SEQ, 1 << (self.at - 2))
        self.come = self.clock.send(block, axis, distance)

    def wait(self):
        self.clock.wait(self.come)
        kept = (self.rows[0::2], self.rows[:1])[self.at] if self.at < 2 else self.rows
        self.rows, self.at = kept + self.come, self.at + 1

    def finish(self):
        self.clock = Free()
        while self.at < 2 + self.count:
            self.start()
            self.wait()
        return self.rows[0]


def split(x):
    high = x.astype(BF16)
    return high, (x - high.astype(F32)).astype(BF16)


def one_pass(left, right, dims=NN):
    return lax.dot_general(left, right, dims, preferred_element_type=F32)


def dot_halves(lh, ll, rh, rl, dims=NN):
    return one_pass(lh, rh, dims) + (one_pass(lh, rl, dims) + one_pass(ll, rh, dims))


def stacked(ref, x):
    rows = x.shape[0]
    ref[:rows], ref[rows:] = split(x)


def dot_stacked(left, high, low, dims=NN):
    rows = left.shape[0] // 2
    top = one_pass(left[...], high, dims)
    return top[:rows] + (top[rows:] + one_pass(left[:rows], low, dims))


def dot3(left, right, dims=NN):
    return dot_halves(*split(left), *split(right), dims)


def dot3c(left, right, dims=NN):
    (one,), (two,) = dims[0]
    lh, ll = split(left)
    rh, rl = split(right)
    left = jnp.concatenate([lh, lh, ll], one)
    right = jnp.concatenate([rh, rl, rh], two)
    return lax.dot_general(left, right, dims, preferred_element_type=F32)


def dot(left, right, dims=NN):
    return lax.dot_general(
        left, right, dims, precision=lax.Precision.HIGH, preferred_element_type=F32
    )


def shape(*dims):
    return jax.ShapeDtypeStruct(dims, F32)


def cost(us):
    return pl.CostEstimate(flops=int(us), bytes_accessed=1024, transcendentals=0)


def call(kernel, grid, in_specs, out_specs, out_shape, name, us, scratch=(), prefetch=0):
    return pl.pallas_call(
        kernel,
        grid_spec=pltpu.PrefetchScalarGridSpec(
            num_scalar_prefetch=prefetch,
            grid=grid,
            in_specs=in_specs,
            out_specs=out_specs,
            scratch_shapes=scratch,
        ),
        out_shape=out_shape,
        name=name,
        compiler_params=pltpu.CompilerParams(
            vmem_limit_bytes=VMEM_BYTES, dimension_semantics=("arbitrary",) * len(grid)
        ),
        cost_estimate=cost(us),
    )


def fixed(array):
    return pl.BlockSpec(array.shape, lambda j, *_: (0,) * len(array.shape))


class Weight:
    def __init__(self, blocks, columns, width, parts, starts):
        self.blocks, self.columns, self.width = blocks, columns, width
        self.parts, self.starts = parts, starts

    def specs(self, tile):
        return [
            pl.BlockSpec((block.shape[0], tile), lambda j, *_, shift=column // tile: (0, j + shift))
            for block, column in zip(self.blocks, self.columns)
        ]


def place_weight(starts, refs, parts, high, low, columns):
    n = 0
    for ref, count in zip(refs, parts):
        size = ref.shape[0] // count
        for part in range(count):
            at = pl.ds(pl.multiple_of(starts[n], 16), size)
            high[at, columns], low[at, columns] = split(ref[part * size : (part + 1) * size])
            n += 1


def block_product(x, weight, tile, name, us):
    tokens, depth = x.shape
    width = weight.width
    count = len(weight.blocks)

    def kernel(starts, x_ref, *refs):
        blocks, refs = refs[:count], refs[count:]
        out, xs, wh, wl = refs

        @pl.when(pl.program_id(0) == 0)
        def _():
            stacked(xs, x_ref[...])

        place_weight(starts, blocks, weight.parts, wh, wl, slice(None))
        out[...] = dot_stacked(xs, wh[...], wl[...])

    tiled = pl.BlockSpec((tokens, tile), lambda j, *_: (0, j))
    return call(
        kernel,
        (width // tile,),
        [fixed(x)] + weight.specs(tile),
        tiled,
        shape(tokens, width),
        name,
        us,
        [pltpu.VMEM((2 * tokens, depth), BF16)] + [pltpu.VMEM((depth, tile), BF16)] * 2,
        prefetch=1,
    )(weight.starts, x, *weight.blocks)


def block_product_back(parts, tile, name, us, add=None):
    tokens, width = parts[0][0].shape[-2:]
    depth = 2 * parts[0][1].blocks[0].shape[0]
    count = len(parts[0][1].blocks)
    planes = parts[0][0].ndim == 3
    steps = width // tile
    n = len(parts)

    def kernel(starts, *refs):
        dys, refs = refs[: 1 if planes else n], refs[1 if planes else n :]
        blocks, refs = refs[: n * count], refs[n * count :]
        if add is not None:
            add_ref, refs = refs[0], refs[1:]
        out, wh, wl = refs
        for p in range(n):
            columns = slice(p * tile, (p + 1) * tile)
            refs_ = blocks[p * count : (p + 1) * count]
            place_weight(starts, refs_, parts[p][1].parts, wh, wl, columns)
        dy = jnp.concatenate([dys[0][p] for p in range(n)], 1) if planes else dys[0][...]
        found = dot_halves(*split(dy), wh[...], wl[...], NT)

        @pl.when(pl.program_id(0) == 0)
        def _():
            out[...] = found if add is None else found + add_ref[...]

        @pl.when(pl.program_id(0) > 0)
        def _():
            out[...] += found

    tiled = pl.BlockSpec((tokens, tile), lambda j, *_: (0, j))
    whole = pl.BlockSpec((tokens, depth), lambda j, *_: (0, 0))
    specs, arrays = [tiled], [parts[0][0]]
    if planes:
        specs = [pl.BlockSpec((n, tokens, tile), lambda j, *_: (0, 0, j))]
    for _, weight in parts:
        specs += weight.specs(tile)
        arrays += weight.blocks
    if add is not None:
        specs, arrays = specs + [whole], arrays + [add]
    return call(
        kernel, (steps,), specs, whole, shape(tokens, depth), name, us,
        [pltpu.VMEM((depth, n * tile), BF16)] * 2, prefetch=1,
    )(parts[0][1].starts, *arrays)


def packed_weight(weight, tile, us):
    depth, width = 2 * weight.blocks[0].shape[0], weight.width

    def kernel(starts, *refs):
        place_weight(starts, refs[:-2], weight.parts, *refs[-2:], slice(None))

    return call(
        kernel,
        (width // tile,),
        weight.specs(tile),
        [pl.BlockSpec((depth, tile), lambda j, *_: (0, j))] * 2,
        [jax.ShapeDtypeStruct((depth, width), BF16)] * 2,
        "packed",
        us,
        prefetch=1,
    )(weight.starts, *weight.blocks)


def product(x, weight, tile, name, us):
    tokens, depth = x.shape
    width = weight[0].shape[1]

    def kernel(x_ref, high, low, out, xs):
        @pl.when(pl.program_id(0) == 0)
        def _():
            stacked(xs, x_ref[...])

        out[...] = dot_stacked(xs, high[...], low[...])

    tiled = pl.BlockSpec((tokens, tile), lambda j: (0, j))
    weights = pl.BlockSpec((depth, tile), lambda j: (0, j))
    return call(
        kernel, (width // tile,), [fixed(x), weights, weights], tiled, shape(tokens, width),
        name, us, [pltpu.VMEM((2 * tokens, depth), BF16)],
    )(x, *weight)


def lifted_product(x, weight_a, weight_b, tile, us):
    tokens, depth = x.shape

    def kernel(x_ref, ah, al, bh, bl, a_out, b_out, hidden, xs):
        @pl.when(pl.program_id(0) == 0)
        def _():
            stacked(xs, x_ref[...])

        a = dot_stacked(xs, ah[...], al[...])
        b = dot_stacked(xs, bh[...], bl[...])
        a_out[...] = a
        b_out[...] = b
        hidden[...] = a * jax.nn.sigmoid(a) * b

    tiled = pl.BlockSpec((tokens, tile), lambda j: (0, j))
    weights = pl.BlockSpec((depth, tile), lambda j: (0, j))
    return call(
        kernel, (FF // tile,), [fixed(x)] + [weights] * 4, [tiled] * 3, [shape(tokens, FF)] * 3,
        "lifted", us, [pltpu.VMEM((2 * tokens, depth), BF16)],
    )(x, *weight_a, *weight_b)


def product_back(dy, weight, tile, name, us, add=None):
    tokens, width = dy.shape
    depth = weight[0].shape[0]

    def kernel(dy_ref, high, low, *refs):
        out, ds = refs[-2:]

        @pl.when(pl.program_id(0) == 0)
        def _():
            stacked(ds, dy_ref[...])

        found = dot_stacked(ds, high[...], low[...], NT)
        out[...] = found if add is None else found + refs[0][...]

    tiled = pl.BlockSpec((tokens, tile), lambda j: (0, j))
    weights = pl.BlockSpec((tile, width), lambda j: (j, 0))
    more = [] if add is None else [add]
    return call(
        kernel, (depth // tile,), [fixed(dy), weights, weights] + [tiled] * len(more), tiled,
        shape(tokens, depth), name, us, [pltpu.VMEM((2 * tokens, width), BF16)],
    )(dy, *weight, *more)


def hidden_back(dy, weight, a, b, tile, us):
    tokens, width = dy.shape

    def kernel(dy_ref, high, low, a_ref, b_ref, d_a, d_b, ds):
        @pl.when(pl.program_id(0) == 0)
        def _():
            stacked(ds, dy_ref[...])

        found = dot_stacked(ds, high[...], low[...], NT)
        opened = jax.nn.sigmoid(a_ref[...])
        d_a[...] = found * b_ref[...] * opened * (1.0 + a_ref[...] * (1.0 - opened))
        d_b[...] = found * a_ref[...] * opened

    tiled = pl.BlockSpec((tokens, tile), lambda j: (0, j))
    weights = pl.BlockSpec((tile, width), lambda j: (j, 0))
    return call(
        kernel, (FF // tile,), [fixed(dy), weights, weights, tiled, tiled], [tiled] * 2,
        [shape(tokens, FF)] * 2, "hidden_back", us, [pltpu.VMEM((2 * tokens, width), BF16)],
    )(dy, *weight, a, b)


def weight_grad(x, dy, halves, groups, tile, name, us, add=None):
    tokens, depth = x.shape
    half, count = depth // 8, halves.shape[0]
    planes = dy.ndim == 3
    width = dy.shape[0] * dy.shape[2] if planes else dy.shape[1]
    size = count * half // groups

    def kernel(halves, x_ref, dy_ref, *refs):
        adds, refs = (refs[:groups], refs[groups:]) if add is not None else ((), refs)
        outs, (xt, xs) = refs[:groups], refs[groups:]

        @pl.when(pl.program_id(0) == 0)
        def _():
            xt[...] = x_ref[...].T
            for n in range(count):
                high, low = split(xt[pl.ds(pl.multiple_of(halves[n], 16), half), :])
                xs[n * half : (n + 1) * half] = high
                xs[(count + n) * half : (count + n + 1) * half] = low

        found = dot_stacked(xs, *split(dy_ref[0] if planes else dy_ref[...]))
        for n in range(groups):
            block = found[n * size : (n + 1) * size]
            outs[n][...] = block + adds[n][...] if adds else block

    tiled = pl.BlockSpec((size, tile), lambda j, *_: (0, j))
    added = [pl.BlockSpec((size, tile), lambda j, *_, n=n: (n, j)) for n in range(groups)]
    of_dy = pl.BlockSpec((tokens, tile), lambda j, *_: (0, j))
    if planes:
        each = dy.shape[2] // tile
        of_dy = pl.BlockSpec((1, tokens, tile), lambda j, *_: (j // each, 0, j % each))
    more = [add] * groups if add is not None else []
    return call(
        kernel,
        (width // tile,),
        [fixed(x), of_dy] + added[: len(more)],
        [tiled] * groups,
        [shape(size, width)] * groups,
        name,
        us,
        [pltpu.VMEM((depth, tokens), F32), pltpu.VMEM((2 * count * half, tokens), BF16)],
        prefetch=1,
    )(halves, x, dy, *more)


def rms_norm(rows, gain):
    return rows * lax.rsqrt(jnp.mean(rows * rows, axis=-1, keepdims=True) + NORM_EPS) * gain


def scalars_of(decay_beta, decay_log, decay_bias, beta_bias):
    log_decay = -jnp.exp(decay_log) * jax.nn.softplus(decay_beta[:, :H] + decay_bias)
    return log_decay, jax.nn.sigmoid(decay_beta[:, H:] + beta_bias)


def total(x, axis):
    return jnp.sum(x, axis, keepdims=True)


def unit(x):
    return lax.rsqrt(total(x * x, 1) + UNIT_EPS)


def convolved(mixed, taps, same):
    tokens = mixed.shape[0] - RIM
    found = taps[0:1] * mixed[RIM:]
    for s in range(1, CONV):
        found = found + taps[s : s + 1] * (mixed[RIM - s : RIM - s + tokens] * same[:, s : s + 1])
    return found


def convolved_back(d_act, mixed, taps, same, d_mixed, d_rim, d_taps):
    tokens, width = d_act.shape
    before = convolved(mixed, taps, same)
    gate = jax.nn.sigmoid(before)
    d_before = d_act * gate * (1.0 + before * (1.0 - gate))
    empty = jnp.zeros((RIM, width), F32)
    found = jnp.concatenate([empty, taps[0:1] * d_before], 0)
    d_taps[0:1] = total(d_before * mixed[RIM:], 0)
    for s in range(1, CONV):
        reached = d_before * same[:, s : s + 1]
        padded = jnp.concatenate([empty, reached, empty], 0)
        found = found + taps[s : s + 1] * padded[s : s + RIM + tokens]
        d_taps[s : s + 1] = total(reached * mixed[RIM - s : RIM - s + tokens], 0)
    d_mixed[...] = found[RIM:]
    d_rim[...] = found[:RIM]


def silu(x):
    return x * jax.nn.sigmoid(x)


def heads_block(rows, width, shift=0):
    return pl.BlockSpec((rows, PAIR * width), lambda h, *_: (0, h + shift))


def per_heads(*dims):
    return pl.BlockSpec((PAIR,) + dims, lambda h, *_: (h,) + (0,) * len(dims))


def per_chunk_heads(chunks, *dims):
    return pl.BlockSpec((chunks, PAIR) + dims, lambda h, *_: (0, h) + (0,) * len(dims))


def positions(size=C):
    row = lax.broadcasted_iota(jnp.int32, (size, size), 0)
    column = lax.broadcasted_iota(jnp.int32, (size, size), 1)
    return row, column


CUM, BETA, LEAD, CLOSE, COUNT = 0, 1, 2, 3, 4


class Scalars:
    def __init__(self, cols, rows, p, c):
        at = pl.ds(c * C, C)
        self.at = at
        block, lines = cols[p, at, :], rows[p, :, at]
        self.cum, self.beta = block[:, CUM : CUM + 1], block[:, BETA : BETA + 1]
        self.lead, self.close = block[:, LEAD : LEAD + 1], block[:, CLOSE : CLOSE + 1]
        self.count = block[:, COUNT : COUNT + 1]
        self.last = block[C - 1 : C, LEAD : LEAD + 1]
        self.cum_row, self.beta_row = lines[CUM : CUM + 1], lines[BETA : BETA + 1]
        self.count_row = lines[COUNT : COUNT + 1]

    def ratios(self):
        row, column = positions()
        near = (self.count == self.count_row) & (row >= column)
        return jnp.where(near, jnp.exp(jnp.minimum(self.cum - self.cum_row, 0.0)), 0.0)


def of_head(p, width):
    return slice(p * width, (p + 1) * width)


def keys_kernel(mixed_q, mixed_k, taps_q, taps_k, same, cols, rows, q, k, lower, within, lower_mix):
    row, column = positions()
    for p in range(PAIR):
        of = of_head(p, DK)
        act = silu(convolved(mixed_q[:, of], taps_q[:, of], same))
        q[:, of] = act * unit(act) * DK ** (-0.5)
        act = silu(convolved(mixed_k[:, of], taps_k[:, of], same))
        k[:, of] = act * unit(act)
    for c in range(q.shape[0] // C):
        for p in range(PAIR):
            s, of = Scalars(cols, rows, p, c), of_head(p, DK)
            key = k[s.at, of]
            dots = dot3c(jnp.concatenate([key, q[s.at, of]], 0), key, NT)
            ratios = s.ratios()
            below = jnp.where(row > column, ratios, 0.0) * dots[:C]
            lower[c, p] = below
            lower_mix[c, p] = below * s.beta_row
            within[c, p] = ratios * dots[C:]


def inverse_kernel(lower, inverse):
    lanes = lower.shape[2]
    inverse[...] = jnp.zeros(inverse.shape, F32)
    for base in range(0, C, 4):
        width = (base + 4 + 7) // 8 * 8
        place = lax.broadcasted_iota(jnp.int32, (width, lanes), 0)
        found = tuple(jnp.where(place == base + n, 1.0, 0.0).astype(F32) for n in range(4))

        def earlier(j, found):
            known = inverse[j, :width, :]
            return tuple(f - lower[base + n, pl.ds(j, 1), :] * known for n, f in enumerate(found))

        if base:
            found = lax.fori_loop(0, base, earlier, found, unroll=4)
        done = []
        for n in range(4):
            one = found[n]
            for m in range(n):
                one = one - lower[base + n, base + m : base + m + 1, :] * done[m]
            done.append(one)
            inverse[base + n, :width, :] = one


def pieces_kernel(
    q, k, mixed_v, taps_v, same, cols, rows, inv, within,
    u_out, w_out, qm_out, trans_out, prefix, map_out,
):
    row, column = positions(DK)
    values = [
        silu(convolved(mixed_v[:, of_head(p, DV)], taps_v[:, of_head(p, DV)], same))
        for p in range(PAIR)
    ]
    start = jnp.concatenate([jnp.zeros((DK, DV), F32), jnp.where(row == column, 1.0, 0.0)], 1)
    carried = [start] * PAIR
    for c in range(q.shape[0] // C):
        for p in range(PAIR):
            s, of, of_v = Scalars(cols, rows, p, c), of_head(p, DK), of_head(p, DV)
            key = k[s.at, of]
            value = values[p][c * C : (c + 1) * C]
            solved = dot3c(inv[c, p], jnp.concatenate([value, s.lead * key], 1))
            w = solved[:, DV:]
            u_out[s.at, of_v] = solved[:, :DV]
            w_out[s.at, of] = w
            qm_out[s.at, of] = s.lead * q[s.at, of] - dot3c(within[c, p] * s.beta_row, w)
            both = dot3c(s.close * s.beta * key, solved, TN)
            trans = jnp.where(row == column, s.last, 0.0) - both[:, DV:]
            trans_out[c, p] = trans
            prefix[c, p] = carried[p]
            if c == 0:
                carried[p] = jnp.concatenate([both[:, :DV], trans], 1)
            else:
                new = dot3c(trans, carried[p])
                carried[p] = jnp.concatenate([new[:, :DV] + both[:, :DV], new[:, DV:]], 1)
    for p in range(PAIR):
        map_out[p] = carried[p]


def locals_kernel(u, qm, cols, rows, within, prefix, out, query_map):
    for c in range(u.shape[0] // C):
        for p in range(PAIR):
            s, of, of_v = Scalars(cols, rows, p, c), of_head(p, DK), of_head(p, DV)
            mixed = dot3c(within[c, p] * s.beta_row, u[s.at, of_v])
            if c == 0:
                out[s.at, of_v] = mixed
                query_map[s.at, of] = qm[s.at, of]
            else:
                read = dot3c(qm[s.at, of], prefix[c, p])
                out[s.at, of_v] = mixed + read[:, :DV]
                query_map[s.at, of] = read[:, DV:]


def outputs_kernel(s_in, local, query_map, gate, head_gain, out, gated):
    for p in range(PAIR):
        of, of_v = of_head(p, DK), of_head(p, DV)
        one = local[:, of_v] + dot3c(query_map[:, of], s_in[p])
        out[:, of_v] = one
        scale = lax.rsqrt(total(one * one, 1) * (1.0 / DV) + NORM_EPS)
        gated[:, of_v] = one * scale * head_gain[...] * silu(gate[:, of_v])


def adjoint_piece_kernel(qm, out, gate, head_gain, d_gated, trans, d_out, d_gate, d_gain, direct):
    for p in range(PAIR):
        of_v = of_head(p, DV)
        one, gates, grad = out[:, of_v], gate[:, of_v], d_gated[:, of_v]
        opened = jax.nn.sigmoid(gates)
        scale = lax.rsqrt(total(one * one, 1) * (1.0 / DV) + NORM_EPS)
        scaled = one * scale
        d_scaled = grad * (gates * opened)
        d_gain[p, 0:1] = total(d_scaled * scaled, 0)
        d_gate[:, of_v] = grad * scaled * head_gain[...] * (opened * (1.0 + gates * (1.0 - opened)))
        d_scaled = d_scaled * head_gain[...]
        d_out[:, of_v] = scale * (d_scaled - scaled * (total(d_scaled * scaled, 1) * (1.0 / DV)))
    carried = [None] * PAIR
    for c in reversed(range(qm.shape[0] // C)):
        for p in range(PAIR):
            at = pl.ds(c * C, C)
            here = dot3(qm[at, of_head(p, DK)], d_out[at, of_head(p, DV)], TN)
            if carried[p] is not None:
                here = here + dot3(trans[c, p], carried[p], TN)
            carried[p] = here
    for p in range(PAIR):
        direct[p] = carried[p]


def adjoint_kernel(
    z_in, s_in, q, k, u, w, cols, rows, inv, lower, within, prefix, d_out,
    dq, dk, dv, dcols, drows,
):
    z = [z_in[p] for p in range(PAIR)]
    entered = [split(s_in[p]) for p in range(PAIR)]
    row, column = positions()
    for c in reversed(range(q.shape[0] // C)):
        for p in range(PAIR):
            s, of, of_v = Scalars(cols, rows, p, c), of_head(p, DK), of_head(p, DV)
            key, query = k[s.at, of], q[s.at, of]
            if c == 0:
                state, state_ = s_in[p], entered[p]
            else:
                maps = prefix[c, p]
                state = maps[:, :DV] + dot_halves(*split(maps[:, DV:]), *entered[p])
                state_ = split(state)
            left = u[s.at, of_v] - dot_halves(*split(w[s.at, of]), *state_)
            left_, z_, grad_ = split(left), split(z[p]), split(d_out[s.at, of_v])
            ratios = s.ratios()
            d_left = dot_halves(*split(within[c, p] * s.beta_row), *grad_, TN)
            d_left = d_left + dot_halves(*split(s.close * s.beta * key), *z_)
            e = dot3(inv[c, p], d_left, TN)
            dv[s.at, of_v] = e
            both_ = [jnp.concatenate(pair, 0) for pair in zip(grad_, split(e))]
            back = dot_halves(*both_, *state_, NT)
            d_mix = dot_halves(*both_, *left_, NT)
            d_within = jnp.where(row >= column, d_mix[:C], 0.0)
            d_lower = jnp.where(row > column, -d_mix[C:], 0.0)
            d_close = dot_halves(*left_, *z_, NT)
            d_last = jnp.sum(z[p] * state)
            asks = jnp.concatenate([s.lead * query, -s.lead * key], 0)
            z[p] = s.last * z[p] + dot_halves(*split(asks), *both_, TN)
            scale = ratios * s.beta_row
            pair = jnp.concatenate([d_within * scale, d_lower * scale], 0)
            pair_, key_, query_ = split(pair), split(key), split(query)
            forth = dot_halves(*pair_, *key_)
            lines = [jnp.concatenate(one, 0) for one in zip(query_, key_)]
            dq[s.at, of] = s.lead * back[:C] + forth[:C]
            dk[s.at, of] = (
                s.close * s.beta * d_close
                - s.lead * back[C:]
                + forth[C:]
                + dot_halves(*pair_, *lines, TN)
            )
            share = d_within * within[c, p] + d_lower * lower[c, p]
            drows[p, 0:1, s.at] = total(share, 0)
            dcols[p, s.at, 0:1] = total(share * s.beta_row, 1)
            dcols[p, s.at, 1:2] = total(key * d_close, 1)
            dcols[p, s.at, 2:3] = total(back[:C] * query - back[C:] * key, 1)
            dcols[p, s.at, 3:4] = jnp.full((C, 1), d_last, F32)


def scalars_back_kernel(rows, drows, dcols, out):
    tokens = rows.shape[2]
    from_, to = positions(tokens)
    together = from_ // C == to // C
    reach, alike = (together & (from_ >= to)).astype(BF16), together.astype(BF16)
    place = lax.broadcasted_iota(jnp.int32, (1, tokens), 1)
    d_cums, ends = [], []
    for h in range(H):
        given, cols = rows[h], dcols[h].T
        beta, lead, close = (given[n : n + 1] for n in (BETA, LEAD, CLOSE))
        share = drows[h, 0:1, :]
        out[H + h : H + h + 1, :] = share + close * cols[1:2]
        closing = close * beta * cols[1:2]
        d_cums.append(cols[0:1] - beta * share + lead * cols[2:3] - closing)
        ends.append(closing + jnp.where(place % C == C - 1, lead * cols[3:4], 0.0))
    found = 0.0
    for part, mask in ((jnp.concatenate(d_cums, 0), reach), (jnp.concatenate(ends, 0), alike)):
        high, rest = split(part)
        middle, low = split(part - high.astype(F32))
        found = found + (one_pass(high, mask) + (one_pass(middle, mask) + one_pass(low, mask)))
    out[:H, :] = found


def front_back_kernel(
    mixed_q, mixed_k, mixed_v, taps_q, taps_k, taps_v, same, dq, dk, dv,
    d_mixed_qk, d_mixed_v, d_rim_q, d_rim_k, d_rim_v, d_taps_q, d_taps_k, d_taps_v,
):
    for p in range(PAIR):
        of, of_v = of_head(p, DK), of_head(p, DV)
        for mixed, taps, grad, d_mixed, d_rim, d_taps, factor in (
            (mixed_q, taps_q, dq, d_mixed_qk.at[0], d_rim_q, d_taps_q, DK ** (-0.5)),
            (mixed_k, taps_k, dk, d_mixed_qk.at[1], d_rim_k, d_taps_k, 1.0),
        ):
            act = silu(convolved(mixed[:, of], taps[:, of], same))
            scale = unit(act)
            d_unit = grad[:, of] * factor
            d_act = scale * (d_unit - act * (scale * scale * total(d_unit * act, 1)))
            convolved_back(
                d_act, mixed[:, of], taps[:, of], same,
                d_mixed.at[:, of], d_rim.at[:, of], d_taps.at[:, of],
            )
        convolved_back(
            dv[:, of_v], mixed_v[:, of_v], taps_v[:, of_v], same,
            d_mixed_v.at[:, of_v], d_rim_v.at[:, of_v], d_taps_v.at[:, of_v],
        )


def states_kernel(maps, out):
    state = jnp.zeros((DK, DV), F32)
    for piece in range(maps.shape[0]):
        out[piece] = state
        if piece < maps.shape[0] - 1:
            held = maps[piece]
            state = dot3(held[:, DV:], state) + held[:, :DV]


def adjoints_kernel(maps, direct, out):
    z = jnp.zeros((DK, DV), F32)
    for piece in reversed(range(maps.shape[0])):
        out[piece] = z
        if piece:
            z = dot3(maps[piece][:, DV:], z, TN) + direct[piece]


def whole_call(kernel, args, out_shape, name):
    return call(kernel, (1,), [fixed(a) for a in args], fixed(out_shape), out_shape, name, 4)(*args)


def heads_exchanged(parts):
    return lax.all_to_all(parts, SEQ, 0, 0)


def compose(earlier, later):
    first = jnp.einsum("hij,hjk->hik", later[0], earlier[0], precision=lax.Precision.HIGHEST)
    second = jnp.einsum("hij,hjk->hik", later[0], earlier[1], precision=lax.Precision.HIGHEST)
    return (first, second + later[1])


def entering(part, reverse):
    count, place = lax.axis_size(SEQ), lax.axis_index(SEQ)
    ahead = count - 1 - place if reverse else place
    gathered = jax.tree.map(lambda a: lax.all_gather(a, SEQ), part)
    state = (jnp.broadcast_to(jnp.eye(DK, dtype=F32), part[0].shape), jnp.zeros_like(part[1]))

    def one(step, state):
        source = count - 1 - step if reverse else step
        here = jax.tree.map(lambda a: lax.dynamic_index_in_dim(a, source, 0, False), gathered)
        return compose(state, here)

    return lax.fori_loop(0, ahead, one, state)[1]


BOTH, CROSS, HALF, DOUBLE, SPREAD, COLLECT, OTHER, SUM = range(8)


class Reduction:
    def __init__(self, clock, bits, place, first, way, both):
        self.clock, self.bits, self.at, self.place, self.way = clock, bits, 0, place, way
        self.first = min(first, len(bits) - 1)
        steps = [n for n in range(len(bits)) if n != self.first]
        beyond = [(HALF, n) for n in steps] + [(DOUBLE, n) for n in reversed(steps)]
        if way == 1 and len(bits) == 3:
            beyond = [(SPREAD, 0), (COLLECT, 0)]
        beyond = [(HALF, self.first)] + beyond + [(OTHER, self.first)]
        across = [(BOTH, 0)] if both else [(CROSS, 1), (CROSS, 0)]
        self.plan = across + ([(SUM, 0)] if way == 2 else beyond)

    def grads(self, x, dy, tile, name, us):
        place, shard = self.place, x.shape[1] // 4
        order = [(place & 2 ^ far) | core for core in range(2) for far in (0, 2)]
        bit, half = 0 if self.way == 2 else self.bits[self.first], shard // 2
        starts = jnp.stack([n * shard + (bit ^ part) * half for n in order for part in range(2)])
        (self.sent,) = self.clock.run(lambda x: weight_grad(x, dy, starts, 1, tile, name, us), x)

    def start_near(self):
        self.come = lax.psum_scatter(
            self.clock.gate(self.sent), FSDP, scatter_dimension=0, tiled=True,
            axis_index_groups=couples(),
        )

    def wait_near(self):
        self.clock.wait(self.come)
        shard = self.come.shape[0] // 2
        self.own, self.give = self.come[:shard], self.come[shard:]

    def start(self):
        kind, step = self.plan[self.at]
        half = self.own.shape[0] // 2
        if kind == BOTH:
            parts = [self.give[half:], self.give[:half]]
            self.come = [self.clock.send(part, FSDP, 2) for part in parts]
        elif kind == CROSS:
            part = self.give[half:] if step else self.give[:half]
            self.come = [self.clock.send(part, FSDP, 2)]
        elif kind == HALF:
            self.come = [self.clock.send(self.give, SEQ, 1 << step)]
        elif kind == SPREAD:
            z, size = self.bits[1] | (self.bits[2] << 1), self.own.shape[0] // 4
            self.come = [
                self.clock.send(rows_of(self.own, (z ^ d) * size, size), SEQ, 2 * d)
                for d in (1, 2, 3)
            ]
        elif kind == COLLECT:
            self.come = [self.clock.send(self.own, SEQ, 2 * d) for d in (1, 2, 3)]
        elif kind == SUM:
            own, give = self.clock.gate(self.own), self.clock.gate(self.give)
            self.come = list(lax.psum((own, give), SEQ))
        else:
            self.come = [self.clock.send(self.own, SEQ, 1 << step)]

    def wait(self):
        (kind, step), come = self.plan[self.at], self.come
        self.clock.wait(*come)
        self.at += 1
        if kind == BOTH:
            half = self.own.shape[0] // 2
            self.give, self.own = self.own[half:] + come[0], self.own[:half] + come[1]
        elif kind == CROSS and step:
            self.second = self.own[self.own.shape[0] // 2 :] + come[0]
        elif kind == CROSS:
            self.own, self.give = self.own[: self.own.shape[0] // 2] + come[0], self.second
        elif kind == HALF and self.plan[self.at][0] == HALF:
            whole, bit = self.own + come[0], self.bits[self.plan[self.at][1]]
            half = whole.shape[0] // 2
            self.own = rows_of(whole, bit * half, half)
            self.give = rows_of(whole, (1 - bit) * half, half)
        elif kind == HALF:
            self.own = self.own + come[0]
        elif kind == SPREAD:
            z, size = self.bits[1] | (self.bits[2] << 1), self.own.shape[0] // 4
            self.own = rows_of(self.own, z * size, size) + (come[0] + (come[1] + come[2]))
        elif kind == COLLECT:
            pairs = [self.joined(1, self.own, come[0]), self.joined(1, come[1], come[2])]
            self.own = self.joined(2, *pairs)
        elif kind == DOUBLE:
            self.own = self.joined(step, self.own, come[0])
        elif kind == OTHER:
            self.whole = self.joined(step, self.own, come[0])
        else:
            self.whole = jnp.concatenate(come, 0)

    def joined(self, step, own, come):
        bit = self.bits[step]
        first, second = jnp.where(bit == 0, own, come), jnp.where(bit == 0, come, own)
        return jnp.concatenate([first, second], 0)

    def finish(self):
        self.clock = Free()
        while self.at < len(self.plan):
            self.start()
            self.wait()


def reduced(*parts):
    return jnp.concatenate([r.whole for r in parts], 1)


def on_device(
    residual_in, doc_starts, out_grad, norm_gain, qkv_weight, gate_weight, decay_beta_weight,
    conv_weight, decay_log, decay_bias, beta_bias, head_gain, out_weight, mlp_gain, up_weight,
    down_weight,
):
    place, piece = lax.axis_index(FSDP), lax.axis_index(SEQ)
    pieces = lax.axis_size(SEQ)
    bits = [(piece >> s) & 1 for s in range(pieces.bit_length() - 1)]
    rows, starts, cotangent = residual_in[0], doc_starts[0], out_grad[0]
    tokens = rows.shape[0]
    chunks = tokens // C
    width_k = H * DK
    spread = pieces == H
    clock = Clock()

    counts = jnp.cumsum(starts)
    behind = jnp.flip(jnp.cumsum(jnp.flip(starts))) - starts
    tail_mask = (behind[tokens - CONV + 1 :] == 0).astype(F32)[:, None]
    by_chunk = counts.reshape(chunks, C)
    before = (counts - starts).reshape(chunks, C)[:, :1]
    of_lead = (by_chunk == before).astype(F32)
    of_close = (by_chunk == by_chunk[:, -1:]).astype(F32)
    extended = jnp.concatenate([jnp.zeros((CONV,), jnp.int32), counts])
    same = jnp.stack(
        [(counts == extended[CONV - s : CONV - s + tokens]).astype(F32) for s in range(CONV)], 1
    )
    same = jnp.pad(same, ((0, 0), (0, 8 - CONV)))

    w_qkv, w_gate, w_out, w_up, w_down = (
        Whole(clock, a) for a in (qkv_weight, gate_weight, out_weight, up_weight, down_weight)
    )
    q, k, v, gate, out, up_a, up_b, down = (
        Piece(clock, *given, bits, place)
        for given in (
            (w_qkv, 0, width_k, 0), (w_qkv, width_k, width_k, 0), (w_qkv, 2 * width_k, H * DV, 1),
            (w_gate, 0, H * DV, 0), (w_out, 0, D, 1), (w_up, 0, FF, 0), (w_up, FF, FF, 1),
            (w_down, 0, D, 0),
        )
    )
    small = [norm_gain, decay_beta_weight, conv_weight, decay_log, decay_bias, beta_bias, head_gain, mlp_gain]
    sizes = [a.size for a in small]
    packed = jnp.concatenate([a.reshape(-1) for a in small])

    steps = (H // PAIR,)
    k_spec, v_spec, mixed_k, mixed_v = (
        heads_block(r, w) for r in (tokens, tokens + RIM) for w in (DK, DV)
    )
    taps_q, taps_k = heads_block(CONV, DK), heads_block(CONV, DK, H // PAIR)
    taps_v = heads_block(CONV, DV, H // PAIR)
    cols_spec, rows_spec = per_heads(tokens, 8), per_heads(8, tokens)
    same_spec, gain_spec = fixed(same), fixed(shape(1, DV))
    square_spec, trans_spec, map_spec = (
        per_chunk_heads(chunks, *dims) for dims in ((C, C), (DK, DK), (DK, DV + DK))
    )
    state_spec = per_heads(DK, DV)
    square, state_shape = shape(chunks, H, C, C), shape(H, DK, DV)
    ks, vs = shape(tokens, H * DK), shape(tokens, H * DV)

    for whole in (w_qkv, w_gate, w_out, w_up, w_down):
        whole.near.start()
    come = [clock.send(packed, FSDP, r) for r in range(1, 4)]
    q.far.start()
    clock.wait(*come)
    rim = passed_along(clock.gate(rows[tokens - CONV + 1 :] * tail_mask), SEQ, 1)
    k.far.start()
    clock.wait(rim)

    held = jnp.stack([packed] + come)[jnp.arange(4) ^ place]
    parts, offset = [], 0
    for a, size in zip(small, sizes):
        parts.append(held[:, offset : offset + size].reshape((4,) + a.shape))
        offset += size
    full_norm, full_decay_beta = parts[0].reshape(-1), parts[1].reshape(D, 2 * H)
    taps = jnp.transpose(parts[2], (1, 0, 2)).reshape(CONV, -1)
    decay = [parts[i].reshape(-1) for i in (3, 4, 5)]
    full_head_gain, full_mlp_gain = parts[6].reshape(1, -1), parts[7].reshape(-1)
    normed, norm_pull = jax.vjp(rms_norm, rows, full_norm)
    rim_rows = jnp.pad(rim, ((RIM - CONV + 1, 0), (0, 0)))
    extended_normed = jnp.concatenate([rms_norm(rim_rows, full_norm), normed], 0)
    projected = jnp.dot(normed, full_decay_beta, precision=lax.Precision.HIGHEST)
    (log_decay, beta), scalars_pull = jax.vjp(scalars_of, projected, *decay)
    ahead = jnp.tril(jnp.ones((C, C), F32))
    cum = jnp.einsum(
        "tj,cjh->cth", ahead, log_decay.reshape(chunks, C, H), precision=lax.Precision.HIGHEST
    )
    lead = jnp.exp(cum) * of_lead[:, :, None]
    close = jnp.exp(cum[:, -1:] - cum) * of_close[:, :, None]
    count_cols = jnp.broadcast_to(counts.astype(F32)[:, None], (tokens, H))
    flat = [a.reshape(tokens, H) for a in (cum, beta, lead, close)] + [count_cols]
    rows_in = jnp.stack([a.T for a in flat], 1)
    rows_in = jnp.concatenate([rows_in, jnp.zeros((H, 3, tokens), F32)], 1)
    cols_in = jnp.transpose(rows_in, (0, 2, 1))
    clock.wait(extended_normed, rows_in, cols_in, taps, same)
    clock.wait(*[p.own for p in (q, k, v, gate, out, up_a, up_b, down)])

    def mixed_of(p, name, us):
        weight = p.weight()
        return clock.run(lambda x: block_product(x, weight, 512, name, us), extended_normed)

    q.far.wait()
    q.side.start()
    q.last_a.start()
    v.far.start()
    q.last_a.wait()
    k.far.wait()
    k.side.start()
    k.last_a.start()
    gate.far.start()
    q.side.wait()
    q.last_b.start()
    k.last_a.wait()
    q.last_b.wait()
    w_qkv.near.wait()
    rows_q = mixed_of(q, "q", 8)
    k.side.wait()
    k.last_b.start()
    k.last_b.wait()
    rows_k = mixed_of(k, "k", 8)
    v.far.wait()
    v.side.start()
    v.last_a.start()
    out.far.start()
    queries, key_rows, lower, within, mix = clock.run(
        call(
            keys_kernel, steps,
            [mixed_k, mixed_k, taps_q, taps_k, same_spec, cols_spec, rows_spec],
            [k_spec, k_spec] + [square_spec] * 3, [ks] * 2 + [square] * 3, "keys", 16,
        ),
        rows_q, rows_k, taps, taps, same, cols_in, rows_in,
    )
    v.last_a.wait()
    gate.far.wait()
    gate.side.start()
    gate.last_a.start()
    up_a.far.start()
    lanes = jnp.transpose(mix.reshape(chunks * H, C, C), (1, 2, 0))
    lanes_shape = shape(C, C, chunks * H)
    inverse = clock.run(
        call(inverse_kernel, (1,), [fixed(lanes)], fixed(lanes), lanes_shape, "inverse", 7), lanes
    )
    inverse = jnp.transpose(inverse, (2, 0, 1)).reshape(chunks, H, C, C)
    v.side.wait()
    v.last_b.start()
    gate.last_a.wait()
    v.last_b.wait()
    rows_v = mixed_of(v, "v", 13)
    gate.side.wait()
    gate.last_b.start()
    out.far.wait()
    out.side.start()
    out.last_a.start()
    solved_values, solved_keys, query_map, trans, prefix, map_ = clock.run(
        call(
            pieces_kernel, steps,
            [k_spec, k_spec, mixed_v, taps_v, same_spec, cols_spec, rows_spec, square_spec, square_spec],
            [v_spec, k_spec, k_spec, trans_spec, map_spec, per_heads(DK, DV + DK)],
            [vs, ks, ks, shape(chunks, H, DK, DK), shape(chunks, H, DK, DV + DK), shape(H, DK, DV + DK)],
            "pieces", 30,
        ),
        queries, key_rows, rows_v, taps, same, cols_in, rows_in, inverse, within,
    )
    up_a.far.wait()
    maps = heads_exchanged(clock.gate(map_)) if spread else map_
    up_a.side.start()
    up_a.last_a.start()
    up_b.far.start()
    local_outputs, read_map = clock.run(
        call(
            locals_kernel, steps,
            [v_spec, k_spec, cols_spec, rows_spec, square_spec, map_spec], [v_spec, k_spec], [vs, ks],
            "locals", 12,
        ),
        solved_values, query_map, cols_in, rows_in, within, prefix,
    )
    gate.last_b.wait()
    w_gate.near.wait()
    gate.pack(1024, 8)
    gate_rows = clock.run(lambda x: product(x, gate.packed, 512, "gate", 11), normed)
    out.last_a.wait()
    out.side.wait()
    out.last_b.start()
    if spread:
        clock.wait(maps)
        incoming = clock.run(lambda m: whole_call(states_kernel, [m], state_shape, "states"), maps)
        state_in = heads_exchanged(clock.gate(incoming))
    else:
        state_in = entering((map_[:, :, DV:], map_[:, :, :DV]), False)
    up_a.last_a.wait()
    out.last_b.wait()
    w_out.near.wait()
    out.pack(512, 8)
    up_a.side.wait()
    up_a.last_b.start()
    up_b.far.wait()
    up_b.side.start()
    up_b.last_a.start()
    down.far.start()
    up_a.last_b.wait()
    w_up.near.wait()
    up_a.pack(1408, 9)
    clock.wait(state_in)
    head_outputs, gated = clock.run(
        call(
            outputs_kernel, steps,
            [state_spec, v_spec, k_spec, v_spec, gain_spec], [v_spec] * 2, [vs] * 2, "outputs", 10,
        ),
        state_in, local_outputs, read_map, gate_rows, full_head_gain,
    )
    mixer = clock.run(lambda x: product(x, out.packed, 256, "out", 12), gated)
    middle = rows + mixer
    lifted_in, lifted_pull = jax.vjp(rms_norm, middle, full_mlp_gain)
    up_b.last_a.wait()
    down.far.wait()
    up_b.side.wait()
    up_b.last_b.start()
    down.side.start()
    down.last_a.start()
    up_b.last_b.wait()
    up_b.pack(1408, 9)
    a, b, hidden = clock.run(
        lambda x: lifted_product(x, up_a.packed, up_b.packed, 256, 25), lifted_in
    )
    down.last_a.wait()
    down.side.wait()
    down.last_b.start()

    r_down, r_a, r_b, r_out, r_gate, r_v, r_qk = (
        Reduction(clock, bits, place, first, way, both)
        for first, way, both in (
            (0, 0, 0), (1, 0, 0), (1, 0, 0), (0, 2, 0), (0, 2, 0), (0, 1, 1), (0, 1, 1),
        )
    )
    r_down.grads(hidden, cotangent, 256, "d_down", 18)
    down.last_b.wait()
    w_down.near.wait()
    r_down.start_near()
    down.pack(512, 10)
    r_down.wait_near()

    r_down.start()
    d_a, d_b = clock.run(lambda dy: hidden_back(dy, down.packed, a, b, 256, 20), cotangent)
    r_a.grads(lifted_in, d_a, 1408, "d_a", 17)
    r_down.wait()

    r_down.start()
    r_a.start_near()
    d_lifted = clock.run(lambda dy: product_back(dy, up_a.packed, 256, "back_a", 15), d_a)
    r_b.grads(lifted_in, d_b, 1408, "d_b", 17)
    r_down.wait()
    r_a.wait_near()

    r_a.start()
    r_b.start_near()
    r_down.start()
    d_lifted = clock.run(lambda dy: product_back(dy, up_b.packed, 256, "back_b", 15, d_lifted), d_b)
    d_middle, grad_mlp = lifted_pull(d_lifted)
    d_middle = d_middle + cotangent
    d_gated = clock.run(lambda dy: product_back(dy, out.packed, 256, "d_gated", 12), d_middle)
    d_heads, d_gate, d_gain, direct = clock.run(
        call(
            adjoint_piece_kernel, steps,
            [k_spec, v_spec, v_spec, gain_spec, v_spec, trans_spec],
            [v_spec, v_spec, per_heads(8, DV), state_spec],
            [vs, vs, shape(H, 8, DV), state_shape], "adjoint_piece", 14,
        ),
        query_map, head_outputs, gate_rows, full_head_gain, d_gated, trans,
    )
    r_a.wait()
    r_down.wait()
    r_b.wait_near()

    directs = heads_exchanged(clock.gate(direct)) if spread else direct
    r_a.start()
    r_down.start()
    r_out.grads(gated, d_middle, 512, "d_out", 14)
    r_gate.grads(normed, d_gate, 1024, "d_gate", 14)
    clock.wait(directs)
    r_a.wait()
    r_down.wait()
    if spread:
        outgoing = clock.run(
            lambda d: whole_call(adjoints_kernel, [maps, d], state_shape, "adjoints"), directs
        )
        adjoint_in = heads_exchanged(clock.gate(outgoing))
    else:
        adjoint_in = entering((jnp.swapaxes(map_[:, :, DV:], 1, 2), direct), True)
    r_b.start()
    r_out.start_near()
    r_gate.start_near()
    d_normed = clock.run(lambda dy: product_back(dy, gate.packed, 256, "back_gate", 12), d_gate)
    branch = clock.run(lambda x: product(x, down.packed, 256, "down", 14), hidden)
    clock.wait(adjoint_in)
    r_b.wait()
    r_out.wait_near()
    r_gate.wait_near()

    r_b.start()
    r_out.start()
    r_a.start()
    r_down.start()
    d_queries, d_keys, d_values, dcols, drows = clock.run(
        call(
            adjoint_kernel, steps,
            [state_spec, state_spec, k_spec, k_spec, v_spec, k_spec, cols_spec, rows_spec,
             square_spec, square_spec, square_spec, map_spec, v_spec],
            [k_spec, k_spec, v_spec, cols_spec, rows_spec],
            [ks, ks, vs, shape(H, tokens, 8), shape(H, 8, tokens)], "adjoint", 55,
        ),
        adjoint_in, state_in, queries, key_rows, solved_values, solved_keys, cols_in, rows_in,
        inverse, lower, within, prefix, d_heads,
    )
    for r in (r_b, r_out, r_a, r_down):
        r.wait()

    for r in (r_out, r_a, r_down):
        r.start()
    rim_k, rim_v, tap_k, tap_v = (heads_block(r, w) for r in (RIM, CONV) for w in (DK, DV))
    qk_spec = pl.BlockSpec((2, tokens, PAIR * DK), lambda h: (0, 0, h))
    d_qk, d_v, *rest = clock.run(
        call(
            front_back_kernel, steps,
            [mixed_k, mixed_k, mixed_v, taps_q, taps_k, taps_v, same_spec, k_spec, k_spec, v_spec],
            [qk_spec, v_spec, rim_k, rim_k, rim_v, tap_k, tap_k, tap_v],
            [shape(2, tokens, width_k), vs] + [shape(r, H * w) for r in (RIM, CONV) for w in (DK, DK, DV)],
            "front_back", 25,
        ),
        rows_q, rows_k, rows_v, taps, taps, taps, same, d_queries, d_keys, d_values,
    )
    d_rims, grad_conv = jnp.concatenate(rest[:3], 1)[RIM - 8 :], jnp.concatenate(rest[3:], 1)
    for r in (r_out, r_a, r_down):
        r.wait()

    returned = passed_along(clock.gate(d_rims), SEQ, -1)
    clock.wait(returned)
    returned = returned * jnp.pad(tail_mask, ((8 - CONV + 1, 0), (0, 0)))
    more = jnp.stack([returned[:, :width_k], returned[:, width_k : 2 * width_k]])
    d_qk = lax.dynamic_update_slice(d_qk, d_qk[:, tokens - 8 :] + more, (0, tokens - 8, 0))
    last = d_v[tokens - 8 :] + returned[:, 2 * width_k :]
    d_v = lax.dynamic_update_slice(d_v, last, (tokens - 8, 0))

    for r in (r_gate, r_b, r_a):
        r.start()
    r_v.grads(normed, d_v, 1024, "d_v", 13)
    r_qk.grads(normed, d_qk, 1024, "d_qk", 13)
    for r in (r_gate, r_b, r_a):
        r.wait()

    for r in (r_gate, r_b, r_down, r_a):
        r.start()
    r_v.start_near()
    r_qk.start_near()
    d_normed = clock.run(
        lambda dy: block_product_back([(dy, v.weight())], 512, "back_v", 15, d_normed), d_v
    )
    r_v.wait_near()
    for r in (r_gate, r_b, r_down, r_a):
        r.wait()

    for r in (r_v, r_b, r_a, r_down):
        r.start()
    d_normed = clock.run(
        lambda dy: block_product_back(
            [(dy, q.weight()), (dy, k.weight())], 256, "back_qk", 15, d_normed
        ),
        d_qk,
    )
    args = [rows_in, drows, dcols]
    scalars_shape = shape(2 * H, tokens)
    found = clock.run(
        call(
            scalars_back_kernel, (1,), [fixed(a) for a in args], fixed(scalars_shape), scalars_shape,
            "scalars_back", 5,
        ),
        *args,
    )
    r_qk.wait_near()
    r_out.start()
    r_gate.start()
    for r in (r_b, r_a, r_v, r_down):
        r.wait()

    for r in (r_qk, r_v, r_b, r_a):
        r.start()
    d_projected, *grad_decay = scalars_pull((clock.gate(found[:H]).T, found[H:].T))
    grad_decay_beta = dot(normed, d_projected, TN)
    d_normed = d_normed + dot(d_projected, full_decay_beta, NT)
    d_rows, grad_norm = norm_pull(d_normed)
    row_grad, result = d_rows + d_middle, middle + branch
    squares = jnp.stack([jnp.sum(x * x) for x in (rows, mixer, branch, result)])
    small_grads = [
        grad_norm, grad_decay_beta, jnp.transpose(grad_conv.reshape(CONV, 4, -1), (1, 0, 2)),
        *grad_decay, jnp.sum(d_gain[:, 0], 0), grad_mlp, jnp.broadcast_to(squares, (4, 4)),
    ]
    rows4 = jnp.concatenate([x.reshape(4, -1) for x in small_grads], 1)[jnp.arange(4) ^ place]
    small_sum = SmallSum(clock, rows4, bits)
    clock.wait(rows4)
    r_v.wait()
    r_v.start()
    for r in (r_b, r_a, r_qk, r_v):
        r.wait()

    for group in ((r_qk, r_v, small_sum), (r_qk, r_v, small_sum), (r_qk, r_b, small_sum), (r_qk, r_b, small_sum)):
        for r in group:
            r.start()
        for r in group:
            r.wait()
    small_sum.start()
    small_sum.wait()
    r_out.wait()
    r_gate.wait()
    for r in (r_down, r_a, r_b, r_out, r_gate, r_v, r_qk):
        r.finish()
    summed = small_sum.finish()

    out_small, offset = [], 0
    for x, size in zip(small, sizes):
        out_small.append(summed[offset : offset + size].reshape(x.shape))
        offset += size
    count = pieces * lax.axis_size(FSDP) * tokens * D
    grad_norm, grad_decay_beta, grad_conv, grad_log, grad_bias, grad_beta, grad_head, grad_mlp = out_small
    return (
        result[None], row_grad[None], grad_norm, reduced(r_qk, r_v), reduced(r_gate),
        grad_decay_beta, grad_conv, grad_log, grad_bias, grad_beta, grad_head, reduced(r_out),
        grad_mlp, reduced(r_a, r_b), reduced(r_down), jnp.sqrt(summed[offset:] / count),
    )


def solution(mesh):
    split_tokens = P(FSDP, SEQ, None)
    lines = P(FSDP, None)
    return jax.shard_map(
        on_device,
        mesh=mesh,
        in_specs=(
            split_tokens, P(FSDP, SEQ), split_tokens, P(FSDP), lines, lines, lines,
            P(None, FSDP), P(FSDP), P(FSDP), P(FSDP), P(FSDP), lines, P(FSDP), lines, lines,
        ),
        out_specs=(
            split_tokens, split_tokens, P(FSDP), lines, lines, lines, P(None, FSDP),
            P(FSDP), P(FSDP), P(FSDP), P(FSDP), lines, P(FSDP), lines, lines, P(),
        ),
        check_vma=False,
    )
```

time: 1810 us -> 1200 us (0.66)
  waiting for transfers between devices: 741 us -> 328 us
  Pallas kernels: 147 us -> 533 us
  matrix products: 300 us -> 7.73 us
  local copies, waits for them, and re-layouts: 335 us -> 80.9 us
  other arithmetic: 135 us -> 104 us
  starting transfers between devices: 139 us -> 119 us
    ppermute x106 -> x88, waiting for transfers between devices: 739 us -> 285 us  [swapped(): lax.ppermute(block, axis, [(i, i ^ distance) for i in range(lax.axis_size...]
    pallas_call x8 -> x37, Pallas kernels: 147 us -> 533 us  [the longest x9 172 us: run(): found = kernel(self.gate(first), *rest)]
    dot_general x33 -> x2, matrix products: 300 us -> 5.48 us  [dot(): lax.dot_general(left, right, dims, precision=lax.Precision.HIGH, preferre...]
    unnamed x392 -> x182, local copies, waits for them, and re-layouts: 153 us -> 16.3 us
    dynamic_update_slice x55 -> x0, local copies, waits for them, and re-layouts: 76 us -> none  [the longest x30 49.4 us: backward_rows(): lax.dynamic_update_slice_in_dim(whole, blocks[:, offset:offset + size], a...]
    ppermute x106 -> x88, starting transfers between devices: 134 us -> 95 us  [swapped(): lax.ppermute(block, axis, [(i, i ^ distance) for i in range(lax.axis_size...]
    mul x10 -> x4, other arithmetic: 33.7 us -> 0.92 us  [the longest x1 0.68 us: scalars_of(): jnp.exp(decay_log)]
    add_any x5 -> x0, other arithmetic: 32.5 us -> none  [the longest x1 12 us: front(): extended = jnp.concatenate([rim_rows, mixed_in], 0)]
  transfers between devices with their start and end apart: 108 -> 107, of which waited for: 47 -> 31; matrix products, arithmetic and copies ran while one was open for 32% -> 14% of each run, Pallas kernels for 7% -> 45%
where the time goes in v2:
time: 1200 us; the launch traced here: 1190 us
  Pallas kernels  533 us (44%)
  waiting for transfers between devices  328 us (27%)
  starting transfers between devices  119 us (10%)
  other arithmetic  104 us (9%)
  local copies, waits for them, and re-layouts  80.9 us (7%)
  between operations  15.8 us (1%)
    ppermute x88, waiting for transfers between devices, swapped(): lax.ppermute(block, axis, [(i, i ^ distance) for i in range(lax.axis_size...  285 us
    pallas_call x9, Pallas kernels, run(): found = kernel(self.gate(first), *rest)  172 us
    pallas_call x7, Pallas kernels, weight_grad(): call(kernel, (width // tile,), [fixed(x), of_dy] + added[:len(more)], [ti...  105 us
    ppermute x88, starting transfers between devices, swapped(): lax.ppermute(block, axis, [(i, i ^ distance) for i in range(lax.axis_size...  95 us
    pallas_call x4, Pallas kernels, product_back(): call(kernel, (depth // tile,), [fixed(dy), weights, weights] + [tiled] *...  59.9 us
    pallas_call x5, Pallas kernels, packed_weight(): call(kernel, (width // tile,), weight.specs(tile), [pl.BlockSpec((depth,...  42.3 us
    pallas_call x3, Pallas kernels, product(): call(kernel, (width // tile,), [fixed(x), weights, weights], tiled, shape...  38.7 us
    pallas_call x3, Pallas kernels, block_product(): call(kernel, (width // tile,), [fixed(x)] + weight.specs(tile), tiled, sh...  32.4 us
  transfers between devices with their start and end apart: 107, of which 31 were waited for; matrix products, arithmetic and copies ran while one was open for 14% of the time, Pallas kernels for 45%

profile of v2, /device:TPU:0, one launch (start us, length us, event | category | flops | bytes accessed | tf_op | source)
XLA Modules:
  0.0 1188.7 jit_solution(6209008658376664705)
XLA Ops:
  95.7 15.9 %keys.1 = (f32[512,1024]{1,0:T(8,128)}, f32[512,1024]{1,0:T(8,128)}, f32[8,8,64,64]{3,2,1,0:T(8,128)}, f32[8,8,64,64]{3,2,1,0:T(8,128)}, f32[8,8,64,64]{3,2,1,0:T(8,128)}) custom-call(f32[528,1024]{1,0:T(8,128)} %q.1.mixed_q, f32[528,1024]{1,0:T(8,128)} %k.1.mixed_k, f32[4,4096]{1,0:T(4,128)} %bitcast.189, f32[4,4096]{1,0:T(4,128)} %bitcast.190, ...), custom_call_target="tpu_custom_call" | custom-call | flops 16 | bytes 1024 | tf_op jit(solution)/shard_map/keys/pallas_call | solution.py:71
  137.1 13.6 %v.1.mixed_v = f32[528,2048]{1,0:T(8,128)} custom-call(s32[5]{0:T(128)} %stack.361.starts, f32[528,1024]{1,0:T(8,128)} %pad_maximum_fusion.1.x_ref, f32[512,4096]{1,0:T(8,128)} %all-gather.6.cloned.1.call-done.refs_0_.refs_1_.refs_6_, f32[128,2048]{1,0:T(8,128)} %copy-done.18, f32[128,2048]{1,0:T(8,128)} %copy-done.20, f32[128,2048]{1,0:T(8,128)} %copy-done.19, ...), custom_call_target="tpu_custom_call" | custom-call | flops 13 | bytes 1024 | tf_op jit(solution)/shard_map/v/pallas_call | solution.py:270
  154.7 17.8 %collective-permute-done.19.refs_1_ = f32[256,1024]{1,0:T(8,128)S(1)} collective-permute-done((f32[256,1024]{1,0:T(8,128)}, f32[256,1024]{1,0:T(8,128)S(1)}, u32[]{:S(2)}, u32[]{:S(2)}) %collective-permute-start.19) | collective-permute-done | bytes 1048608 | tf_op jit(solution)/shard_map/ppermute | solution.py:33
  172.5 30.6 %pieces.1 = (f32[512,2048]{1,0:T(8,128)}, f32[512,1024]{1,0:T(8,128)}, f32[512,1024]{1,0:T(8,128)}, f32[8,8,128,128]{3,2,1,0:T(8,128)}, f32[8,8,128,384]{3,2,1,0:T(8,128)}, /*index=5*/f32[8,128,384]{2,1,0:T(8,128)}) custom-call(f32[512,1024]{1,0:T(8,128)} %get-tuple-element.374.q, f32[512,1024]{1,0:T(8,128)} %get-tuple-element.375.k, f32[528,2048]{1,0:T(8,128)} %v.1.mixed_v, ...), custom_call_target="tpu_custom_call" | custom-call | flops 30 | bytes 1024 | tf_op jit(solution)/shard_map/pieces/pallas_call | solution.py:71
  213.2 13.3 %locals.1 = (f32[512,2048]{1,0:T(8,128)}, f32[512,1024]{1,0:T(8,128)}) custom-call(f32[512,2048]{1,0:T(8,128)} %get-tuple-element.383.u, f32[512,1024]{1,0:T(8,128)} %get-tuple-element.485.qm, f32[8,512,8]{2,1,0:T(8,128)} %copy.110.cols, f32[8,8,512]{2,1,0:T(8,128)} %copy-done.12, f32[8,8,64,64]{3,2,1,0:T(8,128)} %get-tuple-element.376.within, ...), custom_call_target="tpu_custom_call" | custom-call | flops 12 | bytes 1024 | tf_op jit(solution)/shard_map/locals/pallas_call | solution.py:71
  244.6 12.7 %collective-permute-done.23.refs_2_ = f32[256,1024]{1,0:T(8,128)} collective-permute-done((f32[256,1024]{1,0:T(8,128)S(1)}, f32[256,1024]{1,0:T(8,128)}, u32[]{:S(2)}, u32[]{:S(2)}) %collective-permute-start.23) | collective-permute-done | bytes 1048608 | tf_op jit(solution)/shard_map/ppermute | solution.py:33
  303.0 12.1 %out.1 = f32[512,1024]{1,0:T(8,128)} custom-call(f32[512,2048]{1,0:T(8,128)} %get-tuple-element.495.x_ref, bf16[2048,1024]{1,0:T(8,128)(2,1)} %get-tuple-element.412.high, bf16[2048,1024]{1,0:T(8,128)(2,1)} %get-tuple-element.413.low), custom_call_target="tpu_custom_call" | custom-call | flops 12 | bytes 1024 | tf_op jit(solution)/shard_map/out/pallas_call | solution.py:359
  333.8 25.5 %lifted.1 = (f32[512,2816]{1,0:T(8,128)}, f32[512,2816]{1,0:T(8,128)}, f32[512,2816]{1,0:T(8,128)}) custom-call(f32[512,1024]{1,0:T(8,128)} %multiply_multiply_fusion.x_ref, bf16[1024,2816]{1,0:T(8,128)(2,1)} %get-tuple-element.423.ah.high, bf16[1024,2816]{1,0:T(8,128)(2,1)} %get-tuple-element.424.al.low, bf16[1024,2816]{1,0:T(8,128)(2,1)} %get-tuple-element.442.bh.high, ...), custom_call_target="tpu_custom_call" | custom-call | flops 25 | bytes 1024 | tf_op jit(solution)/shard_map/lifted/pallas_call | solution.py:381
  360.2 18.0 %d_down.1 = f32[2816,1024]{1,0:T(8,128)} custom-call(s32[8]{0:T(128)} %stack.376.halves, f32[512,2816]{1,0:T(8,128)} %get-tuple-element.511.x_ref, f32[512,1024]{1,0:T(8,128)} %bitcast.182), custom_call_target="tpu_custom_call" | custom-call | flops 18 | bytes 1024 | tf_op jit(solution)/shard_map/d_down/pallas_call | solution.py:462
  402.3 20.2 %hidden_back.1 = (f32[512,2816]{1,0:T(8,128)}, f32[512,2816]{1,0:T(8,128)}) custom-call(f32[512,1024]{1,0:T(8,128)} %bitcast.183, bf16[2816,1024]{1,0:T(8,128)(2,1)} %get-tuple-element.459.high, bf16[2816,1024]{1,0:T(8,128)(2,1)} %get-tuple-element.460.low, f32[512,2816]{1,0:T(8,128)} %get-tuple-element.447.a_ref, f32[512,2816]{1,0:T(8,128)} %get-tuple-element.465.b_ref), custom_call_target="tpu_custom_call" | custom-call | flops 20 | bytes 1024 | tf_op jit(solution)/shard_map/hidden_back/pallas_call | solution.py:425
  422.5 16.7 %d_a.1 = f32[1024,2816]{1,0:T(8,128)} custom-call(s32[8]{0:T(128)} %stack.391.halves, f32[512,1024]{1,0:T(8,128)} %multiply_multiply_fusion.x_ref, f32[512,2816]{1,0:T(8,128)} %get-tuple-element.472.dy_ref), custom_call_target="tpu_custom_call" | custom-call | flops 17 | bytes 1024 | tf_op jit(solution)/shard_map/d_a/pallas_call | solution.py:462
  444.5 17.1 %back_a.1.refs_0_ = f32[512,1024]{1,0:T(8,128)} custom-call(f32[512,2816]{1,0:T(8,128)} %get-tuple-element.472.dy_ref, bf16[1024,2816]{1,0:T(8,128)(2,1)} %get-tuple-element.423.ah.high, bf16[1024,2816]{1,0:T(8,128)(2,1)} %get-tuple-element.424.al.low), custom_call_target="tpu_custom_call" | custom-call | flops 15 | bytes 1024 | tf_op jit(solution)/shard_map/back_a/pallas_call | solution.py:404
  461.6 16.9 %d_b.1 = f32[1024,2816]{1,0:T(8,128)} custom-call(s32[8]{0:T(128)} %stack.391.halves, f32[512,1024]{1,0:T(8,128)} %multiply_multiply_fusion.x_ref, f32[512,2816]{1,0:T(8,128)} %get-tuple-element.481.dy_ref), custom_call_target="tpu_custom_call" | custom-call | flops 17 | bytes 1024 | tf_op jit(solution)/shard_map/d_b/pallas_call | solution.py:462
  483.4 17.2 %back_b.1 = f32[512,1024]{1,0:T(8,128)} custom-call(f32[512,2816]{1,0:T(8,128)} %get-tuple-element.481.dy_ref, bf16[1024,2816]{1,0:T(8,128)(2,1)} %get-tuple-element.442.bh.high, bf16[1024,2816]{1,0:T(8,128)(2,1)} %get-tuple-element.443.bl.low, f32[512,1024]{1,0:T(8,128)} %back_a.1.refs_0_), custom_call_target="tpu_custom_call" | custom-call | flops 15 | bytes 1024 | tf_op jit(solution)/shard_map/back_b/pallas_call | solution.py:404
  505.3 12.5 %d_gated.1 = f32[512,2048]{1,0:T(8,128)} custom-call(f32[512,1024]{1,0:T(8,128)} %fusion.dy_ref, bf16[2048,1024]{1,0:T(8,128)(2,1)} %get-tuple-element.412.high, bf16[2048,1024]{1,0:T(8,128)(2,1)} %get-tuple-element.413.low), custom_call_target="tpu_custom_call" | custom-call | flops 12 | bytes 1024 | tf_op jit(solution)/shard_map/d_gated/pallas_call | solution.py:404
  517.9 13.5 %adjoint_piece.1 = (f32[512,2048]{1,0:T(8,128)}, f32[512,2048]{1,0:T(8,128)}, f32[8,8,256]{2,1,0:T(8,128)}, f32[8,128,256]{2,1,0:T(8,128)}) custom-call(f32[512,1024]{1,0:T(8,128)} %get-tuple-element.485.qm, f32[512,2048]{1,0:T(8,128)} %get-tuple-element.430.out, f32[512,2048]{1,0:T(8,128)} %gate.1, f32[1,256]{1,0:T(1,128)} %reshape.362.head_gain, ...), custom_call_target="tpu_custom_call" | custom-call | flops 14 | bytes 1024 | tf_op jit(solution)/shard_map/adjoint_piece/pallas_call | solution.py:71
  547.0 14.4 %d_out.1 = f32[2048,1024]{1,0:T(8,128)} custom-call(s32[8]{0:T(128)} %stack.399.halves, f32[512,2048]{1,0:T(8,128)} %get-tuple-element.495.x_ref, f32[512,1024]{1,0:T(8,128)} %fusion.dy_ref), custom_call_target="tpu_custom_call" | custom-call | flops 14 | bytes 1024 | tf_op jit(solution)/shard_map/d_out/pallas_call | solution.py:462
  561.4 12.7 %d_gate.1 = f32[1024,2048]{1,0:T(8,128)} custom-call(s32[8]{0:T(128)} %stack.407.halves, f32[512,1024]{1,0:T(8,128)} %copy-done, f32[512,2048]{1,0:T(8,128)} %get-tuple-element.509.dy_ref), custom_call_target="tpu_custom_call" | custom-call | flops 14 | bytes 1024 | tf_op jit(solution)/shard_map/d_gate/pallas_call | solution.py:462
  588.2 13.2 %back_gate.1.refs_6_ = f32[512,1024]{1,0:T(8,128)} custom-call(f32[512,2048]{1,0:T(8,128)} %get-tuple-element.509.dy_ref, bf16[1024,2048]{1,0:T(8,128)(2,1)} %get-tuple-element.393.high, bf16[1024,2048]{1,0:T(8,128)(2,1)} %get-tuple-element.394.low), custom_call_target="tpu_custom_call" | custom-call | flops 12 | bytes 1024 | tf_op jit(solution)/shard_map/back_gate/pallas_call | solution.py:404
  601.4 15.3 %down.1 = f32[512,1024]{1,0:T(8,128)} custom-call(f32[512,2816]{1,0:T(8,128)} %get-tuple-element.511.x_ref, bf16[2816,1024]{1,0:T(8,128)(2,1)} %get-tuple-element.459.high, bf16[2816,1024]{1,0:T(8,128)(2,1)} %get-tuple-element.460.low), custom_call_target="tpu_custom_call" | custom-call | flops 14 | bytes 1024 | tf_op jit(solution)/shard_map/down/pallas_call | solution.py:359
  633.1 52.7 %adjoint.1 = (f32[512,1024]{1,0:T(8,128)}, f32[512,1024]{1,0:T(8,128)}, f32[512,2048]{1,0:T(8,128)}, f32[8,512,8]{2,1,0:T(8,128)}, f32[8,8,512]{2,1,0:T(8,128)}) custom-call(f32[8,128,256]{2,1,0:T(8,128)} %all-to-all-done.3.z_in, f32[8,128,256]{2,1,0:T(8,128)} %copy-done.8, f32[512,1024]{1,0:T(8,128)} %get-tuple-element.374.q, ...), custom_call_target="tpu_custom_call" | custom-call | flops 55 | bytes 1024 | tf_op jit(solution)/shard_map/adjoint/pallas_call | solution.py:71
  691.5 26.6 %front_back.1 = (f32[2,512,1024]{2,1,0:T(8,128)}, f32[512,2048]{1,0:T(8,128)}, f32[16,1024]{1,0:T(8,128)}, f32[16,1024]{1,0:T(8,128)}, f32[16,2048]{1,0:T(8,128)...) custom-call(f32[528,1024]{1,0:T(8,128)} %q.1.mixed_q, f32[528,1024]{1,0:T(8,128)} %k.1.mixed_k, ...), custom_call_target="tpu_custom_call" | custom-call | flops 25 | bytes 1024 | tf_op jit(solution)/shard_map/front_back/pallas_call | solution.py:71
  720.1 18.4 %collective-permute-done.47 = f32[256,1024]{1,0:T(8,128)S(1)} collective-permute-done((f32[256,1024]{1,0:T(8,128)S(1)}, f32[256,1024]{1,0:T(8,128)S(1)}, u32[]{:S(2)}, u32[]{:S(2)}) %collective-permute-start.47) | collective-permute-done | bytes 1048608 | tf_op jit(solution)/shard_map/ppermute | solution.py:33
  750.4 13.2 %d_v.1 = f32[1024,2048]{1,0:T(8,128)} custom-call(s32[8]{0:T(128)} %stack.419.halves, f32[512,1024]{1,0:T(8,128)} %copy-done, f32[512,2048]{1,0:T(8,128)} %fusion.24.dy_ref.refs_0_), custom_call_target="tpu_custom_call" | custom-call | flops 13 | bytes 1024 | tf_op jit(solution)/shard_map/d_v/pallas_call | solution.py:462
  765.6 12.8 %d_qk.1 = f32[1024,2048]{1,0:T(8,128)} custom-call(s32[8]{0:T(128)} %stack.419.halves, f32[512,1024]{1,0:T(8,128)} %copy-done, f32[2,512,1024]{2,1,0:T(8,128)} %fusion.25.dy_ref.refs_0_), custom_call_target="tpu_custom_call" | custom-call | flops 13 | bytes 1024 | tf_op jit(solution)/shard_map/d_qk/pallas_call | solution.py:462
  798.2 15.0 %back_v.1.refs_11_ = f32[512,1024]{1,0:T(8,128)} custom-call(s32[5]{0:T(128)} %stack.361.starts, f32[512,2048]{1,0:T(8,128)} %fusion.24.dy_ref.refs_0_, f32[512,4096]{1,0:T(8,128)} %all-gather.6.cloned.1.call-done.refs_0_.refs_1_.refs_6_, f32[128,2048]{1,0:T(8,128)} %copy-done.18, f32[128,2048]{1,0:T(8,128)} %copy-done.20, f32[128,2048]{1,0:T(8,128)} %copy-done.19, ...), custom_call_target="tpu_custom_call" | custom-call | flops 15 | bytes 1024 | tf_op jit(solution)/shard_map/back_v/pallas_call | solution.py:322
  845.7 14.8 %back_qk.1 = f32[512,1024]{1,0:T(8,128)} custom-call(s32[5]{0:T(128)} %stack.338.starts, f32[2,512,1024]{2,1,0:T(8,128)} %fusion.25.dy_ref.refs_0_, f32[512,4096]{1,0:T(8,128)} %all-gather.6.cloned.1.call-done.refs_0_.refs_1_.refs_6_, f32[128,1024]{1,0:T(8,128)} %copy-done.31, f32[128,1024]{1,0:T(8,128)} %copy-done.34, f32[128,1024]{1,0:T(8,128)} %copy-done.32, ...), custom_call_target="tpu_custom_call" | custom-call | flops 15 | bytes 1024 | tf_op jit(solution)/shard_map/back_qk/pallas_call | solution.py:322
  873.5 20.5 %collective-permute-done.59 = f32[64,2816]{1,0:T(8,128)} collective-permute-done((f32[64,2816]{1,0:T(8,128)}, f32[64,2816]{1,0:T(8,128)}, u32[]{:S(2)}, u32[]{:S(2)}) %collective-permute-start.59) | collective-permute-done | bytes 720928 | tf_op jit(solution)/shard_map/ppermute | solution.py:33
  897.3 27.1 %collective-permute-done.62 = f32[352,1024]{1,0:T(8,128)} collective-permute-done((f32[352,1024]{1,0:T(8,128)}, f32[352,1024]{1,0:T(8,128)}, u32[]{:S(2)}, u32[]{:S(2)}) %collective-permute-start.62) | collective-permute-done | bytes 1441824 | tf_op jit(solution)/shard_map/ppermute | solution.py:33
  950.9 12.7 %collective-permute-done.64 = f32[32,2816]{1,0:T(8,128)S(1)} collective-permute-done((f32[32,2816]{1,0:T(8,128)}, f32[32,2816]{1,0:T(8,128)S(1)}, u32[]{:S(2)}, u32[]{:S(2)}) %collective-permute-start.64) | collective-permute-done | bytes 360480 | tf_op jit(solution)/shard_map/ppermute | solution.py:33
  972.2 72.4 %collective-permute-done.68 = f32[32,2048]{1,0:T(8,128)S(1)} collective-permute-done((f32[32,2048]{1,0:T(8,128)S(1)}, f32[32,2048]{1,0:T(8,128)S(1)}, u32[]{:S(2)}, u32[]{:S(2)}) %collective-permute-start.68) | collective-permute-done | bytes 262176 | tf_op jit(solution)/shard_map/ppermute | solution.py:33
  1053.0 22.1 %all-reduce.9.cloned.1.call-done = (f32[128,2048]{1,0:T(8,128)}, f32[128,2048]{1,0:T(8,128)}, f32[256,1024]{1,0:T(8,128)}, f32[256,1024]{1,0:T(8,128)}) async-done(((f32[128,2048]{1,0:T(8,128)}, f32[128,2048]{1,0:T(8,128)}, f32[256,1024]{1,0:T(8,128)}, f32[256,1024]{1,0:T(8,128)}), (f32[128,2048]{1,0:T(8,128)}, f32[128,2048]{1,0:T(8,128)}, f32[256,1024]{1,0:T(8,128)}, ...) | async-done | bytes 4194320 | tf_op jit(solution)/shard_map/psum | solution.py:887
  (620 shorter events, 535.3 us)
Async XLA Ops:
  7.2 60.2 %all-gather.6.cloned.1.call-start = ((), (), s32[]{:S(2)}) async-start(), calls=%async_computation.11 | async-start | bytes 12582912 | tf_op jit(solution)/shard_map/all_gather | solution.py:101
  8.0 218.6 %all-gather.8.cloned.1.call-start = ((), (), s32[]{:S(2)}) async-start(), calls=%async_computation.12 | async-start | bytes 6291456 | tf_op jit(solution)/shard_map/all_gather | solution.py:101
  8.7 258.9 %all-gather.10.cloned.1.call-start = ((), (), s32[]{:S(2)}) async-start(), calls=%async_computation.13 | async-start | bytes 6291456 | tf_op jit(solution)/shard_map/all_gather | solution.py:101
  9.5 269.7 %all-gather.12.cloned.1.call-start = ((), (), s32[]{:S(2)}) async-start(), calls=%async_computation.14 | async-start | bytes 17301504 | tf_op jit(solution)/shard_map/all_gather | solution.py:101
  116.8 86.3 %collective-permute-start.20 = (f32[128,2816]{1,0:T(8,128)}, f32[128,2816]{1,0:T(8,128)}, u32[]{:S(2)}, u32[]{:S(2)}) collective-permute-start(f32[128,2816]{1,0:T(8,128)} %get-tuple-element.380), channel_id=1, source_target_pairs={{0,2},{1,3},{2,0},{3,1},{4,6},{5,7},{6,4},{7,5},{8,10},{9,11},{10,... | collective-permute-start | bytes 4325384 | tf_op jit(solution)/shard_map/ppermute | solution.py:33
  203.1 54.2 %all-to-all-start = ((f32[8,128,384]{2,1,0:T(8,128)}), f32[8,128,384]{2,1,0:T(8,128)S(1)}, u32[]{:S(2)}, u32[]{:S(2)}) async-start(f32[8,128,384]{2,1,0:T(8,128)} %get-tuple-element.382), calls=%async_computation | async-start | bytes 3145728 | tf_op jit(solution)/shard_map/all_to_all | solution.py:810
  208.2 170.0 %all-gather.14.cloned.1.call-start = ((), (), s32[]{:S(2)}) async-start(), calls=%async_computation.15 | async-start | bytes 8650752 | tf_op jit(solution)/shard_map/all_gather | solution.py:101
  208.9 48.5 %collective-permute-start.23 = (f32[256,1024]{1,0:T(8,128)S(1)}, f32[256,1024]{1,0:T(8,128)}, u32[]{:S(2)}, u32[]{:S(2)}) collective-permute-start(f32[256,1024]{1,0:T(8,128)S(1)} %copy-done.42), channel_id=1, source_target_pairs={{0,8},{4,12},{8,0},{12,4},{16,24},{20,28},{24,16},{28,20},{1,9},{5... | collective-permute-start | bytes 3145736 | tf_op jit(solution)/shard_map/ppermute | solution.py:33
  210.8 56.9 %collective-permute-start.24 = (f32[128,2816]{1,0:T(8,128)}, f32[128,2816]{1,0:T(8,128)}, u32[]{:S(2)}, u32[]{:S(2)}) collective-permute-start(f32[128,2816]{1,0:T(8,128)} %collective-permute-done.20.refs_1_), channel_id=1, source_target_pairs={{0,1},{1,0},{2,3},{3,2},{4,5},{5,4},{6,7},{7,6},{8,9},{9,8},{10,11... | collective-permute-start | bytes 4325384 | tf_op jit(solution)/shard_map/ppermute | solution.py:33
  210.8 64.2 %collective-permute-start.26 = (f32[128,2816]{1,0:T(8,128)}, f32[128,2816]{1,0:T(8,128)}, u32[]{:S(2)}, u32[]{:S(2)}) collective-permute-start(f32[128,2816]{1,0:T(8,128)} %collective-permute-done.20.refs_1_), channel_id=1, source_target_pairs={{0,4},{4,0},{8,12},{12,8},{16,20},{20,16},{24,28},{28,24},{1,5},{5... | collective-permute-start | bytes 4325384 | tf_op jit(solution)/shard_map/ppermute | solution.py:33
  212.2 63.1 %collective-permute-start.27 = (f32[128,2816]{1,0:T(8,128)}, f32[128,2816]{1,0:T(8,128)}, u32[]{:S(2)}, u32[]{:S(2)}) collective-permute-start(f32[128,2816]{1,0:T(8,128)} %get-tuple-element.416), channel_id=1, source_target_pairs={{0,2},{1,3},{2,0},{3,1},{4,6},{5,7},{6,4},{7,5},{8,10},{9,11},{10,... | collective-permute-start | bytes 4325384 | tf_op jit(solution)/shard_map/ppermute | solution.py:33
  266.9 130.3 %reduce-scatter.8.cloned.1.call-start = ((), (), s32[]{:S(2)}) async-start(), calls=%async_computation.16 | async-start | bytes 17301504 | tf_op jit(solution)/shard_map/reduce_scatter | solution.py:856
  378.2 100.2 %reduce-scatter.10.cloned.1.call-start = ((), (), s32[]{:S(2)}) async-start(), calls=%async_computation.17 | async-start | bytes 17301504 | tf_op jit(solution)/shard_map/reduce_scatter | solution.py:856
  440.4 91.0 %reduce-scatter.12.cloned.1.call-start = ((), (), s32[]{:S(2)}) async-start(), calls=%async_computation.18 | async-start | bytes 17301504 | tf_op jit(solution)/shard_map/reduce_scatter | solution.py:856
  480.0 51.4 %collective-permute-start.38 = (f32[128,2816]{1,0:T(8,128)S(1)}, f32[128,2816]{1,0:T(8,128)}, u32[]{:S(2)}, u32[]{:S(2)}) collective-permute-start(f32[128,2816]{1,0:T(8,128)S(1)} %slice.386), channel_id=1, source_target_pairs={{0,2},{1,3},{2,0},{3,1},{4,6},{5,7},{6,4},{7,5},{8,10},{9,11},{10,... | collective-permute-start | bytes 4325384 | tf_op jit(solution)/shard_map/ppermute | solution.py:33
  481.9 49.5 %collective-permute-start.39 = (f32[352,1024]{1,0:T(8,128)S(1)}, f32[352,1024]{1,0:T(8,128)}, u32[]{:S(2)}, u32[]{:S(2)}) collective-permute-start(f32[352,1024]{1,0:T(8,128)S(1)} %get-tuple-element.491), channel_id=1, source_target_pairs={{0,4},{4,0},{8,12},{12,8},{16,20},{20,16},{24,28},{28,24},{1,5},{5... | collective-permute-start | bytes 4325384 | tf_op jit(solution)/shard_map/ppermute | solution.py:33
  531.4 42.7 %all-to-all-start.2 = ((f32[8,128,256]{2,1,0:T(8,128)}), f32[8,128,256]{2,1,0:T(8,128)}, u32[]{:S(2)}, u32[]{:S(2)}) async-start(f32[8,128,256]{2,1,0:T(8,128)} %get-tuple-element.501), calls=%async_computation.5 | async-start | bytes 2097152 | tf_op jit(solution)/shard_map/all_to_all | solution.py:810
  536.1 84.6 %reduce-scatter.14.cloned.1.call-start = ((), (), s32[]{:S(2)}) async-start(), calls=%async_computation.19 | async-start | bytes 12582912 | tf_op jit(solution)/shard_map/reduce_scatter | solution.py:856
  588.2 249.6 %reduce-scatter.18.cloned.1.call-start = ((), (), s32[]{:S(2)}) async-start(), calls=%async_computation.21 | async-start | bytes 12582912 | tf_op jit(solution)/shard_map/reduce_scatter | solution.py:856
  620.8 65.0 %collective-permute-start.43 = (f32[128,2816]{1,0:T(8,128)}, f32[128,2816]{1,0:T(8,128)}, u32[]{:S(2)}, u32[]{:S(2)}) collective-permute-start(f32[128,2816]{1,0:T(8,128)} %get-tuple-element.526), channel_id=1, source_target_pairs={{0,2},{1,3},{2,0},{3,1},{4,6},{5,7},{6,4},{7,5},{8,10},{9,11},{10,... | collective-permute-start | bytes 4325384 | tf_op jit(solution)/shard_map/ppermute | solution.py:33
  621.2 64.6 %collective-permute-start.45 = (f32[128,2816]{1,0:T(8,128)}, f32[128,2816]{1,0:T(8,128)}, u32[]{:S(2)}, u32[]{:S(2)}) collective-permute-start(f32[128,2816]{1,0:T(8,128)} %get-tuple-element.530), channel_id=1, source_target_pairs={{0,8},{4,12},{8,0},{12,4},{16,24},{20,28},{24,16},{28,20},{1,9},{5... | collective-permute-start | bytes 4325384 | tf_op jit(solution)/shard_map/ppermute | solution.py:33
  626.2 59.6 %collective-permute-start.44 = (f32[256,1024]{1,0:T(8,128)}, f32[256,1024]{1,0:T(8,128)}, u32[]{:S(2)}, u32[]{:S(2)}) collective-permute-start(f32[256,1024]{1,0:T(8,128)} %get-tuple-element.528), channel_id=1, source_target_pairs={{0,2},{1,3},{2,0},{3,1},{4,6},{5,7},{6,4},{7,5},{8,10},{9,11},{10,... | collective-permute-start | bytes 3145736 | tf_op jit(solution)/shard_map/ppermute | solution.py:33
  630.0 55.8 %collective-permute-start.46 = (f32[88,1024]{1,0:T(8,128)S(1)}, f32[88,1024]{1,0:T(8,128)S(1)}, u32[]{:S(2)}, u32[]{:S(2)}) collective-permute-start(f32[88,1024]{1,0:T(8,128)S(1)} %constant_dynamic-slice_fusion.10), channel_id=1, source_target_pairs={{0,16},{4,20},{8,24},{12,28},{16,0},{20,4},{24,8},{28,12},{1,17},{... | collective-permute-start | bytes 1081352 | tf_op jit(solution)/shard_map/ppermute | solution.py:33
  783.9 80.0 %reduce-scatter.20.cloned.1.call-start = ((), (), s32[]{:S(2)}) async-start(), calls=%async_computation.22 | async-start | bytes 12582912 | tf_op jit(solution)/shard_map/reduce_scatter | solution.py:856
  784.4 290.7 %all-reduce.9.cloned.1.call-start = ((), (), s32[]{:S(2)}) async-start(), calls=%async_computation.23 | async-start | bytes 8388608 | tf_op jit(solution)/shard_map/psum | solution.py:887
  864.9 59.5 %collective-permute-start.62 = (f32[352,1024]{1,0:T(8,128)}, f32[352,1024]{1,0:T(8,128)}, u32[]{:S(2)}, u32[]{:S(2)}) collective-permute-start(f32[352,1024]{1,0:T(8,128)} %pad_maximum_fusion.4), channel_id=1, source_target_pairs={{0,4},{4,0},{8,12},{12,8},{16,20},{20,16},{24,28},{28,24},{1,5},{5... | collective-permute-start | bytes 4325384 | tf_op jit(solution)/shard_map/ppermute | solution.py:33
  873.5 54.6 %collective-permute-start.61 = (f32[128,2048]{1,0:T(8,128)S(1)}, f32[128,2048]{1,0:T(8,128)S(1)}, u32[]{:S(2)}, u32[]{:S(2)}) collective-permute-start(f32[128,2048]{1,0:T(8,128)S(1)} %get-tuple-element.586), channel_id=1, source_target_pairs={{0,2},{1,3},{2,0},{3,1},{4,6},{5,7},{6,4},{7,5},{8,10},{9,11},{10,... | collective-permute-start | bytes 3145736 | tf_op jit(solution)/shard_map/ppermute | solution.py:33
  946.1 98.6 %collective-permute-start.65 = (f32[128,2816]{1,0:T(8,128)}, f32[128,2816]{1,0:T(8,128)S(1)}, u32[]{:S(2)}, u32[]{:S(2)}) collective-permute-start(f32[128,2816]{1,0:T(8,128)} %pad_maximum_fusion.5), channel_id=1, source_target_pairs={{0,8},{4,12},{8,0},{12,4},{16,24},{20,28},{24,16},{28,20},{1,9},{5... | collective-permute-start | bytes 4325384 | tf_op jit(solution)/shard_map/ppermute | solution.py:33
  966.5 78.1 %collective-permute-start.68 = (f32[32,2048]{1,0:T(8,128)S(1)}, f32[32,2048]{1,0:T(8,128)S(1)}, u32[]{:S(2)}, u32[]{:S(2)}) collective-permute-start(f32[32,2048]{1,0:T(8,128)S(1)} %get-tuple-element.605), channel_id=1, source_target_pairs={{0,8},{4,12},{8,0},{12,4},{16,24},{20,28},{24,16},{28,20},{1,9},{5... | collective-permute-start | bytes 786440 | tf_op jit(solution)/shard_map/ppermute | solution.py:33
  968.6 76.0 %collective-permute-start.69 = (f32[32,2048]{1,0:T(8,128)S(1)}, f32[32,2048]{1,0:T(8,128)S(1)}, u32[]{:S(2)}, u32[]{:S(2)}) collective-permute-start(f32[32,2048]{1,0:T(8,128)S(1)} %get-tuple-element.606), channel_id=1, source_target_pairs={{0,16},{4,20},{8,24},{12,28},{16,0},{20,4},{24,8},{28,12},{1,17},{... | collective-permute-start | bytes 786440 | tf_op jit(solution)/shard_map/ppermute | solution.py:33
  969.0 75.6 %collective-permute-start.70 = (f32[32,2048]{1,0:T(8,128)S(1)}, f32[32,2048]{1,0:T(8,128)S(1)}, u32[]{:S(2)}, u32[]{:S(2)}) collective-permute-start(f32[32,2048]{1,0:T(8,128)S(1)} %get-tuple-element.607), channel_id=1, source_target_pairs={{0,24},{4,28},{8,16},{12,20},{16,8},{20,12},{24,0},{28,4},{1,25},{... | collective-permute-start | bytes 786440 | tf_op jit(solution)/shard_map/ppermute | solution.py:33
  971.3 75.3 %collective-permute-start.67 = (f32[128,2048]{1,0:T(8,128)S(1)}, f32[128,2048]{1,0:T(8,128)S(1)}, u32[]{:S(2)}, u32[]{:S(2)}) collective-permute-start(f32[128,2048]{1,0:T(8,128)S(1)} %get-tuple-element.603), channel_id=1, source_target_pairs={{0,2},{1,3},{2,0},{3,1},{4,6},{5,7},{6,4},{7,5},{8,10},{9,11},{10,... | collective-permute-start | bytes 3145736 | tf_op jit(solution)/shard_map/ppermute | solution.py:33
  (163 other events, 2579.3 us)
Sparse Core Ops, SparseCore 0:
  9.6 22.5 all-gather.5
  33.7 14.8 all-gather.7
  50.1 16.2 all-gather.9
  67.9 27.3 all-gather.11
  213.4 16.6 all-gather.13
  378.4 18.8 reduce-scatter.7
  439.4 20.2 reduce-scatter.9
  478.6 21.4 reduce-scatter.11
  578.5 17.1 reduce-scatter.13
  598.0 18.0 reduce-scatter.15
  784.0 14.3 reduce-scatter.17
  800.6 18.0 reduce-scatter.19
  866.0 209.0 all-reduce.8

commit v3 on v2

--- a/solution.py
+++ b/solution.py
@@ -1083,9 +1083,6 @@
     rows_v = mixed_of(v, "v", 13)
     gate.side.wait()
     gate.last_b.start()
-    out.far.wait()
-    out.side.start()
-    out.last_a.start()
     solved_values, solved_keys, query_map, trans, prefix, map_ = clock.run(
         call(
             pieces_kernel, steps,
@@ -1096,8 +1093,11 @@
         ),
         queries, key_rows, rows_v, taps, same, cols_in, rows_in, inverse, within,
     )
+    out.far.wait()
     up_a.far.wait()
     maps = heads_exchanged(clock.gate(map_)) if spread else map_
+    out.side.start()
+    out.last_a.start()
     up_a.side.start()
     up_a.last_a.start()
     up_b.far.start()
@@ -1293,7 +1293,7 @@
     for r in (r_gate, r_b, r_down, r_a):
         r.wait()
 
-    for r in (r_v, r_b, r_a, r_down):
+    for r in (r_v, r_b, r_a, r_down, r_out, r_gate):
         r.start()
     d_normed = clock.run(
         lambda dy: block_product_back(
@@ -1311,8 +1311,6 @@
         *args,
     )
     r_qk.wait_near()
-    r_out.start()
-    r_gate.start()
     for r in (r_b, r_a, r_v, r_down):
         r.wait()
 

time: 1200 us -> 1180 us (0.983)
  waiting for transfers between devices: 328 us -> 316 us
    ppermute x88, waiting for transfers between devices: 285 us -> 266 us  [swapped(): lax.ppermute(block, axis, [(i, i ^ distance) for i in range(lax.axis_size...]
  transfers between devices with their start and end apart: 107 -> 107, of which waited for: 31 -> 30; matrix products, arithmetic and copies ran while one was open for 14% -> 14% of each run, Pallas kernels for 45% -> 45%
where the time goes in v3:
time: 1180 us; the launch traced here: 1170 us
  Pallas kernels  533 us (45%)
  waiting for transfers between devices  316 us (27%)
  starting transfers between devices  115 us (10%)
  other arithmetic  103 us (9%)
  local copies, waits for them, and re-layouts  81.9 us (7%)
  between operations  15.8 us (1%)
    ppermute x88, waiting for transfers between devices, swapped(): lax.ppermute(block, axis, [(i, i ^ distance) for i in range(lax.axis_size...  266 us
    pallas_call x9, Pallas kernels, run(): found = kernel(self.gate(first), *rest)  172 us
    pallas_call x7, Pallas kernels, weight_grad(): call(kernel, (width // tile,), [fixed(x), of_dy] + added[:len(more)], [ti...  105 us
    ppermute x88, starting transfers between devices, swapped(): lax.ppermute(block, axis, [(i, i ^ distance) for i in range(lax.axis_size...  91.2 us
    pallas_call x4, Pallas kernels, product_back(): call(kernel, (depth // tile,), [fixed(dy), weights, weights] + [tiled] *...  59.9 us
    pallas_call x5, Pallas kernels, packed_weight(): call(kernel, (width // tile,), weight.specs(tile), [pl.BlockSpec((depth,...  41.9 us
    pallas_call x3, Pallas kernels, product(): call(kernel, (width // tile,), [fixed(x), weights, weights], tiled, shape...  38.7 us
    pallas_call x3, Pallas kernels, block_product(): call(kernel, (width // tile,), [fixed(x)] + weight.specs(tile), tiled, sh...  32.4 us
  transfers between devices with their start and end apart: 107, of which 30 were waited for; matrix products, arithmetic and copies ran while one was open for 14% of the time, Pallas kernels for 45%

profile of v3, /device:TPU:0, one launch (start us, length us, event | category | flops | bytes accessed | tf_op | source)
XLA Modules:
  0.0 1172.7 jit_solution(18031992908927645090)
XLA Ops:
  51.3 11.7 collective-permute-done.6.refs_1_.refs_7_
  95.7 15.9 %keys.1 = (f32[512,1024]{1,0:T(8,128)}, f32[512,1024]{1,0:T(8,128)}, f32[8,8,64,64]{3,2,1,0:T(8,128)}, f32[8,8,64,64]{3,2,1,0:T(8,128)}, f32[8,8,64,64]{3,2,1,0:T(8,128)}) custom-call(f32[528,1024]{1,0:T(8,128)} %q.1.mixed_q, f32[528,1024]{1,0:T(8,128)} %k.1.mixed_k, f32[4,4096]{1,0:T(4,128)} %bitcast.189, f32[4,4096]{1,0:T(4,128)} %bitcast.190, ...), custom_call_target="tpu_custom_call" | custom-call | flops 16 | bytes 1024 | tf_op jit(solution)/shard_map/keys/pallas_call | solution.py:71
  137.1 13.6 %v.1.mixed_v = f32[528,2048]{1,0:T(8,128)} custom-call(s32[5]{0:T(128)} %stack.361.starts, f32[528,1024]{1,0:T(8,128)} %pad_maximum_fusion.1.x_ref, f32[512,4096]{1,0:T(8,128)} %all-gather.6.cloned.1.call-done.refs_0_.refs_1_.refs_6_, f32[128,2048]{1,0:T(8,128)} %copy-done.18, f32[128,2048]{1,0:T(8,128)} %copy-done.20, f32[128,2048]{1,0:T(8,128)} %copy-done.19, ...), custom_call_target="tpu_custom_call" | custom-call | flops 13 | bytes 1024 | tf_op jit(solution)/shard_map/v/pallas_call | solution.py:270
  154.7 30.5 %pieces.1 = (f32[512,2048]{1,0:T(8,128)}, f32[512,1024]{1,0:T(8,128)}, f32[512,1024]{1,0:T(8,128)}, f32[8,8,128,128]{3,2,1,0:T(8,128)}, f32[8,8,128,384]{3,2,1,0:T(8,128)}, /*index=5*/f32[8,128,384]{2,1,0:T(8,128)}) custom-call(f32[512,1024]{1,0:T(8,128)} %get-tuple-element.372.q, f32[512,1024]{1,0:T(8,128)} %get-tuple-element.373.k, f32[528,2048]{1,0:T(8,128)} %v.1.mixed_v, ...), custom_call_target="tpu_custom_call" | custom-call | flops 30 | bytes 1024 | tf_op jit(solution)/shard_map/pieces/pallas_call | solution.py:71
  196.0 13.3 %locals.1 = (f32[512,2048]{1,0:T(8,128)}, f32[512,1024]{1,0:T(8,128)}) custom-call(f32[512,2048]{1,0:T(8,128)} %get-tuple-element.383.u, f32[512,1024]{1,0:T(8,128)} %get-tuple-element.485.qm, f32[8,512,8]{2,1,0:T(8,128)} %copy.110.cols, f32[8,8,512]{2,1,0:T(8,128)} %copy-done.12, f32[8,8,64,64]{3,2,1,0:T(8,128)} %get-tuple-element.374.within, ...), custom_call_target="tpu_custom_call" | custom-call | flops 12 | bytes 1024 | tf_op jit(solution)/shard_map/locals/pallas_call | solution.py:71
  227.4 13.1 %collective-permute-done.23.refs_2_ = f32[256,1024]{1,0:T(8,128)} collective-permute-done((f32[256,1024]{1,0:T(8,128)}, f32[256,1024]{1,0:T(8,128)}, u32[]{:S(2)}, u32[]{:S(2)}) %collective-permute-start.23) | collective-permute-done | bytes 1048608 | tf_op jit(solution)/shard_map/ppermute | solution.py:33
  286.1 12.1 %out.1 = f32[512,1024]{1,0:T(8,128)} custom-call(f32[512,2048]{1,0:T(8,128)} %get-tuple-element.495.x_ref, bf16[2048,1024]{1,0:T(8,128)(2,1)} %get-tuple-element.412.high, bf16[2048,1024]{1,0:T(8,128)(2,1)} %get-tuple-element.413.low), custom_call_target="tpu_custom_call" | custom-call | flops 12 | bytes 1024 | tf_op jit(solution)/shard_map/out/pallas_call | solution.py:359
  316.9 25.5 %lifted.1 = (f32[512,2816]{1,0:T(8,128)}, f32[512,2816]{1,0:T(8,128)}, f32[512,2816]{1,0:T(8,128)}) custom-call(f32[512,1024]{1,0:T(8,128)} %multiply_multiply_fusion.x_ref, bf16[1024,2816]{1,0:T(8,128)(2,1)} %get-tuple-element.423.ah.high, bf16[1024,2816]{1,0:T(8,128)(2,1)} %get-tuple-element.424.al.low, bf16[1024,2816]{1,0:T(8,128)(2,1)} %get-tuple-element.442.bh.high, ...), custom_call_target="tpu_custom_call" | custom-call | flops 25 | bytes 1024 | tf_op jit(solution)/shard_map/lifted/pallas_call | solution.py:381
  343.3 18.0 %d_down.1 = f32[2816,1024]{1,0:T(8,128)} custom-call(s32[8]{0:T(128)} %stack.376.halves, f32[512,2816]{1,0:T(8,128)} %get-tuple-element.511.x_ref, f32[512,1024]{1,0:T(8,128)} %bitcast.182), custom_call_target="tpu_custom_call" | custom-call | flops 18 | bytes 1024 | tf_op jit(solution)/shard_map/d_down/pallas_call | solution.py:462
  385.6 20.2 %hidden_back.1 = (f32[512,2816]{1,0:T(8,128)}, f32[512,2816]{1,0:T(8,128)}) custom-call(f32[512,1024]{1,0:T(8,128)} %bitcast.183, bf16[2816,1024]{1,0:T(8,128)(2,1)} %get-tuple-element.459.high, bf16[2816,1024]{1,0:T(8,128)(2,1)} %get-tuple-element.460.low, f32[512,2816]{1,0:T(8,128)} %get-tuple-element.447.a_ref, f32[512,2816]{1,0:T(8,128)} %get-tuple-element.465.b_ref), custom_call_target="tpu_custom_call" | custom-call | flops 20 | bytes 1024 | tf_op jit(solution)/shard_map/hidden_back/pallas_call | solution.py:425
  405.7 16.7 %d_a.1 = f32[1024,2816]{1,0:T(8,128)} custom-call(s32[8]{0:T(128)} %stack.391.halves, f32[512,1024]{1,0:T(8,128)} %multiply_multiply_fusion.x_ref, f32[512,2816]{1,0:T(8,128)} %get-tuple-element.472.dy_ref), custom_call_target="tpu_custom_call" | custom-call | flops 17 | bytes 1024 | tf_op jit(solution)/shard_map/d_a/pallas_call | solution.py:462
  427.7 17.1 %back_a.1.refs_0_ = f32[512,1024]{1,0:T(8,128)} custom-call(f32[512,2816]{1,0:T(8,128)} %get-tuple-element.472.dy_ref, bf16[1024,2816]{1,0:T(8,128)(2,1)} %get-tuple-element.423.ah.high, bf16[1024,2816]{1,0:T(8,128)(2,1)} %get-tuple-element.424.al.low), custom_call_target="tpu_custom_call" | custom-call | flops 15 | bytes 1024 | tf_op jit(solution)/shard_map/back_a/pallas_call | solution.py:404
  444.8 16.9 %d_b.1 = f32[1024,2816]{1,0:T(8,128)} custom-call(s32[8]{0:T(128)} %stack.391.halves, f32[512,1024]{1,0:T(8,128)} %multiply_multiply_fusion.x_ref, f32[512,2816]{1,0:T(8,128)} %get-tuple-element.481.dy_ref), custom_call_target="tpu_custom_call" | custom-call | flops 17 | bytes 1024 | tf_op jit(solution)/shard_map/d_b/pallas_call | solution.py:462
  466.6 17.2 %back_b.1 = f32[512,1024]{1,0:T(8,128)} custom-call(f32[512,2816]{1,0:T(8,128)} %get-tuple-element.481.dy_ref, bf16[1024,2816]{1,0:T(8,128)(2,1)} %get-tuple-element.442.bh.high, bf16[1024,2816]{1,0:T(8,128)(2,1)} %get-tuple-element.443.bl.low, f32[512,1024]{1,0:T(8,128)} %back_a.1.refs_0_), custom_call_target="tpu_custom_call" | custom-call | flops 15 | bytes 1024 | tf_op jit(solution)/shard_map/back_b/pallas_call | solution.py:404
  488.6 12.5 %d_gated.1 = f32[512,2048]{1,0:T(8,128)} custom-call(f32[512,1024]{1,0:T(8,128)} %fusion.dy_ref, bf16[2048,1024]{1,0:T(8,128)(2,1)} %get-tuple-element.412.high, bf16[2048,1024]{1,0:T(8,128)(2,1)} %get-tuple-element.413.low), custom_call_target="tpu_custom_call" | custom-call | flops 12 | bytes 1024 | tf_op jit(solution)/shard_map/d_gated/pallas_call | solution.py:404
  501.1 13.5 %adjoint_piece.1 = (f32[512,2048]{1,0:T(8,128)}, f32[512,2048]{1,0:T(8,128)}, f32[8,8,256]{2,1,0:T(8,128)}, f32[8,128,256]{2,1,0:T(8,128)}) custom-call(f32[512,1024]{1,0:T(8,128)} %get-tuple-element.485.qm, f32[512,2048]{1,0:T(8,128)} %get-tuple-element.430.out, f32[512,2048]{1,0:T(8,128)} %gate.1, f32[1,256]{1,0:T(1,128)} %reshape.362.head_gain, ...), custom_call_target="tpu_custom_call" | custom-call | flops 14 | bytes 1024 | tf_op jit(solution)/shard_map/adjoint_piece/pallas_call | solution.py:71
  530.3 14.4 %d_out.1 = f32[2048,1024]{1,0:T(8,128)} custom-call(s32[8]{0:T(128)} %stack.399.halves, f32[512,2048]{1,0:T(8,128)} %get-tuple-element.495.x_ref, f32[512,1024]{1,0:T(8,128)} %fusion.dy_ref), custom_call_target="tpu_custom_call" | custom-call | flops 14 | bytes 1024 | tf_op jit(solution)/shard_map/d_out/pallas_call | solution.py:462
  544.6 12.7 %d_gate.1 = f32[1024,2048]{1,0:T(8,128)} custom-call(s32[8]{0:T(128)} %stack.407.halves, f32[512,1024]{1,0:T(8,128)} %copy-done, f32[512,2048]{1,0:T(8,128)} %get-tuple-element.509.dy_ref), custom_call_target="tpu_custom_call" | custom-call | flops 14 | bytes 1024 | tf_op jit(solution)/shard_map/d_gate/pallas_call | solution.py:462
  571.4 13.2 %back_gate.1.refs_6_ = f32[512,1024]{1,0:T(8,128)} custom-call(f32[512,2048]{1,0:T(8,128)} %get-tuple-element.509.dy_ref, bf16[1024,2048]{1,0:T(8,128)(2,1)} %get-tuple-element.393.high, bf16[1024,2048]{1,0:T(8,128)(2,1)} %get-tuple-element.394.low), custom_call_target="tpu_custom_call" | custom-call | flops 12 | bytes 1024 | tf_op jit(solution)/shard_map/back_gate/pallas_call | solution.py:404
  584.6 15.4 %down.1 = f32[512,1024]{1,0:T(8,128)} custom-call(f32[512,2816]{1,0:T(8,128)} %get-tuple-element.511.x_ref, bf16[2816,1024]{1,0:T(8,128)(2,1)} %get-tuple-element.459.high, bf16[2816,1024]{1,0:T(8,128)(2,1)} %get-tuple-element.460.low), custom_call_target="tpu_custom_call" | custom-call | flops 14 | bytes 1024 | tf_op jit(solution)/shard_map/down/pallas_call | solution.py:359
  616.3 52.7 %adjoint.1 = (f32[512,1024]{1,0:T(8,128)}, f32[512,1024]{1,0:T(8,128)}, f32[512,2048]{1,0:T(8,128)}, f32[8,512,8]{2,1,0:T(8,128)}, f32[8,8,512]{2,1,0:T(8,128)}) custom-call(f32[8,128,256]{2,1,0:T(8,128)} %all-to-all-done.3.z_in, f32[8,128,256]{2,1,0:T(8,128)} %copy-done.8, f32[512,1024]{1,0:T(8,128)} %get-tuple-element.372.q, ...), custom_call_target="tpu_custom_call" | custom-call | flops 55 | bytes 1024 | tf_op jit(solution)/shard_map/adjoint/pallas_call | solution.py:71
  674.7 26.6 %front_back.1 = (f32[2,512,1024]{2,1,0:T(8,128)}, f32[512,2048]{1,0:T(8,128)}, f32[16,1024]{1,0:T(8,128)}, f32[16,1024]{1,0:T(8,128)}, f32[16,2048]{1,0:T(8,128)...) custom-call(f32[528,1024]{1,0:T(8,128)} %q.1.mixed_q, f32[528,1024]{1,0:T(8,128)} %k.1.mixed_k, ...), custom_call_target="tpu_custom_call" | custom-call | flops 25 | bytes 1024 | tf_op jit(solution)/shard_map/front_back/pallas_call | solution.py:71
  703.3 18.5 %collective-permute-done.47 = f32[256,1024]{1,0:T(8,128)S(1)} collective-permute-done((f32[256,1024]{1,0:T(8,128)S(1)}, f32[256,1024]{1,0:T(8,128)S(1)}, u32[]{:S(2)}, u32[]{:S(2)}) %collective-permute-start.47) | collective-permute-done | bytes 1048608 | tf_op jit(solution)/shard_map/ppermute | solution.py:33
  733.6 13.2 %d_v.1 = f32[1024,2048]{1,0:T(8,128)} custom-call(s32[8]{0:T(128)} %stack.419.halves, f32[512,1024]{1,0:T(8,128)} %copy-done, f32[512,2048]{1,0:T(8,128)} %fusion.24.dy_ref.refs_0_), custom_call_target="tpu_custom_call" | custom-call | flops 13 | bytes 1024 | tf_op jit(solution)/shard_map/d_v/pallas_call | solution.py:462
  748.9 12.8 %d_qk.1 = f32[1024,2048]{1,0:T(8,128)} custom-call(s32[8]{0:T(128)} %stack.419.halves, f32[512,1024]{1,0:T(8,128)} %copy-done, f32[2,512,1024]{2,1,0:T(8,128)} %fusion.25.dy_ref.refs_0_), custom_call_target="tpu_custom_call" | custom-call | flops 13 | bytes 1024 | tf_op jit(solution)/shard_map/d_qk/pallas_call | solution.py:462
  781.5 15.0 %back_v.1.refs_11_ = f32[512,1024]{1,0:T(8,128)} custom-call(s32[5]{0:T(128)} %stack.361.starts, f32[512,2048]{1,0:T(8,128)} %fusion.24.dy_ref.refs_0_, f32[512,4096]{1,0:T(8,128)} %all-gather.6.cloned.1.call-done.refs_0_.refs_1_.refs_6_, f32[128,2048]{1,0:T(8,128)} %copy-done.18, f32[128,2048]{1,0:T(8,128)} %copy-done.20, f32[128,2048]{1,0:T(8,128)} %copy-done.19, ...), custom_call_target="tpu_custom_call" | custom-call | flops 15 | bytes 1024 | tf_op jit(solution)/shard_map/back_v/pallas_call | solution.py:322
  829.1 14.8 %back_qk.1 = f32[512,1024]{1,0:T(8,128)} custom-call(s32[5]{0:T(128)} %stack.338.starts, f32[2,512,1024]{2,1,0:T(8,128)} %fusion.25.dy_ref.refs_0_, f32[512,4096]{1,0:T(8,128)} %all-gather.6.cloned.1.call-done.refs_0_.refs_1_.refs_6_, f32[128,1024]{1,0:T(8,128)} %copy-done.31, f32[128,1024]{1,0:T(8,128)} %copy-done.34, f32[128,1024]{1,0:T(8,128)} %copy-done.32, ...), custom_call_target="tpu_custom_call" | custom-call | flops 15 | bytes 1024 | tf_op jit(solution)/shard_map/back_qk/pallas_call | solution.py:322
  857.0 20.4 %collective-permute-done.59 = f32[64,2816]{1,0:T(8,128)} collective-permute-done((f32[64,2816]{1,0:T(8,128)}, f32[64,2816]{1,0:T(8,128)}, u32[]{:S(2)}, u32[]{:S(2)}) %collective-permute-start.59) | collective-permute-done | bytes 720928 | tf_op jit(solution)/shard_map/ppermute | solution.py:33
  880.8 26.8 %collective-permute-done.62 = f32[352,1024]{1,0:T(8,128)} collective-permute-done((f32[352,1024]{1,0:T(8,128)}, f32[352,1024]{1,0:T(8,128)}, u32[]{:S(2)}, u32[]{:S(2)}) %collective-permute-start.62) | collective-permute-done | bytes 1441824 | tf_op jit(solution)/shard_map/ppermute | solution.py:33
  934.0 12.9 %collective-permute-done.64 = f32[32,2816]{1,0:T(8,128)S(1)} collective-permute-done((f32[32,2816]{1,0:T(8,128)}, f32[32,2816]{1,0:T(8,128)S(1)}, u32[]{:S(2)}, u32[]{:S(2)}) %collective-permute-start.64) | collective-permute-done | bytes 360480 | tf_op jit(solution)/shard_map/ppermute | solution.py:33
  955.5 71.6 %collective-permute-done.68 = f32[32,2048]{1,0:T(8,128)S(1)} collective-permute-done((f32[32,2048]{1,0:T(8,128)S(1)}, f32[32,2048]{1,0:T(8,128)S(1)}, u32[]{:S(2)}, u32[]{:S(2)}) %collective-permute-start.68) | collective-permute-done | bytes 262176 | tf_op jit(solution)/shard_map/ppermute | solution.py:33
  1033.4 28.7 %all-reduce.9.cloned.1.call-done = (f32[128,2048]{1,0:T(8,128)}, f32[128,2048]{1,0:T(8,128)}, f32[256,1024]{1,0:T(8,128)}, f32[256,1024]{1,0:T(8,128)}) async-done(((f32[128,2048]{1,0:T(8,128)}, f32[128,2048]{1,0:T(8,128)}, f32[256,1024]{1,0:T(8,128)}, f32[256,1024]{1,0:T(8,128)}), (f32[128,2048]{1,0:T(8,128)}, f32[128,2048]{1,0:T(8,128)}, f32[256,1024]{1,0:T(8,128)}, ...) | async-done | bytes 4194320 | tf_op jit(solution)/shard_map/psum | solution.py:887
  (620 shorter events, 519.4 us)
Async XLA Ops:
  7.2 60.2 %all-gather.6.cloned.1.call-start = ((), (), s32[]{:S(2)}) async-start(), calls=%async_computation.11 | async-start | bytes 12582912 | tf_op jit(solution)/shard_map/all_gather | solution.py:101
  8.0 201.3 %all-gather.8.cloned.1.call-start = ((), (), s32[]{:S(2)}) async-start(), calls=%async_computation.12 | async-start | bytes 6291456 | tf_op jit(solution)/shard_map/all_gather | solution.py:101
  8.7 242.0 %all-gather.10.cloned.1.call-start = ((), (), s32[]{:S(2)}) async-start(), calls=%async_computation.13 | async-start | bytes 6291456 | tf_op jit(solution)/shard_map/all_gather | solution.py:101
  9.5 253.0 %all-gather.12.cloned.1.call-start = ((), (), s32[]{:S(2)}) async-start(), calls=%async_computation.14 | async-start | bytes 17301504 | tf_op jit(solution)/shard_map/all_gather | solution.py:101
  116.8 68.4 %collective-permute-start.20 = (f32[128,2816]{1,0:T(8,128)}, f32[128,2816]{1,0:T(8,128)}, u32[]{:S(2)}, u32[]{:S(2)}) collective-permute-start(f32[128,2816]{1,0:T(8,128)} %get-tuple-element.380), channel_id=1, source_target_pairs={{0,2},{1,3},{2,0},{3,1},{4,6},{5,7},{6,4},{7,5},{8,10},{9,11},{10,... | collective-permute-start | bytes 4325384 | tf_op jit(solution)/shard_map/ppermute | solution.py:33
  130.7 54.4 %collective-permute-start.19 = (f32[256,1024]{1,0:T(8,128)}, f32[256,1024]{1,0:T(8,128)S(1)}, u32[]{:S(2)}, u32[]{:S(2)}) collective-permute-start(f32[256,1024]{1,0:T(8,128)} %constant_dynamic-slice_fusion.14), channel_id=1, source_target_pairs={{0,2},{1,3},{2,0},{3,1},{4,6},{5,7},{6,4},{7,5},{8,10},{9,11},{10,... | collective-permute-start | bytes 3145736 | tf_op jit(solution)/shard_map/ppermute | solution.py:33
  186.1 54.4 %all-to-all-start = ((f32[8,128,384]{2,1,0:T(8,128)}), f32[8,128,384]{2,1,0:T(8,128)S(1)}, u32[]{:S(2)}, u32[]{:S(2)}) async-start(f32[8,128,384]{2,1,0:T(8,128)} %get-tuple-element.382), calls=%async_computation | async-start | bytes 3145728 | tf_op jit(solution)/shard_map/all_to_all | solution.py:810
  190.9 170.5 %all-gather.14.cloned.1.call-start = ((), (), s32[]{:S(2)}) async-start(), calls=%async_computation.15 | async-start | bytes 8650752 | tf_op jit(solution)/shard_map/all_gather | solution.py:101
  191.5 49.0 %collective-permute-start.23 = (f32[256,1024]{1,0:T(8,128)}, f32[256,1024]{1,0:T(8,128)}, u32[]{:S(2)}, u32[]{:S(2)}) collective-permute-start(f32[256,1024]{1,0:T(8,128)} %copy-done.41), channel_id=1, source_target_pairs={{0,8},{4,12},{8,0},{12,4},{16,24},{20,28},{24,16},{28,20},{1,9},{5... | collective-permute-start | bytes 3145736 | tf_op jit(solution)/shard_map/ppermute | solution.py:33
  193.4 57.3 %collective-permute-start.24 = (f32[128,2816]{1,0:T(8,128)}, f32[128,2816]{1,0:T(8,128)}, u32[]{:S(2)}, u32[]{:S(2)}) collective-permute-start(f32[128,2816]{1,0:T(8,128)} %collective-permute-done.20.refs_1_), channel_id=1, source_target_pairs={{0,1},{1,0},{2,3},{3,2},{4,5},{5,4},{6,7},{7,6},{8,9},{9,8},{10,11... | collective-permute-start | bytes 4325384 | tf_op jit(solution)/shard_map/ppermute | solution.py:33
  193.4 64.7 %collective-permute-start.26 = (f32[128,2816]{1,0:T(8,128)}, f32[128,2816]{1,0:T(8,128)}, u32[]{:S(2)}, u32[]{:S(2)}) collective-permute-start(f32[128,2816]{1,0:T(8,128)} %collective-permute-done.20.refs_1_), channel_id=1, source_target_pairs={{0,4},{4,0},{8,12},{12,8},{16,20},{20,16},{24,28},{28,24},{1,5},{5... | collective-permute-start | bytes 4325384 | tf_op jit(solution)/shard_map/ppermute | solution.py:33
  194.9 63.5 %collective-permute-start.27 = (f32[128,2816]{1,0:T(8,128)}, f32[128,2816]{1,0:T(8,128)}, u32[]{:S(2)}, u32[]{:S(2)}) collective-permute-start(f32[128,2816]{1,0:T(8,128)} %get-tuple-element.416), channel_id=1, source_target_pairs={{0,2},{1,3},{2,0},{3,1},{4,6},{5,7},{6,4},{7,5},{8,10},{9,11},{10,... | collective-permute-start | bytes 4325384 | tf_op jit(solution)/shard_map/ppermute | solution.py:33
  250.1 130.4 %reduce-scatter.8.cloned.1.call-start = ((), (), s32[]{:S(2)}) async-start(), calls=%async_computation.16 | async-start | bytes 17301504 | tf_op jit(solution)/shard_map/reduce_scatter | solution.py:856
  361.4 100.3 %reduce-scatter.10.cloned.1.call-start = ((), (), s32[]{:S(2)}) async-start(), calls=%async_computation.17 | async-start | bytes 17301504 | tf_op jit(solution)/shard_map/reduce_scatter | solution.py:856
  423.6 91.1 %reduce-scatter.12.cloned.1.call-start = ((), (), s32[]{:S(2)}) async-start(), calls=%async_computation.18 | async-start | bytes 17301504 | tf_op jit(solution)/shard_map/reduce_scatter | solution.py:856
  463.2 51.5 %collective-permute-start.38 = (f32[128,2816]{1,0:T(8,128)S(1)}, f32[128,2816]{1,0:T(8,128)}, u32[]{:S(2)}, u32[]{:S(2)}) collective-permute-start(f32[128,2816]{1,0:T(8,128)S(1)} %slice.386), channel_id=1, source_target_pairs={{0,2},{1,3},{2,0},{3,1},{4,6},{5,7},{6,4},{7,5},{8,10},{9,11},{10,... | collective-permute-start | bytes 4325384 | tf_op jit(solution)/shard_map/ppermute | solution.py:33
  465.1 49.5 %collective-permute-start.39 = (f32[352,1024]{1,0:T(8,128)S(1)}, f32[352,1024]{1,0:T(8,128)}, u32[]{:S(2)}, u32[]{:S(2)}) collective-permute-start(f32[352,1024]{1,0:T(8,128)S(1)} %get-tuple-element.491), channel_id=1, source_target_pairs={{0,4},{4,0},{8,12},{12,8},{16,20},{20,16},{24,28},{28,24},{1,5},{5... | collective-permute-start | bytes 4325384 | tf_op jit(solution)/shard_map/ppermute | solution.py:33
  519.3 84.7 %reduce-scatter.14.cloned.1.call-start = ((), (), s32[]{:S(2)}) async-start(), calls=%async_computation.19 | async-start | bytes 12582912 | tf_op jit(solution)/shard_map/reduce_scatter | solution.py:856
  571.4 249.8 %reduce-scatter.18.cloned.1.call-start = ((), (), s32[]{:S(2)}) async-start(), calls=%async_computation.21 | async-start | bytes 12582912 | tf_op jit(solution)/shard_map/reduce_scatter | solution.py:856
  604.0 65.0 %collective-permute-start.43 = (f32[128,2816]{1,0:T(8,128)}, f32[128,2816]{1,0:T(8,128)}, u32[]{:S(2)}, u32[]{:S(2)}) collective-permute-start(f32[128,2816]{1,0:T(8,128)} %get-tuple-element.526), channel_id=1, source_target_pairs={{0,2},{1,3},{2,0},{3,1},{4,6},{5,7},{6,4},{7,5},{8,10},{9,11},{10,... | collective-permute-start | bytes 4325384 | tf_op jit(solution)/shard_map/ppermute | solution.py:33
  604.4 64.6 %collective-permute-start.45 = (f32[128,2816]{1,0:T(8,128)}, f32[128,2816]{1,0:T(8,128)}, u32[]{:S(2)}, u32[]{:S(2)}) collective-permute-start(f32[128,2816]{1,0:T(8,128)} %get-tuple-element.530), channel_id=1, source_target_pairs={{0,8},{4,12},{8,0},{12,4},{16,24},{20,28},{24,16},{28,20},{1,9},{5... | collective-permute-start | bytes 4325384 | tf_op jit(solution)/shard_map/ppermute | solution.py:33
  609.4 59.6 %collective-permute-start.44 = (f32[256,1024]{1,0:T(8,128)}, f32[256,1024]{1,0:T(8,128)}, u32[]{:S(2)}, u32[]{:S(2)}) collective-permute-start(f32[256,1024]{1,0:T(8,128)} %get-tuple-element.528), channel_id=1, source_target_pairs={{0,2},{1,3},{2,0},{3,1},{4,6},{5,7},{6,4},{7,5},{8,10},{9,11},{10,... | collective-permute-start | bytes 3145736 | tf_op jit(solution)/shard_map/ppermute | solution.py:33
  613.3 55.7 %collective-permute-start.46 = (f32[88,1024]{1,0:T(8,128)S(1)}, f32[88,1024]{1,0:T(8,128)S(1)}, u32[]{:S(2)}, u32[]{:S(2)}) collective-permute-start(f32[88,1024]{1,0:T(8,128)S(1)} %constant_dynamic-slice_fusion.10), channel_id=1, source_target_pairs={{0,16},{4,20},{8,24},{12,28},{16,0},{20,4},{24,8},{28,12},{1,17},{... | collective-permute-start | bytes 1081352 | tf_op jit(solution)/shard_map/ppermute | solution.py:33
  767.2 80.0 %reduce-scatter.20.cloned.1.call-start = ((), (), s32[]{:S(2)}) async-start(), calls=%async_computation.22 | async-start | bytes 12582912 | tf_op jit(solution)/shard_map/reduce_scatter | solution.py:856
  767.8 294.4 %all-reduce.9.cloned.1.call-start = ((), (), s32[]{:S(2)}) async-start(), calls=%async_computation.23 | async-start | bytes 8388608 | tf_op jit(solution)/shard_map/psum | solution.py:887
  848.6 59.0 %collective-permute-start.62 = (f32[352,1024]{1,0:T(8,128)}, f32[352,1024]{1,0:T(8,128)}, u32[]{:S(2)}, u32[]{:S(2)}) collective-permute-start(f32[352,1024]{1,0:T(8,128)} %pad_maximum_fusion.4), channel_id=1, source_target_pairs={{0,4},{4,0},{8,12},{12,8},{16,20},{20,16},{24,28},{28,24},{1,5},{5... | collective-permute-start | bytes 4325384 | tf_op jit(solution)/shard_map/ppermute | solution.py:33
  856.9 54.4 %collective-permute-start.61 = (f32[128,2048]{1,0:T(8,128)S(1)}, f32[128,2048]{1,0:T(8,128)S(1)}, u32[]{:S(2)}, u32[]{:S(2)}) collective-permute-start(f32[128,2048]{1,0:T(8,128)S(1)} %get-tuple-element.586), channel_id=1, source_target_pairs={{0,2},{1,3},{2,0},{3,1},{4,6},{5,7},{6,4},{7,5},{8,10},{9,11},{10,... | collective-permute-start | bytes 3145736 | tf_op jit(solution)/shard_map/ppermute | solution.py:33
  929.5 97.7 %collective-permute-start.65 = (f32[128,2816]{1,0:T(8,128)}, f32[128,2816]{1,0:T(8,128)S(1)}, u32[]{:S(2)}, u32[]{:S(2)}) collective-permute-start(f32[128,2816]{1,0:T(8,128)} %pad_maximum_fusion.5), channel_id=1, source_target_pairs={{0,8},{4,12},{8,0},{12,4},{16,24},{20,28},{24,16},{28,20},{1,9},{5... | collective-permute-start | bytes 4325384 | tf_op jit(solution)/shard_map/ppermute | solution.py:33
  949.8 77.3 %collective-permute-start.68 = (f32[32,2048]{1,0:T(8,128)S(1)}, f32[32,2048]{1,0:T(8,128)S(1)}, u32[]{:S(2)}, u32[]{:S(2)}) collective-permute-start(f32[32,2048]{1,0:T(8,128)S(1)} %get-tuple-element.605), channel_id=1, source_target_pairs={{0,8},{4,12},{8,0},{12,4},{16,24},{20,28},{24,16},{28,20},{1,9},{5... | collective-permute-start | bytes 786440 | tf_op jit(solution)/shard_map/ppermute | solution.py:33
  951.3 75.8 %collective-permute-start.69 = (f32[32,2048]{1,0:T(8,128)S(1)}, f32[32,2048]{1,0:T(8,128)S(1)}, u32[]{:S(2)}, u32[]{:S(2)}) collective-permute-start(f32[32,2048]{1,0:T(8,128)S(1)} %get-tuple-element.606), channel_id=1, source_target_pairs={{0,16},{4,20},{8,24},{12,28},{16,0},{20,4},{24,8},{28,12},{1,17},{... | collective-permute-start | bytes 786440 | tf_op jit(solution)/shard_map/ppermute | solution.py:33
  952.2 74.9 %collective-permute-start.70 = (f32[32,2048]{1,0:T(8,128)S(1)}, f32[32,2048]{1,0:T(8,128)S(1)}, u32[]{:S(2)}, u32[]{:S(2)}) collective-permute-start(f32[32,2048]{1,0:T(8,128)S(1)} %get-tuple-element.607), channel_id=1, source_target_pairs={{0,24},{4,28},{8,16},{12,20},{16,8},{20,12},{24,0},{28,4},{1,25},{... | collective-permute-start | bytes 786440 | tf_op jit(solution)/shard_map/ppermute | solution.py:33
  954.5 74.6 %collective-permute-start.67 = (f32[128,2048]{1,0:T(8,128)S(1)}, f32[128,2048]{1,0:T(8,128)S(1)}, u32[]{:S(2)}, u32[]{:S(2)}) collective-permute-start(f32[128,2048]{1,0:T(8,128)S(1)} %get-tuple-element.603), channel_id=1, source_target_pairs={{0,2},{1,3},{2,0},{3,1},{4,6},{5,7},{6,4},{7,5},{8,10},{9,11},{10,... | collective-permute-start | bytes 3145736 | tf_op jit(solution)/shard_map/ppermute | solution.py:33
  (163 other events, 2569.8 us)
Sparse Core Ops, SparseCore 0:
  9.6 22.5 all-gather.5
  33.7 14.8 all-gather.7
  50.1 16.2 all-gather.9
  67.9 27.3 all-gather.11
  196.1 16.6 all-gather.13
  361.5 18.9 reduce-scatter.7
  422.6 20.2 reduce-scatter.9
  461.8 21.5 reduce-scatter.11
  561.7 17.1 reduce-scatter.13
  581.2 18.0 reduce-scatter.15
  767.3 14.3 reduce-scatter.17
  783.9 18.0 reduce-scatter.19
  849.4 212.6 all-reduce.8
